TPU v7x, 32 devices: a whole 2x2x4 slice. The times are simulated.
32 devices in a mesh: ctx: 8 (over z, x), head: 4 (over y, core).
Axes of the slice: x: 2, y: 2, z: 4, core: 2. Of those that a mesh axis runs over, the one named last changes fastest.
Arguments:
- queries: bfloat16 [4096, 4096], P('ctx', 'head'), may hold values from -200 to 200
- keys_values: bfloat16 [2, 4096, 4096], P(None, 'ctx', 'head'), may hold values from -7 to 7
- w_out: bfloat16 [4096, 4096], P('head'), may hold values from -0.09375 to 0.09375
- doc_index: int32 [4096], replicated, may hold values from 0 to 7, never falling along the last dimension, each value on 1 to 1152 neighbouring positions
Outputs:
- mixed: bfloat16 [4096, 4096], P(('ctx', 'head'))
Inputs may be any that keep to these rules, and one draw needn't show every extreme that they name: `doc_index`: ids never fall along the pack; each document is a run of 1 to 1152 tokens and one has exactly 1152.
All inputs are finite; a program needn't handle non-finite values.
Results may differ from a plain program's by a relative error of at most 0.0095.
Values may be sent and summed in bfloat16 or wider, within the bound.
No kernel may reach another device: no remote copies, remote signals or barrier semaphores. Data moves between devices by JAX's collectives and lax.ppermute only.
A program may use at most 64 MiB of HBM per device.

v0:
```python
import jax
import jax.numpy as jnp
from jax import lax
from jax.sharding import PartitionSpec as P

HD = 128
SPAN = 3


def from_behind(shard, axis, by):
    peers = lax.axis_size(axis)
    pairs = [(i, i + by) for i in range(peers) if 0 <= i + by < peers]
    return lax.ppermute(shard, axis, pairs)


def masked_scores(query_head, key_head, allowed):
    raw = lax.dot_general(
        query_head, key_head, (((1,), (1,)), ((), ())), preferred_element_type=jnp.float32
    ) * HD ** (-0.5)
    return jnp.where(allowed, raw, jnp.float32(-1e30))


def weighted_values(probs, value_head):
    return jnp.dot(probs, value_head, preferred_element_type=jnp.float32)


def per_device(queries, keys_values, w_out, doc_index):
    shard_rows = queries.shape[0]
    my_index = lax.axis_index("ctx")
    first_row = my_index * shard_rows
    offsets = jnp.arange(shard_rows, dtype=jnp.int32)
    query_docs = lax.dynamic_slice_in_dim(doc_index, first_row, shard_rows)
    query_place = first_row + offsets
    earlier = [from_behind(keys_values, "ctx", distance) for distance in range(1, SPAN)]
    tail_rows = shard_rows // 4
    tail_part = keys_values[:, shard_rows - tail_rows :, :]
    far_tail = from_behind(tail_part, "ctx", SPAN)
    filler = jnp.zeros((2, shard_rows - tail_rows, keys_values.shape[2]), keys_values.dtype)
    earlier.append(jnp.concatenate([filler, far_tail], axis=1))
    blocks = [keys_values] + earlier
    masks = []
    live_flags = []
    for distance in range(SPAN + 1):
        start = first_row - distance * shard_rows
        safe_start = jnp.maximum(start, 0)
        docs_here = lax.dynamic_slice_in_dim(doc_index, safe_start, shard_rows)
        docs_here = jnp.where(start >= 0, docs_here, -1)
        key_place = safe_start + offsets
        masks.append(
            (docs_here[None, :] == query_docs[:, None])
            & (key_place[None, :] <= query_place[:, None])
        )
        live_flags.append(docs_here[shard_rows - 1] == query_docs[0])
    head_count = queries.shape[1] // HD

    def one_head(head):
        query_head = lax.dynamic_slice_in_dim(queries, head * HD, HD, 1)
        score_list = []
        value_list = []
        for number, block in enumerate(blocks):
            key_head = lax.dynamic_slice_in_dim(block[0], head * HD, HD, 1)
            value_list.append(lax.dynamic_slice_in_dim(block[1], head * HD, HD, 1))
            score_list.append(masked_scores(query_head, key_head, masks[number]))
        top = jnp.max(jnp.stack([jnp.max(entry, axis=1) for entry in score_list]), axis=0)[:, None]
        total = jnp.zeros((shard_rows, 1), jnp.float32)
        summed = jnp.zeros((shard_rows, HD), jnp.float32)
        for number, entry in enumerate(score_list):
            weights = jnp.exp(entry - top)
            total = total + jnp.sum(weights, axis=1, keepdims=True)
            probs = weights.astype(jnp.bfloat16)
            summed = summed + weighted_values(probs, value_list[number])
        return summed / total

    per_head = lax.map(one_head, jnp.arange(head_count, dtype=jnp.int32))
    attended = (
        jnp.transpose(per_head, (1, 0, 2)).reshape(shard_rows, head_count * HD).astype(jnp.bfloat16)
    )
    term = jnp.dot(attended, w_out, preferred_element_type=jnp.float32).astype(jnp.bfloat16)
    return lax.psum_scatter(
        lax.optimization_barrier(term).astype(jnp.float32).astype(jnp.bfloat16),
        "head",
        scatter_dimension=0,
        tiled=True,
    )


def solution(mesh):
    in_specs = (P("ctx", "head"), P(None, "ctx", "head"), P("head", None), P())
    out_specs = P(("ctx", "head"), None)
    return jax.shard_map(
        per_device, mesh=mesh, in_specs=in_specs, out_specs=out_specs, check_vma=False
    )
```

profile of v0, /device:TPU:24, one launch (start us, length us, event | category | flops | bytes accessed | tf_op | source)
XLA Modules:
  0.0 270.9 jit_solution(892223649638075373)
XLA Ops:
  6.5 3.4 %collective-permute-start = (bf16[2,512,1024]{2,1,0:T(8,128)(2,1)}, bf16[2,512,1024]{2,1,0:T(8,128)(2,1)}, u32[]{:S(2)}, u32[]{:S(2)}) collective-permute-start(bf16[2,512,1024]{2,1,0:T(8,128)(2,1)} %param.7), channel_id=1, source_target_pairs={{0,4},{4,8},{8,12},{12,16},{16,20},{20,24},{24,28},{1,5},{5,9},{9,... | collective-permute-start | bytes 6291464 | tf_op jit(solution)/shard_map/ppermute | solution.py:13
  9.9 1.3 collective-permute-start.1
  11.2 1.1 slice.27
  12.3 1.3 collective-permute-start.2
  13.7 0.9 dynamic-slice_select_fusion
  14.6 109.6 %collective-permute-done.2 = bf16[2,128,1024]{2,1,0:T(8,128)(2,1)S(1)} collective-permute-done((bf16[2,128,1024]{2,1,0:T(8,128)(2,1)S(1)}, bf16[2,128,1024]{2,1,0:T(8,128)(2,1)S(1)}, u32[]{:S(2)}, u32[]{:S(2)}) %collective-permute-start.2) | collective-permute-done | bytes 524320 | tf_op jit(solution)/shard_map/ppermute | solution.py:13
  124.5 84.5 %while.12 = (s32[]{:T(128)}, bf16[8,512,128]{1,2,0:T(8,128)(2,1)}, s32[8]{0:T(128)S(1)}, bf16[512,1024]{1,0:T(8,128)(2,1)}, bf16[2,512,1024]{2,1,0:T(8,128)(2,1)...) while((s32[]{:T(128)}, bf16[8,512,128]{1,2,0:T(8,128)(2,1)}, ...), condition=%wide.region_9.10_spmd.clone.clone, body=%wide.region_0.9_spmd.clone.clone.sunk | while | flops 547683328 | bytes 45830980 | solution.py:74
  124.5 0.6 dynamic_slice.189
  125.7 2.1 fusion.96
  127.8 0.4 fusion.97
  128.6 0.8 copy-done
  129.4 2.0 fusion.94
  132.2 0.6 fusion.101
  134.4 0.7 constant_dynamic-update-slice_fusion.2
  135.0 0.6 dynamic_slice.189
  136.3 2.1 fusion.96
  138.4 0.4 fusion.97
  139.2 0.8 copy-done
  139.9 2.0 fusion.94
  142.3 0.4 fusion.95
  142.8 0.6 fusion.101
  144.9 0.7 constant_dynamic-update-slice_fusion.2
  145.6 0.6 dynamic_slice.189
  146.8 2.1 fusion.96
  149.7 0.8 copy-done
  150.5 2.0 fusion.94
  152.5 0.4 fusion.99
  153.3 0.6 fusion.101
  155.5 0.7 constant_dynamic-update-slice_fusion.2
  156.2 0.6 dynamic_slice.189
  157.4 2.1 fusion.96
  160.3 0.8 copy-done
  161.1 2.0 fusion.94
  163.9 0.6 fusion.101
  166.1 0.7 constant_dynamic-update-slice_fusion.2
  166.8 0.6 dynamic_slice.189
  168.0 2.1 fusion.96
  170.9 0.8 copy-done
  171.7 2.0 fusion.94
  174.5 0.6 fusion.101
  176.7 0.7 constant_dynamic-update-slice_fusion.2
  177.3 0.6 dynamic_slice.189
  178.6 2.1 fusion.96
  180.7 0.4 fusion.97
  181.5 0.8 copy-done
  182.2 2.0 fusion.94
  185.1 0.6 fusion.101
  187.2 0.7 constant_dynamic-update-slice_fusion.2
  187.9 0.6 dynamic_slice.189
  189.1 2.1 fusion.96
  191.2 0.4 fusion.97
  192.0 0.8 copy-done
  192.8 2.0 fusion.94
  195.6 0.6 fusion.101
  197.8 0.7 constant_dynamic-update-slice_fusion.2
  198.5 0.6 dynamic_slice.189
  199.7 2.1 fusion.96
  202.6 0.8 copy-done
  203.4 2.0 fusion.94
  205.4 0.4 fusion.99
  206.2 0.6 fusion.101
  208.4 0.7 constant_dynamic-update-slice_fusion.2
  209.0 10.2 %convolution_convert_fusion = bf16[512,4096]{1,0:T(8,128)(2,1)} fusion(bf16[512,1024]{0,1:T(8,128)(2,1)} %bitcast.60, bf16[1024,4096]{1,0:T(8,128)(2,1)} %param.8), kind=kOutput, calls=%fused_computation.65 | convolution fusion | flops 4297064448 | bytes 13631488 | tf_op jit(solution)/shard_map/dot_general | solution.py:78
  219.3 44.7 %reduce-scatter.2.cloned.1.call-done = bf16[128,4096]{1,0:T(8,128)(2,1)} async-done(((bf16[512,4096]{1,0:T(8,128)(2,1)}), bf16[128,4096]{1,0:T(8,128)(2,1)}) %reduce-scatter.2.cloned.1.call-update) | async-done | bytes 1048592 | tf_op jit(solution)/shard_map/reduce_scatter | solution.py:79
  (114 shorter events, 23.0 us)
Async XLA Ops:
  6.5 257.5 %reduce-scatter.2.cloned.1.call-start = ((), (), s32[]{:S(2)}) async-start(), calls=%async_computation.1 | async-start | bytes 5242880 | tf_op jit(solution)/shard_map/reduce_scatter | solution.py:79
  6.5 117.9 %collective-permute-start = (bf16[2,512,1024]{2,1,0:T(8,128)(2,1)}, bf16[2,512,1024]{2,1,0:T(8,128)(2,1)}, u32[]{:S(2)}, u32[]{:S(2)}) collective-permute-start(bf16[2,512,1024]{2,1,0:T(8,128)(2,1)} %param.7), channel_id=1, source_target_pairs={{0,4},{4,8},{8,12},{12,16},{16,20},{20,24},{24,28},{1,5},{5,9},{9,... | collective-permute-start | bytes 6291464 | tf_op jit(solution)/shard_map/ppermute | solution.py:13
  9.9 114.5 %collective-permute-start.1 = (bf16[2,512,1024]{2,1,0:T(8,128)(2,1)}, bf16[2,512,1024]{2,1,0:T(8,128)(2,1)}, u32[]{:S(2)}, u32[]{:S(2)}) collective-permute-start(bf16[2,512,1024]{2,1,0:T(8,128)(2,1)} %param.7), channel_id=1, source_target_pairs={{0,8},{4,12},{8,16},{12,20},{16,24},{20,28},{1,9},{5,13},{9,17},{1... | collective-permute-start | bytes 6291464 | tf_op jit(solution)/shard_map/ppermute | solution.py:13
  12.3 111.9 %collective-permute-start.2 = (bf16[2,128,1024]{2,1,0:T(8,128)(2,1)S(1)}, bf16[2,128,1024]{2,1,0:T(8,128)(2,1)S(1)}, u32[]{:S(2)}, u32[]{:S(2)}) collective-permute-start(bf16[2,128,1024]{2,1,0:T(8,128)(2,1)S(1)} %slice.27), channel_id=1, source_target_pairs={{0,12},{4,16},{8,20},{12,24},{16,28},{1,13},{5,17},{9,21},{13,25},... | collective-permute-start | bytes 1572872 | tf_op jit(solution)/shard_map/ppermute | solution.py:13
  125.7 2.1 copy-start.1
  127.8 1.6 copy-start
  136.3 2.1 copy-start.1
  138.3 1.6 copy-start
  146.8 2.1 copy-start.1
  148.9 1.6 copy-start
  157.4 2.1 copy-start.1
  159.5 1.6 copy-start
  168.0 2.1 copy-start.1
  170.1 1.6 copy-start
  178.6 2.1 copy-start.1
  180.6 1.6 copy-start
  189.1 2.1 copy-start.1
  191.2 1.6 copy-start
  199.7 2.1 copy-start.1
  201.8 1.6 copy-start
Sparse Core Ops, SparseCore 0:
  219.4 44.5 reduce-scatter.1
where the time goes:
time: 273 us; the launch traced here: 271 us
  waiting for transfers between devices  154 us (56%)
  local copies, waits for them, and re-layouts  51.1 us (19%)
  matrix products  34.6 us (13%)
  between operations  13.5 us (5%)
  starting transfers between devices  5.98 us (2%)
  loops' own time  5.67 us (2%)
  other arithmetic  5.66 us (2%)
    ppermute x3, waiting for transfers between devices, from_behind(): return lax.ppermute(shard, axis, pairs)  110 us
    reduce_scatter x1, waiting for transfers between devices, per_device(): lax.psum_scatter(lax.optimization_barrier(term).astype(jnp.float32).astyp...  44.7 us
    slice x16, local copies, waits for them, and re-layouts, one_head(): value_list.append(lax.dynamic_slice_in_dim(block[1], head * HD, HD, 1))  32.6 us
    dot_general x32, matrix products, masked_scores(): lax.dot_general(query_head, key_head, (((1,), (1,)), ((), ())), preferred...  12.9 us
    dot_general x32, matrix products, weighted_values(): return jnp.dot(probs, value_head, preferred_element_type=jnp.float32)  11.5 us
    dot_general x1, matrix products, per_device(): jnp.dot(attended, w_out, preferred_element_type=jnp.float32)  10.2 us
    dynamic_update_slice x16, local copies, waits for them, and re-layouts, per_device(): per_head = lax.map(one_head, jnp.arange(head_count, dtype=jnp.int32))  6.27 us
    while x32, local copies, waits for them, and re-layouts  6.19 us
  transfers between devices with their start and end apart: 4, of which 2 were waited for; matrix products, arithmetic and copies ran while one was open for 1% of the time, Pallas kernels for 0%

commit v1 on v0

v1 whole, which is shorter than its diff:
```python
import functools
import math

import jax
import jax.numpy as jnp
from jax import lax
from jax.experimental import pallas as pl
from jax.experimental.pallas import tpu as pltpu
from jax.sharding import PartitionSpec as P

HD = 128
TILE = 256
FAR_ROWS = 128
NEG = -1e30
SCALE = HD ** (-0.5) * math.log2(math.e)


def tile_bias(query_docs, key_docs, causal):
    allowed = query_docs == key_docs
    if causal:
        rows = lax.broadcasted_iota(jnp.int32, allowed.shape, 0)
        cols = lax.broadcasted_iota(jnp.int32, allowed.shape, 1)
        allowed = allowed & (cols <= rows)
    return jnp.where(allowed, jnp.float32(0), jnp.float32(NEG))


def scores_of(query, key, bias):
    raw = lax.dot_general(query, key, (((1,), (1,)), ((), ())), preferred_element_type=jnp.float32)
    return raw * SCALE + bias


def fold_tile(head, query, key, value, bias, top, total, summed):
    entry = scores_of(query, key, bias)
    old = top[head]
    new = jnp.maximum(old, jnp.max(entry, axis=1, keepdims=True))
    weights = jnp.exp2(entry - new)
    shrink = jnp.exp2(old - new)
    top[head] = new
    total[head] = total[head] * shrink + jnp.sum(weights, axis=1, keepdims=True)
    cols = pl.ds(head * HD, HD)
    summed[:, cols] = summed[:, cols] * shrink + jnp.dot(
        weights.astype(jnp.bfloat16), value, preferred_element_type=jnp.float32
    )


def local_kernel(heads, rows, pad, place, docs, q_own, q_other, kv_own, kv_other, docs_col, docs_row,
                 summed_out, stats_out, qs, kvs, top, total, summed):
    half = rows // 2
    own = pl.ds(pl.multiple_of(place[0] * half, half), half)
    other = pl.ds(pl.multiple_of((1 - place[0]) * half, half), half)
    qs[own, :] = q_own[...]
    qs[other, :] = q_other[...]
    kvs[:, own, :] = kv_own[...]
    kvs[:, other, :] = kv_other[...]

    def one_tile(step, _):
        here = pl.multiple_of(step * TILE, TILE)
        span = pl.ds(here, TILE)
        query_docs = docs_col[span, :]
        bias = tile_bias(query_docs, docs_row[:, span], True)
        for head in range(heads):
            cols = pl.ds(head * HD, HD)
            entry = scores_of(qs[span, cols], kvs[0, span, cols], bias)
            new = jnp.max(entry, axis=1, keepdims=True)
            weights = jnp.exp2(entry - new)
            top[head] = new
            total[head] = jnp.sum(weights, axis=1, keepdims=True)
            summed[:, cols] = jnp.dot(
                weights.astype(jnp.bfloat16), kvs[1, span, cols], preferred_element_type=jnp.float32
            )
        first_doc = docs[pad + here]
        live = jnp.int32(0)
        for back in range(1, rows // TILE):
            last = jnp.maximum(pad + here - (back - 1) * TILE - 1, 0)
            live += ((docs[last] == first_doc) & (step >= back)).astype(jnp.int32)

        def one_back(back, _):
            there = pl.ds(pl.multiple_of(here - (back + 1) * TILE, TILE), TILE)
            bias = tile_bias(query_docs, docs_row[:, there], False)
            for head in range(heads):
                cols = pl.ds(head * HD, HD)
                fold_tile(head, qs[span, cols], kvs[0, there, cols], kvs[1, there, cols], bias, top, total, summed)
            return 0

        lax.fori_loop(0, live, one_back, 0)
        summed_out[span, :] = summed[...]
        stats_out[span, :] = jnp.concatenate([top[h] for h in range(heads)] + [total[h] for h in range(heads)], axis=1)
        return 0

    lax.fori_loop(0, rows // TILE, one_tile, 0)


def remote_kernel(heads, rows, pad, place, docs, q_own, q_other, kv_same, kv_cross, kv_far, docs_col, docs_row,
                  summed_in, stats_in, *rest):
    outs, (qs, kvs, done, top, total, summed) = rest[:8], rest[8:]
    half = rows // 2
    side = place[0]
    own = pl.ds(pl.multiple_of(side * half, half), half)
    other = pl.ds(pl.multiple_of((1 - side) * half, half), half)
    qs[own, :] = q_own[...]
    qs[other, :] = q_other[...]
    front = pad - rows
    kvs[:, : front - FAR_ROWS, :] = jnp.zeros((2, front - FAR_ROWS, heads * HD), jnp.bfloat16)
    kvs[:, front - FAR_ROWS : front, :] = kv_far[...]
    kvs[:, pl.ds(pl.multiple_of(front + side * half, FAR_ROWS), half), :] = kv_same[...]
    kvs[:, pl.ds(pl.multiple_of(front + (1 - side) * half, FAR_ROWS), half), :] = kv_cross[...]

    def one_tile(step, _):
        here = pl.multiple_of(step * TILE, TILE)
        span = pl.ds(here, TILE)
        stats = stats_in[span, :]
        for head in range(heads):
            top[head] = stats[:, head : head + 1]
            total[head] = stats[:, heads + head : heads + head + 1]
        summed[...] = summed_in[span, :]
        first_doc = docs[pad + here]
        live = jnp.int32(0)
        for back in range(pad // TILE):
            live += (docs[pad - back * TILE - 1] == first_doc).astype(jnp.int32)

        def one_back(back, _):
            there = pl.ds(pl.multiple_of(pad - (back + 1) * TILE, TILE), TILE)
            bias = tile_bias(docs_col[span, :], docs_row[:, there], False)
            for head in range(heads):
                cols = pl.ds(head * HD, HD)
                fold_tile(head, qs[span, cols], kvs[0, there, cols], kvs[1, there, cols], bias, top, total, summed)
            return 0

        lax.fori_loop(0, live, one_back, 0)
        for head in range(heads):
            cols = pl.ds(head * HD, HD)
            done[span, cols] = (summed[:, cols] / total[head]).astype(jnp.bfloat16)
        return 0

    lax.fori_loop(0, rows // TILE, one_tile, 0)
    block = outs[0].shape[0]
    for number, out in enumerate(outs):
        out[...] = done[pl.ds(pl.multiple_of(place[1 + number] * block, block), block), :]


def project_kernel(place, same, core, cross, both, w_mine, w_other, out):
    straight = place[0] == 0
    here = jnp.concatenate([same[...], cross[...]], axis=1)
    here_turned = jnp.concatenate([cross[...], same[...]], axis=1)
    there = jnp.concatenate([core[...], both[...]], axis=1)
    there_turned = jnp.concatenate([both[...], core[...]], axis=1)
    mine = jnp.where(straight, here, here_turned)
    others = jnp.where(straight, there, there_turned)
    out[...] = (
        jnp.dot(mine, w_mine[...], preferred_element_type=jnp.float32)
        + jnp.dot(others, w_other[...], preferred_element_type=jnp.float32)
    ).astype(out.dtype)


def project(place, pieces, w_mine, w_other, kind):
    block, width = pieces[0].shape
    depth, columns = w_mine.shape
    step = 512
    whole = pl.BlockSpec((block, width), lambda i, s: (0, 0))
    slab = pl.BlockSpec((depth, step), lambda i, s: (0, i))
    return pl.pallas_call(
        project_kernel,
        grid_spec=pltpu.PrefetchScalarGridSpec(
            num_scalar_prefetch=1,
            grid=(columns // step,),
            in_specs=[whole] * 4 + [slab] * 2,
            out_specs=pl.BlockSpec((block, step), lambda i, s: (0, i)),
        ),
        out_shape=jax.ShapeDtypeStruct((block, columns), kind),
        compiler_params=pltpu.CompilerParams(vmem_limit_bytes=40 << 20),
        cost_estimate=pl.CostEstimate(
            flops=4 * block * depth * columns, bytes_accessed=4 * depth * columns, transcendentals=0
        ),
    )(place, *pieces, w_mine, w_other)


def per_device(queries, keys_values, w_out, doc_index):
    shard, width = queries.shape
    n_ctx, n_head = lax.axis_size("ctx"), lax.axis_size("head")
    me, group = lax.axis_index("ctx"), lax.axis_index("head")
    half = width // 2
    heads = half // HD
    rows = 2 * shard
    pad = rows + TILE
    side = lax.rem(me, 2)
    base = (me - side) * shard

    padded = jnp.concatenate([jnp.full((pad,), -1, jnp.int32), doc_index])
    docs = lax.dynamic_slice_in_dim(padded, base, pad + rows)
    docs_col = docs[pad:].reshape(rows, 1)
    docs_row = docs.reshape(1, pad + rows)

    swap = [(c, c ^ 1) for c in range(n_ctx)]
    hop = [(c, c + 2) for c in range(n_ctx - 2)]
    far = [(c, c + 4) for c in range(n_ctx - 4)]
    core = [(h, h ^ 1) for h in range(n_head)]
    both = [
        (c * n_head + h, (c ^ 1) * n_head + (h ^ 1)) for c in range(n_ctx) for h in range(n_head)
    ]
    far_y = [(h, h ^ 2) for h in range(n_head)]

    kv_send = lax.dynamic_slice_in_dim(keys_values, (1 - side) * half, half, 2)
    kv_own = lax.dynamic_slice_in_dim(keys_values, side * half, half, 2)
    q_send = lax.dynamic_slice_in_dim(queries, (1 - side) * half, half, 1)
    q_own = lax.dynamic_slice_in_dim(queries, side * half, half, 1)
    kv_other = lax.ppermute(kv_send, "ctx", swap)
    kv_same = lax.ppermute(kv_own, "ctx", hop)
    w_other = lax.ppermute(w_out, "head", core)
    q_other = lax.ppermute(q_send, "ctx", swap)
    kv_cross = lax.ppermute(kv_other, "ctx", hop)
    tail = jnp.where(side == 1, kv_own[:, shard - FAR_ROWS :], kv_other[:, shard - FAR_ROWS :])
    kv_far = lax.ppermute(tail, "ctx", far)

    side_1 = side.reshape(1).astype(jnp.int32)
    vmem = pl.BlockSpec(memory_space=pltpu.VMEM)
    smem = pl.BlockSpec(memory_space=pltpu.SMEM)
    state = [
        pltpu.VMEM((heads, TILE, 1), jnp.float32),
        pltpu.VMEM((heads, TILE, 1), jnp.float32),
        pltpu.VMEM((TILE, half), jnp.float32),
    ]
    summed, stats = pl.pallas_call(
        functools.partial(local_kernel, heads, rows, pad),
        in_specs=[smem, smem] + [vmem] * 6,
        out_specs=[vmem] * 2,
        out_shape=[
            jax.ShapeDtypeStruct((rows, half), jnp.float32),
            jax.ShapeDtypeStruct((rows, 2 * heads), jnp.float32),
        ],
        scratch_shapes=[
            pltpu.VMEM((rows, half), jnp.bfloat16),
            pltpu.VMEM((2, rows, half), jnp.bfloat16),
        ]
        + state,
        compiler_params=pltpu.CompilerParams(vmem_limit_bytes=40 << 20),
        cost_estimate=pl.CostEstimate(
            flops=2 * rows * rows * half, bytes_accessed=6 << 20, transcendentals=rows * rows * heads // 2
        ),
    )(side_1, docs, q_own, q_other, kv_own, kv_other, docs_col, docs_row[:, pad:])

    block = shard // n_head
    places = [side]
    for wave in range(2):
        y_part = (group // 2) ^ (1 - wave)
        for turn in range(4):
            to_side, to_core = side ^ (turn // 2), lax.rem(group, 2) ^ (turn % 2)
            places.append(to_side * n_head + y_part * 2 + to_core)
    place = jnp.stack(places).astype(jnp.int32)
    pieces = pl.pallas_call(
        functools.partial(remote_kernel, heads, rows, pad),
        in_specs=[smem, smem] + [vmem] * 9,
        out_specs=[vmem] * 8,
        out_shape=[jax.ShapeDtypeStruct((block, half), jnp.bfloat16)] * 8,
        scratch_shapes=[
            pltpu.VMEM((rows, half), jnp.bfloat16),
            pltpu.VMEM((2, pad, half), jnp.bfloat16),
            pltpu.VMEM((rows, half), jnp.bfloat16),
        ]
        + state,
        compiler_params=pltpu.CompilerParams(vmem_limit_bytes=40 << 20),
        cost_estimate=pl.CostEstimate(
            flops=2 * rows * rows * half, bytes_accessed=8 << 20, transcendentals=rows * rows * heads // 2
        ),
    )(place, docs, q_own, q_other, kv_same, kv_cross, kv_far, docs_col, docs_row[:, :pad], summed, stats)

    waves = []
    for wave in range(2):
        mine = pieces[4 * wave : 4 * wave + 4]
        waves.append(
            [
                mine[0],
                lax.ppermute(mine[1], "head", core),
                lax.ppermute(mine[2], "ctx", swap),
                lax.ppermute(mine[3], ("ctx", "head"), both),
            ]
        )
    leaving = project(side_1, waves[0], w_out, w_other, jnp.bfloat16)
    arrived = lax.ppermute(leaving, "head", far_y)
    staying = project(side_1, waves[1], w_out, w_other, jnp.float32)
    return (staying + arrived.astype(jnp.float32)).astype(jnp.bfloat16)


def solution(mesh):
    in_specs = (P("ctx", "head"), P(None, "ctx", "head"), P("head", None), P())
    out_specs = P(("ctx", "head"), None)
    return jax.shard_map(
        per_device, mesh=mesh, in_specs=in_specs, out_specs=out_specs, check_vma=False
    )
```

time: 273 us -> 126 us (0.46); the launches traced: 271 us -> 128 us
  waiting for transfers between devices: 154 us -> 57.1 us
  Pallas kernels: 0 us -> 52 us
  local copies, waits for them, and re-layouts: 51.1 us -> 3.24 us
  matrix products: 34.6 us -> 0 us
  between operations: 13.5 us -> 0.15 us
  starting transfers between devices: 5.98 us -> 12.3 us
  loops' own time: 5.67 us -> 0 us
    ppermute x3 -> x13, waiting for transfers between devices: 110 us -> 57.1 us  [the longest x1 22.9 us: per_device(): kv_other = lax.ppermute(kv_send, 'ctx', swap)]
    pallas_call x0 -> x4, Pallas kernels: none -> 52 us  [the longest x1 19.3 us: per_device(): pl.pallas_call(functools.partial(remote_kernel, heads, rows, pad), in_spe...]
    reduce_scatter x1 -> x0, waiting for transfers between devices: 44.7 us -> none  [per_device(): lax.psum_scatter(lax.optimization_barrier(term).astype(jnp.float32).astyp...]
    dot_general x65 -> x0, matrix products: 34.6 us -> none  [the longest x32 12.9 us: masked_scores(): lax.dot_general(query_head, key_head, (((1,), (1,)), ((), ())), preferred...]
    slice x17 -> x3, local copies, waits for them, and re-layouts: 33.7 us -> 0.09 us  [the longest x1 0.08 us: per_device(): docs_col = docs[pad:].reshape(rows, 1)]
    ppermute x3 -> x13, starting transfers between devices: 5.97 us -> 12.3 us  [the longest x2 3.05 us: per_device(): lax.ppermute(mine[2], 'ctx', swap)]
    dynamic_update_slice x16 -> x0, local copies, waits for them, and re-layouts: 6.27 us -> none  [per_device(): per_head = lax.map(one_head, jnp.arange(head_count, dtype=jnp.int32))]
    while x32 -> x0, local copies, waits for them, and re-layouts: 6.19 us -> none
  transfers between devices with their start and end apart: 4 -> 13, of which waited for: 2 -> 8; matrix products, arithmetic and copies ran while one was open for 1% -> 4% of each run, Pallas kernels for 0% -> 35%
where the time goes in v1:
time: 126 us; the launch traced here: 128 us
  waiting for transfers between devices  57.1 us (45%)
  Pallas kernels  52 us (41%)
  starting transfers between devices  12.3 us (10%)
  local copies, waits for them, and re-layouts  3.24 us (3%)
  other arithmetic  2.97 us (2%)
    ppermute x1, waiting for transfers between devices, per_device(): kv_other = lax.ppermute(kv_send, 'ctx', swap)  22.9 us
    pallas_call x1, Pallas kernels, per_device(): pl.pallas_call(functools.partial(remote_kernel, heads, rows, pad), in_spe...  19.3 us
    pallas_call x1, Pallas kernels, per_device(): pl.pallas_call(functools.partial(local_kernel, heads, rows, pad), in_spec...  16.9 us
    pallas_call x2, Pallas kernels, project(): pl.pallas_call(project_kernel, grid_spec=pltpu.PrefetchScalarGridSpec(num...  15.8 us
    ppermute x2, waiting for transfers between devices, per_device(): lax.ppermute(mine[2], 'ctx', swap)  8.93 us
    ppermute x1, waiting for transfers between devices, per_device(): q_other = lax.ppermute(q_send, 'ctx', swap)  8.76 us
    ppermute x1, waiting for transfers between devices, per_device(): arrived = lax.ppermute(leaving, 'head', far_y)  7.58 us
    ppermute x1, waiting for transfers between devices, per_device(): kv_far = lax.ppermute(tail, 'ctx', far)  4.96 us
  transfers between devices with their start and end apart: 13, of which 8 were waited for; matrix products, arithmetic and copies ran while one was open for 4% of the time, Pallas kernels for 35%

profile of v1, /device:TPU:24, one launch (start us, length us, event | category | flops | bytes accessed | tf_op | source)
XLA Modules:
  0.0 127.7 jit_solution(1701328920461802062)
XLA Ops:
  0.0 0.0 collective-permute-start.8
  0.0 0.0 copy-start.1
  0.0 1.8 %constant_dynamic-slice_fusion = (bf16[2,512,512]{2,1,0:T(8,128)(2,1)S(1)}, bf16[2,512,512]{2,1,0:T(8,128)(2,1)S(1)}) fusion(bf16[2,512,1024]{2,1,0:T(8,128)(2,1)} %param.5, s32[]{:T(128)S(6)} %select_n.28, s32[]{:T(128)S(6)} %select_n.27), kind=kLoop, calls=%fused_computation.4 | loop fusion | bytes 4194312 | tf_op jit(solution)/shard_map/dynamic_slice | solution.py:202
  1.8 0.0 copy-start.2
  1.8 1.6 %collective-permute-start.2 = (bf16[2,512,512]{2,1,0:T(8,128)(2,1)S(1)}, bf16[2,512,512]{2,1,0:T(8,128)(2,1)}, u32[]{:S(2)}, u32[]{:S(2)}) collective-permute-start(bf16[2,512,512]{2,1,0:T(8,128)(2,1)S(1)} %get-tuple-element.25), channel_id=1, source_target_pairs={{0,4},{4,0},{8,12},{12,8},{16,20},{20,16},{24,28},{28,24},{1,5},{5... | collective-permute-start | bytes 3145736 | tf_op jit(solution)/shard_map/ppermute | solution.py:206
  3.4 1.3 %collective-permute-start.1 = (bf16[2,512,512]{2,1,0:T(8,128)(2,1)S(1)}, bf16[2,512,512]{2,1,0:T(8,128)(2,1)S(1)}, u32[]{:S(2)}, u32[]{:S(2)}) collective-permute-start(bf16[2,512,512]{2,1,0:T(8,128)(2,1)S(1)} %get-tuple-element.26.kv_own), channel_id=1, source_target_pairs={{0,8},{4,12},{8,16},{12,20},{16,24},{20,28},{1,9},{5,13},{9,17},{1... | collective-permute-start | bytes 3145736 | tf_op jit(solution)/shard_map/ppermute | solution.py:207
  4.7 22.9 %collective-permute-done.2.kv_other = bf16[2,512,512]{2,1,0:T(8,128)(2,1)} collective-permute-done((bf16[2,512,512]{2,1,0:T(8,128)(2,1)S(1)}, bf16[2,512,512]{2,1,0:T(8,128)(2,1)}, u32[]{:S(2)}, u32[]{:S(2)}) %collective-permute-start.2) | collective-permute-done | bytes 1048608 | tf_op jit(solution)/shard_map/ppermute | solution.py:206
  27.6 1.3 %collective-permute-start.3 = (bf16[2,512,512]{2,1,0:T(8,128)(2,1)}, bf16[2,512,512]{2,1,0:T(8,128)(2,1)}, u32[]{:S(2)}, u32[]{:S(2)}) collective-permute-start(bf16[2,512,512]{2,1,0:T(8,128)(2,1)} %collective-permute-done.2.kv_other), channel_id=1, source_target_pairs={{0,8},{4,12},{8,16},{12,20},{16,24},{20,28},{1,9},{5,13},{9,17},{1... | collective-permute-start | bytes 3145736 | tf_op jit(solution)/shard_map/ppermute | solution.py:210
  28.9 0.0 copy-done.1
  28.9 0.9 constant_dynamic-slice_fusion.2
  29.8 1.5 %collective-permute-start = (bf16[512,512]{1,0:T(8,128)(2,1)}, bf16[512,512]{1,0:T(8,128)(2,1)}, u32[]{:S(2)}, u32[]{:S(2)}) collective-permute-start(bf16[512,512]{1,0:T(8,128)(2,1)} %get-tuple-element.27), channel_id=1, source_target_pairs={{0,4},{4,0},{8,12},{12,8},{16,20},{20,16},{24,28},{28,24},{1,5},{5... | collective-permute-start | bytes 1572872 | tf_op jit(solution)/shard_map/ppermute | solution.py:209
  31.3 1.8 %slice_select_fusion = bf16[2,128,512]{2,1,0:T(8,128)(2,1)} fusion(bf16[2,512,512]{2,1,0:T(8,128)(2,1)} %collective-permute-done.2.kv_other, bf16[2,512,1024]{2,1,0:T(8,128)(2,1)} %param.5, s32[]{:T(128)S(6)} %add.73, s32[]{:T(128)S(6)} %select_n.27, pred[]{:T(512)S(6)} %eq.3), kind=kLoop, calls=%fused_computation.1 | loop fusion | flops 131072 | bytes 786441 | tf_op jit(solution)/shard_map/jit(_where)/select_n | solution.py:211
  33.1 1.3 %collective-permute-start.4 = (bf16[2,128,512]{2,1,0:T(8,128)(2,1)}, bf16[2,128,512]{2,1,0:T(8,128)(2,1)S(1)}, u32[]{:S(2)}, u32[]{:S(2)}) collective-permute-start(bf16[2,128,512]{2,1,0:T(8,128)(2,1)} %slice_select_fusion), channel_id=1, source_target_pairs={{0,16},{4,20},{8,24},{12,28},{1,17},{5,21},{9,25},{13,29},{2,18},{... | collective-permute-start | bytes 786440 | tf_op jit(solution)/shard_map/ppermute | solution.py:212
  34.4 0.0 copy-done.2
  34.4 0.1 pad_dynamic-slice_fusion.1.docs
  34.5 0.1 pad_dynamic-slice_fusion
  34.6 0.2 copy.6.docs_col
  34.8 0.1 stack.36.place
  34.9 8.8 %collective-permute-done.q_other = bf16[512,512]{1,0:T(8,128)(2,1)} collective-permute-done((bf16[512,512]{1,0:T(8,128)(2,1)}, bf16[512,512]{1,0:T(8,128)(2,1)}, u32[]{:S(2)}, u32[]{:S(2)}) %collective-permute-start) | collective-permute-done | bytes 524320 | tf_op jit(solution)/shard_map/ppermute | solution.py:209
  43.7 0.0 copy-start
  43.7 16.9 %shard_map.46 = (f32[1024,512]{1,0:T(8,128)S(1)}, f32[1024,8]{1,0:T(8,128)S(1)}) custom-call(s32[1]{0:T(128)} %bitcast.place, s32[2304]{0:T(1024)S(1)} %pad_dynamic-slice_fusion.1.docs, bf16[512,512]{1,0:T(8,128)(2,1)S(1)} %get-tuple-element.28.q_own, bf16[512,512]{1,0:T(8,128)(2,1)} %collective-permute-done.q_other, ...), custom_call_target="tpu_custom_call" | custom-call | flops 1073741824 | bytes 6291456 | tf_op jit(solution)/shard_map/pallas_call | solution.py:222
  60.6 0.0 collective-permute-done.1.kv_same
  60.6 5.0 %collective-permute-done.4.kv_far = bf16[2,128,512]{2,1,0:T(8,128)(2,1)S(1)} collective-permute-done((bf16[2,128,512]{2,1,0:T(8,128)(2,1)}, bf16[2,128,512]{2,1,0:T(8,128)(2,1)S(1)}, u32[]{:S(2)}, u32[]{:S(2)}) %collective-permute-start.4) | collective-permute-done | bytes 262176 | tf_op jit(solution)/shard_map/ppermute | solution.py:212
  65.6 0.0 collective-permute-done.3.kv_cross
  65.6 19.3 %shard_map.47 = (bf16[128,512]{1,0:T(8,128)(2,1)S(1)}, bf16[128,512]{1,0:T(8,128)(2,1)S(1)}, bf16[128,512]{1,0:T(8,128)(2,1)S(1)}, bf16[128,512]{1,0:T(8,128)(2,...) custom-call(s32[9]{0:T(128)S(1)} %stack.36.place, ...), custom_call_target="tpu_custom_call" | custom-call | flops 1073741824 | bytes 8388608 | tf_op jit(solution)/shard_map/pallas_call | solution.py:249
  84.9 0.1 collective-permute-start.9
  85.0 1.6 %collective-permute-start.10 = (bf16[128,512]{1,0:T(8,128)(2,1)S(1)}, bf16[128,512]{1,0:T(8,128)(2,1)S(1)}, u32[]{:S(2)}, u32[]{:S(2)}) collective-permute-start(bf16[128,512]{1,0:T(8,128)(2,1)S(1)} %get-tuple-element.23), channel_id=1, source_target_pairs={{0,4},{4,0},{8,12},{12,8},{16,20},{20,16},{24,28},{28,24},{1,5},{5... | collective-permute-start | bytes 393224 | tf_op jit(solution)/shard_map/ppermute | solution.py:273
  86.5 0.3 collective-permute-start.11
  86.8 0.0 collective-permute-done.9.core
  86.8 4.5 %collective-permute-done.10.cross = bf16[128,512]{1,0:T(8,128)(2,1)S(1)} collective-permute-done((bf16[128,512]{1,0:T(8,128)(2,1)S(1)}, bf16[128,512]{1,0:T(8,128)(2,1)S(1)}, u32[]{:S(2)}, u32[]{:S(2)}) %collective-permute-start.10) | collective-permute-done | bytes 131104 | tf_op jit(solution)/shard_map/ppermute | solution.py:273
  91.3 1.9 %collective-permute-done.11.both = bf16[128,512]{1,0:T(8,128)(2,1)S(1)} collective-permute-done((bf16[128,512]{1,0:T(8,128)(2,1)S(1)}, bf16[128,512]{1,0:T(8,128)(2,1)S(1)}, u32[]{:S(2)}, u32[]{:S(2)}) %collective-permute-start.11) | collective-permute-done | bytes 131104 | tf_op jit(solution)/shard_map/ppermute | solution.py:274
  93.2 0.0 collective-permute-done.8.w_other
  93.2 0.0 copy-done
  93.2 7.9 %shard_map.49 = bf16[128,4096]{1,0:T(8,128)(2,1)S(1)} custom-call(s32[1]{0:T(128)} %bitcast.place, bf16[128,512]{1,0:T(8,128)(2,1)S(1)} %get-tuple-element.21.same, bf16[128,512]{1,0:T(8,128)(2,1)S(1)} %collective-permute-done.9.core, bf16[128,512]{1,0:T(8,128)(2,1)S(1)} %collective-permute-done.10.cross, bf16[128,512]{1,0:T(8,128)(2,1)S(1)} %collective-permute-done.11.both, ...), custom_call_target="tpu_custom_call" | custom-call | flops 2147483648 | bytes 16777216 | tf_op jit(solution)/shard_map/pallas_call | solution.py:161
  101.1 1.6 %collective-permute-start.12 = (bf16[128,4096]{1,0:T(8,128)(2,1)S(1)}, bf16[128,4096]{1,0:T(8,128)(2,1)S(1)}, u32[]{:S(2)}, u32[]{:S(2)}) collective-permute-start(bf16[128,4096]{1,0:T(8,128)(2,1)S(1)} %shard_map.49), channel_id=1, source_target_pairs={{0,2},{1,3},{2,0},{3,1},{4,6},{5,7},{6,4},{7,5},{8,10},{9,11},{10,... | collective-permute-start | bytes 3145736 | tf_op jit(solution)/shard_map/ppermute | solution.py:278
  102.7 0.0 collective-permute-start.5
  102.7 1.5 %collective-permute-start.6 = (bf16[128,512]{1,0:T(8,128)(2,1)S(1)}, bf16[128,512]{1,0:T(8,128)(2,1)S(1)}, u32[]{:S(2)}, u32[]{:S(2)}) collective-permute-start(bf16[128,512]{1,0:T(8,128)(2,1)S(1)} %get-tuple-element.19), channel_id=1, source_target_pairs={{0,4},{4,0},{8,12},{12,8},{16,20},{20,16},{24,28},{28,24},{1,5},{5... | collective-permute-start | bytes 393224 | tf_op jit(solution)/shard_map/ppermute | solution.py:273
  104.2 0.4 collective-permute-start.7
  104.6 0.0 collective-permute-done.5.core
  104.6 4.4 %collective-permute-done.6.cross = bf16[128,512]{1,0:T(8,128)(2,1)S(1)} collective-permute-done((bf16[128,512]{1,0:T(8,128)(2,1)S(1)}, bf16[128,512]{1,0:T(8,128)(2,1)S(1)}, u32[]{:S(2)}, u32[]{:S(2)}) %collective-permute-start.6) | collective-permute-done | bytes 131104 | tf_op jit(solution)/shard_map/ppermute | solution.py:273
  109.0 2.0 %collective-permute-done.7.both = bf16[128,512]{1,0:T(8,128)(2,1)S(1)} collective-permute-done((bf16[128,512]{1,0:T(8,128)(2,1)S(1)}, bf16[128,512]{1,0:T(8,128)(2,1)S(1)}, u32[]{:S(2)}, u32[]{:S(2)}) %collective-permute-start.7) | collective-permute-done | bytes 131104 | tf_op jit(solution)/shard_map/ppermute | solution.py:274
  111.0 7.9 %shard_map.48 = f32[128,4096]{1,0:T(8,128)S(1)} custom-call(s32[1]{0:T(128)} %bitcast.place, bf16[128,512]{1,0:T(8,128)(2,1)S(1)} %get-tuple-element.17.same, bf16[128,512]{1,0:T(8,128)(2,1)S(1)} %collective-permute-done.5.core, bf16[128,512]{1,0:T(8,128)(2,1)S(1)} %collective-permute-done.6.cross, bf16[128,512]{1,0:T(8,128)(2,1)S(1)} %collective-permute-done.7.both, ...), custom_call_target="tpu_custom_call" | custom-call | flops 2147483648 | bytes 16777216 | tf_op jit(solution)/shard_map/pallas_call | solution.py:161
  119.0 7.6 %collective-permute-done.12 = bf16[128,4096]{1,0:T(8,128)(2,1)S(1)} collective-permute-done((bf16[128,4096]{1,0:T(8,128)(2,1)S(1)}, bf16[128,4096]{1,0:T(8,128)(2,1)S(1)}, u32[]{:S(2)}, u32[]{:S(2)}) %collective-permute-start.12) | collective-permute-done | bytes 1048608 | tf_op jit(solution)/shard_map/ppermute | solution.py:278
  126.5 1.2 add_convert_fusion
  (3 shorter events, 0.0 us)
Async XLA Ops:
  0.0 93.2 %collective-permute-start.8 = (bf16[1024,4096]{1,0:T(8,128)(2,1)}, bf16[1024,4096]{1,0:T(8,128)(2,1)}, u32[]{:S(2)}, u32[]{:S(2)}) collective-permute-start(bf16[1024,4096]{1,0:T(8,128)(2,1)} %w_mine.3), channel_id=1, source_target_pairs={{0,1},{1,0},{2,3},{3,2},{4,5},{5,4},{6,7},{7,6},{8,9},{9,8},{10,11... | collective-permute-start | bytes 25165832 | tf_op jit(solution)/shard_map/ppermute | solution.py:208
  0.0 28.9 %copy-start.1 = (bf16[512,1024]{1,0:T(8,128)(2,1)S(1)}, bf16[512,1024]{1,0:T(8,128)(2,1)}, u32[]{:S(2)}) copy-start(bf16[512,1024]{1,0:T(8,128)(2,1)} %param.4) | copy-start | bytes 3145732
  1.8 32.5 %copy-start.2 = (s32[4096]{0:T(1024)S(1)}, s32[4096]{0:T(1024)}, u32[]{:S(2)}) copy-start(s32[4096]{0:T(1024)} %param.7) | copy-start | bytes 49156
  1.8 25.7 %collective-permute-start.2 = (bf16[2,512,512]{2,1,0:T(8,128)(2,1)S(1)}, bf16[2,512,512]{2,1,0:T(8,128)(2,1)}, u32[]{:S(2)}, u32[]{:S(2)}) collective-permute-start(bf16[2,512,512]{2,1,0:T(8,128)(2,1)S(1)} %get-tuple-element.25), channel_id=1, source_target_pairs={{0,4},{4,0},{8,12},{12,8},{16,20},{20,16},{24,28},{28,24},{1,5},{5... | collective-permute-start | bytes 3145736 | tf_op jit(solution)/shard_map/ppermute | solution.py:206
  3.4 57.2 %collective-permute-start.1 = (bf16[2,512,512]{2,1,0:T(8,128)(2,1)S(1)}, bf16[2,512,512]{2,1,0:T(8,128)(2,1)S(1)}, u32[]{:S(2)}, u32[]{:S(2)}) collective-permute-start(bf16[2,512,512]{2,1,0:T(8,128)(2,1)S(1)} %get-tuple-element.26.kv_own), channel_id=1, source_target_pairs={{0,8},{4,12},{8,16},{12,20},{16,24},{20,28},{1,9},{5,13},{9,17},{1... | collective-permute-start | bytes 3145736 | tf_op jit(solution)/shard_map/ppermute | solution.py:207
  27.6 38.0 %collective-permute-start.3 = (bf16[2,512,512]{2,1,0:T(8,128)(2,1)}, bf16[2,512,512]{2,1,0:T(8,128)(2,1)}, u32[]{:S(2)}, u32[]{:S(2)}) collective-permute-start(bf16[2,512,512]{2,1,0:T(8,128)(2,1)} %collective-permute-done.2.kv_other), channel_id=1, source_target_pairs={{0,8},{4,12},{8,16},{12,20},{16,24},{20,28},{1,9},{5,13},{9,17},{1... | collective-permute-start | bytes 3145736 | tf_op jit(solution)/shard_map/ppermute | solution.py:210
  29.8 13.9 %collective-permute-start = (bf16[512,512]{1,0:T(8,128)(2,1)}, bf16[512,512]{1,0:T(8,128)(2,1)}, u32[]{:S(2)}, u32[]{:S(2)}) collective-permute-start(bf16[512,512]{1,0:T(8,128)(2,1)} %get-tuple-element.27), channel_id=1, source_target_pairs={{0,4},{4,0},{8,12},{12,8},{16,20},{20,16},{24,28},{28,24},{1,5},{5... | collective-permute-start | bytes 1572872 | tf_op jit(solution)/shard_map/ppermute | solution.py:209
  33.1 32.5 %collective-permute-start.4 = (bf16[2,128,512]{2,1,0:T(8,128)(2,1)}, bf16[2,128,512]{2,1,0:T(8,128)(2,1)S(1)}, u32[]{:S(2)}, u32[]{:S(2)}) collective-permute-start(bf16[2,128,512]{2,1,0:T(8,128)(2,1)} %slice_select_fusion), channel_id=1, source_target_pairs={{0,16},{4,20},{8,24},{12,28},{1,17},{5,21},{9,25},{13,29},{2,18},{... | collective-permute-start | bytes 786440 | tf_op jit(solution)/shard_map/ppermute | solution.py:212
  43.7 49.6 %copy-start = (bf16[1024,4096]{1,0:T(8,128)(2,1)S(1)}, bf16[1024,4096]{1,0:T(8,128)(2,1)}, u32[]{:S(2)}) copy-start(bf16[1024,4096]{1,0:T(8,128)(2,1)} %w_mine.3) | copy-start | bytes 25165828
  84.9 1.9 %collective-permute-start.9 = (bf16[128,512]{1,0:T(8,128)(2,1)S(1)}, bf16[128,512]{1,0:T(8,128)(2,1)S(1)}, u32[]{:S(2)}, u32[]{:S(2)}) collective-permute-start(bf16[128,512]{1,0:T(8,128)(2,1)S(1)} %get-tuple-element.22), channel_id=1, source_target_pairs={{0,1},{1,0},{2,3},{3,2},{4,5},{5,4},{6,7},{7,6},{8,9},{9,8},{10,11... | collective-permute-start | bytes 393224 | tf_op jit(solution)/shard_map/ppermute | solution.py:272
  85.0 6.4 %collective-permute-start.10 = (bf16[128,512]{1,0:T(8,128)(2,1)S(1)}, bf16[128,512]{1,0:T(8,128)(2,1)S(1)}, u32[]{:S(2)}, u32[]{:S(2)}) collective-permute-start(bf16[128,512]{1,0:T(8,128)(2,1)S(1)} %get-tuple-element.23), channel_id=1, source_target_pairs={{0,4},{4,0},{8,12},{12,8},{16,20},{20,16},{24,28},{28,24},{1,5},{5... | collective-permute-start | bytes 393224 | tf_op jit(solution)/shard_map/ppermute | solution.py:273
  86.5 6.7 %collective-permute-start.11 = (bf16[128,512]{1,0:T(8,128)(2,1)S(1)}, bf16[128,512]{1,0:T(8,128)(2,1)S(1)}, u32[]{:S(2)}, u32[]{:S(2)}) collective-permute-start(bf16[128,512]{1,0:T(8,128)(2,1)S(1)} %get-tuple-element.24), channel_id=1, source_target_pairs={{0,5},{1,4},{2,7},{3,6},{4,1},{5,0},{6,3},{7,2},{8,13},{9,12},{10,... | collective-permute-start | bytes 393224 | tf_op jit(solution)/shard_map/ppermute | solution.py:274
  101.1 25.4 %collective-permute-start.12 = (bf16[128,4096]{1,0:T(8,128)(2,1)S(1)}, bf16[128,4096]{1,0:T(8,128)(2,1)S(1)}, u32[]{:S(2)}, u32[]{:S(2)}) collective-permute-start(bf16[128,4096]{1,0:T(8,128)(2,1)S(1)} %shard_map.49), channel_id=1, source_target_pairs={{0,2},{1,3},{2,0},{3,1},{4,6},{5,7},{6,4},{7,5},{8,10},{9,11},{10,... | collective-permute-start | bytes 3145736 | tf_op jit(solution)/shard_map/ppermute | solution.py:278
  102.7 1.9 %collective-permute-start.5 = (bf16[128,512]{1,0:T(8,128)(2,1)S(1)}, bf16[128,512]{1,0:T(8,128)(2,1)S(1)}, u32[]{:S(2)}, u32[]{:S(2)}) collective-permute-start(bf16[128,512]{1,0:T(8,128)(2,1)S(1)} %get-tuple-element.18), channel_id=1, source_target_pairs={{0,1},{1,0},{2,3},{3,2},{4,5},{5,4},{6,7},{7,6},{8,9},{9,8},{10,11... | collective-permute-start | bytes 393224 | tf_op jit(solution)/shard_map/ppermute | solution.py:272
  102.7 6.3 %collective-permute-start.6 = (bf16[128,512]{1,0:T(8,128)(2,1)S(1)}, bf16[128,512]{1,0:T(8,128)(2,1)S(1)}, u32[]{:S(2)}, u32[]{:S(2)}) collective-permute-start(bf16[128,512]{1,0:T(8,128)(2,1)S(1)} %get-tuple-element.19), channel_id=1, source_target_pairs={{0,4},{4,0},{8,12},{12,8},{16,20},{20,16},{24,28},{28,24},{1,5},{5... | collective-permute-start | bytes 393224 | tf_op jit(solution)/shard_map/ppermute | solution.py:273
  104.2 6.8 %collective-permute-start.7 = (bf16[128,512]{1,0:T(8,128)(2,1)S(1)}, bf16[128,512]{1,0:T(8,128)(2,1)S(1)}, u32[]{:S(2)}, u32[]{:S(2)}) collective-permute-start(bf16[128,512]{1,0:T(8,128)(2,1)S(1)} %get-tuple-element.20), channel_id=1, source_target_pairs={{0,5},{1,4},{2,7},{3,6},{4,1},{5,0},{6,3},{7,2},{8,13},{9,12},{10,... | collective-permute-start | bytes 393224 | tf_op jit(solution)/shard_map/ppermute | solution.py:274

commit v2 on v1

v2 whole, which is shorter than its diff:
```python
import functools
import math

import jax
import jax.numpy as jnp
from jax import lax
from jax.experimental import pallas as pl
from jax.experimental.pallas import tpu as pltpu
from jax.sharding import PartitionSpec as P

HD = 128
TILE = 256
FAR_ROWS = 128
NEG = -1e30
SCALE = HD ** (-0.5) * math.log2(math.e)


def tile_bias(key_docs, query_docs, causal):
    allowed = key_docs == query_docs
    if causal:
        keys = lax.broadcasted_iota(jnp.int32, allowed.shape, 0)
        queries = lax.broadcasted_iota(jnp.int32, allowed.shape, 1)
        allowed = allowed & (keys <= queries)
    return jnp.where(allowed, jnp.float32(0), jnp.float32(NEG))


def scores_of(key, query, bias):
    raw = lax.dot_general(key, query, (((1,), (1,)), ((), ())), preferred_element_type=jnp.float32)
    return raw * SCALE + bias


def head_cols(head):
    return pl.ds(head * HD, HD)


def fresh_tiles(heads, keys, queries, values, bias, span, summed, stats):
    entries = [scores_of(k, q, bias) for k, q in zip(keys, queries)]
    tops = [jnp.max(e, axis=0, keepdims=True) for e in entries]
    weights = [jnp.exp2(e - t) for e, t in zip(entries, tops)]
    totals = [jnp.sum(w, axis=0, keepdims=True) for w in weights]
    sums = [
        jnp.dot(v, w.astype(jnp.bfloat16), preferred_element_type=jnp.float32)
        for v, w in zip(values, weights)
    ]
    stats[:, span] = jnp.concatenate(tops + totals, axis=0)
    for h in range(heads):
        summed[head_cols(h), span] = sums[h]


def fold_tiles(heads, keys, queries, values, bias, span, summed, stats):
    before = stats[:, span]
    olds = [summed[head_cols(h), span] for h in range(heads)]
    entries = [scores_of(k, q, bias) for k, q in zip(keys, queries)]
    tops = [
        jnp.maximum(before[h : h + 1], jnp.max(e, axis=0, keepdims=True))
        for h, e in enumerate(entries)
    ]
    shrinks = [jnp.exp2(before[h : h + 1] - t) for h, t in enumerate(tops)]
    weights = [jnp.exp2(e - t) for e, t in zip(entries, tops)]
    totals = [
        before[heads + h : heads + h + 1] * shrinks[h] + jnp.sum(w, axis=0, keepdims=True)
        for h, w in enumerate(weights)
    ]
    sums = [
        o * s + jnp.dot(v, w.astype(jnp.bfloat16), preferred_element_type=jnp.float32)
        for o, s, v, w in zip(olds, shrinks, values, weights)
    ]
    stats[:, span] = jnp.concatenate(tops + totals, axis=0)
    for h in range(heads):
        summed[head_cols(h), span] = sums[h]


def local_kernel(heads, rows, pad, place, docs, q_own, q_other, kv_own, kv_other, docs_col, docs_row,
                 summed, stats, qs, ks, vts):
    half = rows // 2
    own = pl.ds(pl.multiple_of(place[0] * half, half), half)
    other = pl.ds(pl.multiple_of((1 - place[0]) * half, half), half)
    qs[own, :] = q_own[...]
    qs[other, :] = q_other[...]
    ks[own, :] = kv_own[0]
    ks[other, :] = kv_other[0]
    for head in range(heads):
        vts[head_cols(head), own] = kv_own[1, :, head_cols(head)].T
        vts[head_cols(head), other] = kv_other[1, :, head_cols(head)].T

    def one_tile(step, _):
        here = pl.multiple_of(step * TILE, TILE)
        span = pl.ds(here, TILE)
        query_docs = docs_row[:, span]

        def operands(keys_at):
            return (
                [ks[keys_at, head_cols(h)] for h in range(heads)],
                [qs[span, head_cols(h)] for h in range(heads)],
                [vts[head_cols(h), keys_at] for h in range(heads)],
            )

        bias = tile_bias(docs_col[span, :], query_docs, True)
        fresh_tiles(heads, *operands(span), bias, span, summed, stats)
        first_doc = docs[pad + here]
        live = jnp.int32(0)
        for back in range(1, rows // TILE):
            last = jnp.maximum(pad + here - (back - 1) * TILE - 1, 0)
            live += ((docs[last] == first_doc) & (step >= back)).astype(jnp.int32)

        def one_back(back, _):
            there = pl.ds(pl.multiple_of(here - (back + 1) * TILE, TILE), TILE)
            bias = tile_bias(docs_col[there, :], query_docs, False)
            fold_tiles(heads, *operands(there), bias, span, summed, stats)
            return 0

        lax.fori_loop(0, live, one_back, 0)
        return 0

    lax.fori_loop(0, rows // TILE, one_tile, 0)


def remote_kernel(heads, rows, pad, place, docs, q_own, q_other, kv_same, kv_cross, kv_far, docs_col, docs_row,
                  summed_in, stats_in, *rest):
    outs, (qs, ks, vts, done, summed, stats) = rest[:8], rest[8:]
    half = rows // 2
    side = place[0]
    qs[pl.ds(pl.multiple_of(side * half, half), half), :] = q_own[...]
    qs[pl.ds(pl.multiple_of((1 - side) * half, half), half), :] = q_other[...]
    front = pad - rows

    def reach(query_at):
        first_doc = docs[pad + query_at]
        live = jnp.int32(0)
        for back in range(pad // TILE):
            live += (docs[pad - back * TILE - 1] == first_doc).astype(jnp.int32)
        return live

    most = reach(0)

    def place_keys(source, at, lead, size):
        ks[pl.ds(at + lead, size), :] = source[0]
        for head in range(heads):
            vts[head_cols(head), pl.ds(at + lead, size)] = source[1, :, head_cols(head)].T

    for source, offset in ((kv_same, side * half), (kv_cross, (1 - side) * half)):
        for part in range(half // TILE):
            at = pl.multiple_of(front + offset + part * TILE, TILE)

            @pl.when(most > pad // TILE - 1 - at // TILE)
            def _():
                place_keys(source.at[:, pl.ds(part * TILE, TILE)], at, 0, TILE)

    @pl.when(most > pad // TILE - 1)
    def _():
        ks[: front - FAR_ROWS, :] = jnp.zeros((front - FAR_ROWS, heads * HD), jnp.bfloat16)
        vts[:, : front - FAR_ROWS] = jnp.zeros((heads * HD, front - FAR_ROWS), jnp.bfloat16)
        place_keys(kv_far, front - FAR_ROWS, 0, FAR_ROWS)

    whole = pl.ds(0, TILE)

    def one_tile(step, _):
        here = pl.multiple_of(step * TILE, TILE)
        span = pl.ds(here, TILE)
        stats[...] = stats_in[:, span]
        summed[...] = summed_in[:, span]

        def one_back(back, _):
            there = pl.ds(pl.multiple_of(pad - (back + 1) * TILE, TILE), TILE)
            bias = tile_bias(docs_col[there, :], docs_row[:, span], False)
            fold_tiles(
                heads,
                [ks[there, head_cols(h)] for h in range(heads)],
                [qs[span, head_cols(h)] for h in range(heads)],
                [vts[head_cols(h), there] for h in range(heads)],
                bias, whole, summed, stats,
            )
            return 0

        lax.fori_loop(0, reach(here), one_back, 0)
        for head in range(heads):
            part = summed[head_cols(head), :] / stats[heads + head : heads + head + 1, :]
            done[span, head_cols(head)] = part.astype(jnp.bfloat16).T
        return 0

    lax.fori_loop(0, rows // TILE, one_tile, 0)
    block = outs[0].shape[0]
    for number, out in enumerate(outs):
        out[...] = done[pl.ds(pl.multiple_of(place[1 + number] * block, block), block), :]


def project_kernel(first, second, w_first, w_second, *rest):
    out = rest[-1]
    term = jnp.dot(first[...], w_first[...], preferred_element_type=jnp.float32) + jnp.dot(
        second[...], w_second[...], preferred_element_type=jnp.float32
    )
    if len(rest) == 2:
        term = term + rest[0][...]
    out[...] = term.astype(out.dtype)


def project_body(place, *refs):
    project_kernel(*refs)


def project(row, first, second, w_first, w_second, begun, kind):
    block, width = first.shape
    columns = w_first.shape[1]
    step = 1024
    whole = pl.BlockSpec((block, width), lambda i, s: (0, 0))
    slab = pl.BlockSpec((width, step), lambda i, s: (s[0], i))
    tile = pl.BlockSpec((block, step), lambda i, s: (0, i))
    more = [] if begun is None else [begun]
    return pl.pallas_call(
        project_body,
        grid_spec=pltpu.PrefetchScalarGridSpec(
            num_scalar_prefetch=1,
            grid=(columns // step,),
            in_specs=[whole] * 2 + [slab] * 2 + [tile] * len(more),
            out_specs=tile,
        ),
        out_shape=jax.ShapeDtypeStruct((block, columns), kind),
        compiler_params=pltpu.CompilerParams(vmem_limit_bytes=24 << 20),
        cost_estimate=pl.CostEstimate(
            flops=4 * block * width * columns, bytes_accessed=4 * width * columns, transcendentals=0
        ),
    )(row, first, second, w_first, w_second, *more)


def per_device(queries, keys_values, w_out, doc_index):
    shard, width = queries.shape
    n_ctx, n_head = lax.axis_size("ctx"), lax.axis_size("head")
    me, group = lax.axis_index("ctx"), lax.axis_index("head")
    half = width // 2
    heads = half // HD
    rows = 2 * shard
    pad = rows + TILE
    side = lax.rem(me, 2)
    base = (me - side) * shard

    padded = jnp.concatenate([jnp.full((pad,), -1, jnp.int32), doc_index])
    docs = lax.dynamic_slice_in_dim(padded, base, pad + rows)
    docs_col = docs.reshape(pad + rows, 1)
    docs_row = docs[pad:].reshape(1, rows)

    swap = [(c, c ^ 1) for c in range(n_ctx)]
    hop = [(c, c + 2) for c in range(n_ctx - 2)]
    far = [(c, c + 4) for c in range(n_ctx - 4)]
    core = [(h, h ^ 1) for h in range(n_head)]
    both = [
        (c * n_head + h, (c ^ 1) * n_head + (h ^ 1)) for c in range(n_ctx) for h in range(n_head)
    ]
    far_y = [(h, h ^ 2) for h in range(n_head)]

    kv_send = lax.dynamic_slice_in_dim(keys_values, (1 - side) * half, half, 2)
    kv_own = lax.dynamic_slice_in_dim(keys_values, side * half, half, 2)
    q_send = lax.dynamic_slice_in_dim(queries, (1 - side) * half, half, 1)
    q_own = lax.dynamic_slice_in_dim(queries, side * half, half, 1)
    kv_other = lax.ppermute(kv_send, "ctx", swap)
    kv_same = lax.ppermute(kv_own, "ctx", hop)
    w_other = lax.ppermute(w_out, "head", core)
    q_send, kv_other = lax.optimization_barrier((q_send, kv_other))
    q_other = lax.ppermute(q_send, "ctx", swap)
    kv_cross = lax.ppermute(kv_other, "ctx", hop)
    tail = jnp.where(side == 1, kv_own[:, shard - FAR_ROWS :], kv_other[:, shard - FAR_ROWS :])
    kv_far = lax.ppermute(tail, "ctx", far)

    side_1 = side.reshape(1).astype(jnp.int32)
    vmem = pl.BlockSpec(memory_space=pltpu.VMEM)
    smem = pl.BlockSpec(memory_space=pltpu.SMEM)
    summed, stats = pl.pallas_call(
        functools.partial(local_kernel, heads, rows, pad),
        in_specs=[smem, smem] + [vmem] * 6,
        out_specs=[vmem] * 2,
        out_shape=[
            jax.ShapeDtypeStruct((half, rows), jnp.float32),
            jax.ShapeDtypeStruct((2 * heads, rows), jnp.float32),
        ],
        scratch_shapes=[
            pltpu.VMEM((rows, half), jnp.bfloat16),
            pltpu.VMEM((rows, half), jnp.bfloat16),
            pltpu.VMEM((half, rows), jnp.bfloat16),
        ],
        compiler_params=pltpu.CompilerParams(vmem_limit_bytes=24 << 20),
        cost_estimate=pl.CostEstimate(
            flops=2 * rows * rows * half, bytes_accessed=6 << 20, transcendentals=rows * rows * heads // 2
        ),
    )(side_1, docs, q_own, q_other, kv_own, kv_other, docs_col[pad:], docs_row)

    block = shard // n_head
    places = [side]
    for wave in range(2):
        y_part = (group // 2) ^ (1 - wave)
        for turn in range(4):
            to_side, to_core = side ^ (turn // 2), lax.rem(group, 2) ^ (turn % 2)
            places.append(to_side * n_head + y_part * 2 + to_core)
    place = jnp.stack(places).astype(jnp.int32)
    pieces = pl.pallas_call(
        functools.partial(remote_kernel, heads, rows, pad),
        in_specs=[smem, smem] + [vmem] * 9,
        out_specs=[vmem] * 8,
        out_shape=[jax.ShapeDtypeStruct((block, half), jnp.bfloat16)] * 8,
        scratch_shapes=[
            pltpu.VMEM((rows, half), jnp.bfloat16),
            pltpu.VMEM((pad, half), jnp.bfloat16),
            pltpu.VMEM((half, pad), jnp.bfloat16),
            pltpu.VMEM((rows, half), jnp.bfloat16),
            pltpu.VMEM((half, TILE), jnp.float32),
            pltpu.VMEM((2 * heads, TILE), jnp.float32),
        ],
        compiler_params=pltpu.CompilerParams(vmem_limit_bytes=24 << 20),
        cost_estimate=pl.CostEstimate(
            flops=2 * rows * rows * half, bytes_accessed=8 << 20, transcendentals=rows * rows * heads // 2
        ),
    )(place, docs, q_own, q_other, kv_same, kv_cross, kv_far, docs_col[:pad], docs_row, summed, stats)

    here, there = side_1, 1 - side_1

    def projected(pieces, kind):
        mine = pieces[0]
        core_piece = lax.ppermute(pieces[1], "head", core)
        cross_piece = lax.ppermute(pieces[2], "ctx", swap)
        both_piece = lax.ppermute(pieces[3], ("ctx", "head"), both)
        begun = project(here, mine, core_piece, w_out, w_other, None, jnp.float32)
        return project(there, cross_piece, both_piece, w_out, w_other, begun, kind)

    leaving = projected(pieces[:4], jnp.bfloat16)
    arrived = lax.ppermute(leaving, "head", far_y)
    staying = projected(pieces[4:], jnp.float32)
    return (staying + arrived.astype(jnp.float32)).astype(jnp.bfloat16)


def solution(mesh):
    in_specs = (P("ctx", "head"), P(None, "ctx", "head"), P("head", None), P())
    out_specs = P(("ctx", "head"), None)
    return jax.shard_map(
        per_device, mesh=mesh, in_specs=in_specs, out_specs=out_specs, check_vma=False
    )
```

time: 126 us -> 111 us (0.88); the launches traced: 128 us -> 110 us
  Pallas kernels: 52 us -> 30.4 us
  local copies, waits for them, and re-layouts: 3.24 us -> 7.08 us
    pallas_call x1, Pallas kernels: 19.3 us -> 4.65 us  [per_device(): pl.pallas_call(functools.partial(remote_kernel, heads, rows, pad), in_spe...]
    ppermute x6, waiting for transfers between devices: 12.9 us -> 4.37 us  [the longest x2 3.94 us: projected(): both_piece = lax.ppermute(pieces[3], ('ctx', 'head'), both)]
    pallas_call x1, Pallas kernels: 16.9 us -> 8.8 us  [per_device(): pl.pallas_call(functools.partial(local_kernel, heads, rows, pad), in_spec...]
    ppermute x1, waiting for transfers between devices: 4.96 us -> 12.9 us  [per_device(): kv_far = lax.ppermute(tail, 'ctx', far)]
    ppermute x1, waiting for transfers between devices: 7.58 us -> 11.2 us  [per_device(): arrived = lax.ppermute(leaving, 'head', far_y)]
    ppermute x1, waiting for transfers between devices: 8.76 us -> 6.98 us  [per_device(): q_other = lax.ppermute(q_send, 'ctx', swap)]
    slice x3 -> x4, local copies, waits for them, and re-layouts: 0.09 us -> 1.41 us  [the longest x1 1.03 us: per_device(): docs_col[pad:]]
    pallas_call x2 -> x4, Pallas kernels: 15.8 us -> 17 us  [project(): pl.pallas_call(project_body, grid_spec=pltpu.PrefetchScalarGridSpec(num_s...]
  transfers between devices with their start and end apart: 13 -> 13, of which waited for: 8 -> 8; matrix products, arithmetic and copies ran while one was open for 4% -> 7% of each run, Pallas kernels for 35% -> 24%
where the time goes in v2:
time: 111 us; the launch traced here: 110 us
  waiting for transfers between devices  57.4 us (52%)
  Pallas kernels  30.4 us (27%)
  starting transfers between devices  12.3 us (11%)
  local copies, waits for them, and re-layouts  7.08 us (6%)
  other arithmetic  2.98 us (3%)
    ppermute x1, waiting for transfers between devices, per_device(): kv_other = lax.ppermute(kv_send, 'ctx', swap)  21.9 us
    pallas_call x4, Pallas kernels, project(): pl.pallas_call(project_body, grid_spec=pltpu.PrefetchScalarGridSpec(num_s...  17 us
    ppermute x1, waiting for transfers between devices, per_device(): kv_far = lax.ppermute(tail, 'ctx', far)  12.9 us
    ppermute x1, waiting for transfers between devices, per_device(): arrived = lax.ppermute(leaving, 'head', far_y)  11.2 us
    pallas_call x1, Pallas kernels, per_device(): pl.pallas_call(functools.partial(local_kernel, heads, rows, pad), in_spec...  8.8 us
    ppermute x1, waiting for transfers between devices, per_device(): q_other = lax.ppermute(q_send, 'ctx', swap)  6.98 us
    pallas_call x1, Pallas kernels, per_device(): pl.pallas_call(functools.partial(remote_kernel, heads, rows, pad), in_spe...  4.65 us
    ppermute x2, waiting for transfers between devices, projected(): both_piece = lax.ppermute(pieces[3], ('ctx', 'head'), both)  3.94 us
  transfers between devices with their start and end apart: 13, of which 8 were waited for; matrix products, arithmetic and copies ran while one was open for 7% of the time, Pallas kernels for 24%

profile of v2, /device:TPU:24, one launch (start us, length us, event | category | flops | bytes accessed | tf_op | source)
XLA Modules:
  0.0 110.3 jit_solution(8914833312680883752)
XLA Ops:
  0.0 0.0 collective-permute-start.7
  0.0 0.0 copy-start.2
  0.0 2.8 %constant_dynamic-slice_fusion = (bf16[2,512,512]{2,1,0:T(8,128)(2,1)}, bf16[2,512,512]{2,1,0:T(8,128)(2,1)S(1)}) fusion(bf16[2,512,1024]{2,1,0:T(8,128)(2,1)} %param.5, s32[]{:T(128)S(6)} %select_n.27, s32[]{:T(128)S(6)} %select_n.28), kind=kLoop, calls=%fused_computation.5 | loop fusion | bytes 4194312 | tf_op jit(solution)/shard_map/dynamic_slice | solution.py:251
  2.8 0.0 copy-start.3
  2.8 1.5 %collective-permute-start = (bf16[2,512,512]{2,1,0:T(8,128)(2,1)S(1)}, bf16[2,512,512]{2,1,0:T(8,128)(2,1)}, u32[]{:S(2)}, u32[]{:S(2)}) collective-permute-start(bf16[2,512,512]{2,1,0:T(8,128)(2,1)S(1)} %get-tuple-element.30), channel_id=1, source_target_pairs={{0,4},{4,0},{8,12},{12,8},{16,20},{20,16},{24,28},{28,24},{1,5},{5... | collective-permute-start | bytes 3145736 | tf_op jit(solution)/shard_map/ppermute | solution.py:254
  4.3 1.3 %collective-permute-start.2 = (bf16[2,512,512]{2,1,0:T(8,128)(2,1)}, bf16[2,512,512]{2,1,0:T(8,128)(2,1)S(1)}, u32[]{:S(2)}, u32[]{:S(2)}) collective-permute-start(bf16[2,512,512]{2,1,0:T(8,128)(2,1)} %get-tuple-element.29.kv_own), channel_id=1, source_target_pairs={{0,8},{4,12},{8,16},{12,20},{16,24},{20,28},{1,9},{5,13},{9,17},{1... | collective-permute-start | bytes 3145736 | tf_op jit(solution)/shard_map/ppermute | solution.py:255
  5.6 0.0 copy-done.2
  5.6 0.9 constant_dynamic-slice_fusion.2
  6.5 21.9 %collective-permute-done.kv_other = bf16[2,512,512]{2,1,0:T(8,128)(2,1)} collective-permute-done((bf16[2,512,512]{2,1,0:T(8,128)(2,1)S(1)}, bf16[2,512,512]{2,1,0:T(8,128)(2,1)}, u32[]{:S(2)}, u32[]{:S(2)}) %collective-permute-start) | collective-permute-done | bytes 1048608 | tf_op jit(solution)/shard_map/ppermute | solution.py:254
  28.5 1.3 %collective-permute-start.3 = (bf16[2,512,512]{2,1,0:T(8,128)(2,1)}, bf16[2,512,512]{2,1,0:T(8,128)(2,1)S(1)}, u32[]{:S(2)}, u32[]{:S(2)}) collective-permute-start(bf16[2,512,512]{2,1,0:T(8,128)(2,1)} %collective-permute-done.kv_other), channel_id=1, source_target_pairs={{0,8},{4,12},{8,16},{12,20},{16,24},{20,28},{1,9},{5,13},{9,17},{1... | collective-permute-start | bytes 3145736 | tf_op jit(solution)/shard_map/ppermute | solution.py:259
  29.8 1.6 %collective-permute-start.1 = (bf16[512,512]{1,0:T(8,128)(2,1)}, bf16[512,512]{1,0:T(8,128)(2,1)}, u32[]{:S(2)}, u32[]{:S(2)}) collective-permute-start(bf16[512,512]{1,0:T(8,128)(2,1)} %get-tuple-element.17), channel_id=1, source_target_pairs={{0,4},{4,0},{8,12},{12,8},{16,20},{20,16},{24,28},{28,24},{1,5},{5... | collective-permute-start | bytes 1572872 | tf_op jit(solution)/shard_map/ppermute | solution.py:258
  31.3 0.0 copy-done.3
  31.3 0.1 pad_dynamic-slice_fusion.1
  31.4 1.8 %dynamic-slice_select_fusion = bf16[2,128,512]{2,1,0:T(8,128)(2,1)} fusion(bf16[2,512,1024]{2,1,0:T(8,128)(2,1)} %param.5, s32[]{:T(128)S(6)} %add.73, s32[]{:T(128)S(6)} %select_n.27, bf16[2,512,512]{2,1,0:T(8,128)(2,1)} %collective-permute-done.kv_other, pred[]{:T(512)S(6)} %eq.3), kind=kLoop, calls=%fused_computation.1 | loop fusion | flops 131072 | bytes 786441 | tf_op jit(solution)/shard_map/jit(_where)/select_n | solution.py:260
  33.2 1.3 %collective-permute-start.4 = (bf16[2,128,512]{2,1,0:T(8,128)(2,1)}, bf16[2,128,512]{2,1,0:T(8,128)(2,1)S(1)}, u32[]{:S(2)}, u32[]{:S(2)}) collective-permute-start(bf16[2,128,512]{2,1,0:T(8,128)(2,1)} %dynamic-slice_select_fusion), channel_id=1, source_target_pairs={{0,16},{4,20},{8,24},{12,28},{1,17},{5,21},{9,25},{13,29},{2,18},{... | collective-permute-start | bytes 786440 | tf_op jit(solution)/shard_map/ppermute | solution.py:261
  34.5 0.1 pad_dynamic-slice_fusion
  34.6 1.0 copy.5.docs_col
  35.6 0.2 slice.25.docs_col
  35.9 0.1 stack.36.place
  35.9 0.8 pad_dynamic-slice_fusion.2.docs
  36.7 7.0 %collective-permute-done.1.q_other = bf16[512,512]{1,0:T(8,128)(2,1)} collective-permute-done((bf16[512,512]{1,0:T(8,128)(2,1)}, bf16[512,512]{1,0:T(8,128)(2,1)}, u32[]{:S(2)}, u32[]{:S(2)}) %collective-permute-start.1) | collective-permute-done | bytes 524320 | tf_op jit(solution)/shard_map/ppermute | solution.py:258
  43.7 0.0 copy-start.1
  43.7 1.0 copy-done.1
  44.8 0.0 copy-start
  44.8 8.8 %shard_map.46 = (f32[512,1024]{1,0:T(8,128)S(1)}, f32[8,1024]{1,0:T(8,128)S(1)}) custom-call(s32[1]{0:T(128)} %bitcast.place, s32[2304]{0:T(1024)S(1)} %pad_dynamic-slice_fusion.2.docs, bf16[512,512]{1,0:T(8,128)(2,1)S(1)} %get-tuple-element.32.q_own, bf16[512,512]{1,0:T(8,128)(2,1)} %collective-permute-done.1.q_other, ...), custom_call_target="tpu_custom_call" | custom-call | flops 1073741824 | bytes 6291456 | tf_op jit(solution)/shard_map/pallas_call | solution.py:266
  53.6 0.0 collective-permute-done.2.kv_same
  53.6 12.9 %collective-permute-done.4.kv_far = bf16[2,128,512]{2,1,0:T(8,128)(2,1)S(1)} collective-permute-done((bf16[2,128,512]{2,1,0:T(8,128)(2,1)}, bf16[2,128,512]{2,1,0:T(8,128)(2,1)S(1)}, u32[]{:S(2)}, u32[]{:S(2)}) %collective-permute-start.4) | collective-permute-done | bytes 262176 | tf_op jit(solution)/shard_map/ppermute | solution.py:261
  66.5 0.0 collective-permute-done.3.kv_cross
  66.5 4.6 %shard_map.47 = (bf16[128,512]{1,0:T(8,128)(2,1)S(1)}, bf16[128,512]{1,0:T(8,128)(2,1)S(1)}, bf16[128,512]{1,0:T(8,128)(2,1)S(1)}, bf16[128,512]{1,0:T(8,128)(2,...) custom-call(s32[9]{0:T(128)S(1)} %stack.36.place, ...), custom_call_target="tpu_custom_call" | custom-call | flops 1073741824 | bytes 8388608 | tf_op jit(solution)/shard_map/pallas_call | solution.py:293
  71.1 0.1 collective-permute-start.11
  71.2 1.6 %collective-permute-start.9 = (bf16[128,512]{1,0:T(8,128)(2,1)S(1)}, bf16[128,512]{1,0:T(8,128)(2,1)S(1)}, u32[]{:S(2)}, u32[]{:S(2)}) collective-permute-start(bf16[128,512]{1,0:T(8,128)(2,1)S(1)} %get-tuple-element.25), channel_id=1, source_target_pairs={{0,4},{4,0},{8,12},{12,8},{16,20},{20,16},{24,28},{28,24},{1,5},{5... | collective-permute-start | bytes 393224 | tf_op jit(solution)/shard_map/ppermute | solution.py:317
  72.8 0.3 collective-permute-start.10
  73.1 0.0 collective-permute-done.11.refs_1_
  73.1 0.0 collective-permute-done.7.refs_3_
  73.1 0.0 copy-done
  73.1 4.3 %shard_map.50.refs_4_ = f32[128,4096]{1,0:T(8,128)S(1)} custom-call(s32[1]{0:T(128)} %bitcast.place, bf16[128,512]{1,0:T(8,128)(2,1)S(1)} %get-tuple-element.27.refs_0_, bf16[128,512]{1,0:T(8,128)(2,1)S(1)} %collective-permute-done.11.refs_1_, bf16[1024,4096]{1,0:T(8,128)(2,1)S(1)} %copy-done, bf16[1024,4096]{1,0:T(8,128)(2,1)} %collective-permute-done.7.refs_3_), custom_call_target="tpu_custom_call" | custom-call | flops 1073741824 | bytes 8388608 | tf_op jit(solution)/shard_map/pallas_call | solution.py:209
  77.4 0.2 collective-permute-done.9.refs_0_
  77.6 1.9 %collective-permute-done.10.refs_1_ = bf16[128,512]{1,0:T(8,128)(2,1)S(1)} collective-permute-done((bf16[128,512]{1,0:T(8,128)(2,1)S(1)}, bf16[128,512]{1,0:T(8,128)(2,1)S(1)}, u32[]{:S(2)}, u32[]{:S(2)}) %collective-permute-start.10) | collective-permute-done | bytes 131104 | tf_op jit(solution)/shard_map/ppermute | solution.py:318
  79.5 4.2 %shard_map.51 = bf16[128,4096]{1,0:T(8,128)(2,1)S(1)} custom-call(s32[1]{0:T(128)S(6)} %sub.15.place, bf16[128,512]{1,0:T(8,128)(2,1)S(1)} %collective-permute-done.9.refs_0_, bf16[128,512]{1,0:T(8,128)(2,1)S(1)} %collective-permute-done.10.refs_1_, bf16[1024,4096]{1,0:T(8,128)(2,1)S(1)} %copy-done, bf16[1024,4096]{1,0:T(8,128)(2,1)} %collective-permute-done.7.refs_3_, ...), custom_call_target="tpu_custom_call" | custom-call | flops 1073741824 | bytes 8388608 | tf_op jit(solution)/shard_map/pallas_call | solution.py:209
  83.7 1.6 %collective-permute-start.12 = (bf16[128,4096]{1,0:T(8,128)(2,1)S(1)}, bf16[128,4096]{1,0:T(8,128)(2,1)S(1)}, u32[]{:S(2)}, u32[]{:S(2)}) collective-permute-start(bf16[128,4096]{1,0:T(8,128)(2,1)S(1)} %shard_map.51), channel_id=1, source_target_pairs={{0,2},{1,3},{2,0},{3,1},{4,6},{5,7},{6,4},{7,5},{8,10},{9,11},{10,... | collective-permute-start | bytes 3145736 | tf_op jit(solution)/shard_map/ppermute | solution.py:323
  85.3 0.0 collective-permute-start.8
  85.3 1.5 %collective-permute-start.5 = (bf16[128,512]{1,0:T(8,128)(2,1)S(1)}, bf16[128,512]{1,0:T(8,128)(2,1)S(1)}, u32[]{:S(2)}, u32[]{:S(2)}) collective-permute-start(bf16[128,512]{1,0:T(8,128)(2,1)S(1)} %get-tuple-element.21), channel_id=1, source_target_pairs={{0,4},{4,0},{8,12},{12,8},{16,20},{20,16},{24,28},{28,24},{1,5},{5... | collective-permute-start | bytes 393224 | tf_op jit(solution)/shard_map/ppermute | solution.py:317
  86.8 0.4 collective-permute-start.6
  87.2 0.0 collective-permute-done.8.refs_1_
  87.2 4.2 %shard_map.48.refs_4_ = f32[128,4096]{1,0:T(8,128)S(1)} custom-call(s32[1]{0:T(128)} %bitcast.place, bf16[128,512]{1,0:T(8,128)(2,1)S(1)} %get-tuple-element.23.refs_0_, bf16[128,512]{1,0:T(8,128)(2,1)S(1)} %collective-permute-done.8.refs_1_, bf16[1024,4096]{1,0:T(8,128)(2,1)S(1)} %copy-done, bf16[1024,4096]{1,0:T(8,128)(2,1)} %collective-permute-done.7.refs_3_), custom_call_target="tpu_custom_call" | custom-call | flops 1073741824 | bytes 8388608 | tf_op jit(solution)/shard_map/pallas_call | solution.py:209
  91.4 0.2 collective-permute-done.5.refs_0_
  91.6 2.0 %collective-permute-done.6.refs_1_ = bf16[128,512]{1,0:T(8,128)(2,1)S(1)} collective-permute-done((bf16[128,512]{1,0:T(8,128)(2,1)S(1)}, bf16[128,512]{1,0:T(8,128)(2,1)S(1)}, u32[]{:S(2)}, u32[]{:S(2)}) %collective-permute-start.6) | collective-permute-done | bytes 131104 | tf_op jit(solution)/shard_map/ppermute | solution.py:318
  93.7 4.3 %shard_map.49 = f32[128,4096]{1,0:T(8,128)S(1)} custom-call(s32[1]{0:T(128)S(6)} %sub.15.place, bf16[128,512]{1,0:T(8,128)(2,1)S(1)} %collective-permute-done.5.refs_0_, bf16[128,512]{1,0:T(8,128)(2,1)S(1)} %collective-permute-done.6.refs_1_, bf16[1024,4096]{1,0:T(8,128)(2,1)S(1)} %copy-done, bf16[1024,4096]{1,0:T(8,128)(2,1)} %collective-permute-done.7.refs_3_, ...), custom_call_target="tpu_custom_call" | custom-call | flops 1073741824 | bytes 8388608 | tf_op jit(solution)/shard_map/pallas_call | solution.py:209
  98.0 11.2 %collective-permute-done.12 = bf16[128,4096]{1,0:T(8,128)(2,1)S(1)} collective-permute-done((bf16[128,4096]{1,0:T(8,128)(2,1)S(1)}, bf16[128,4096]{1,0:T(8,128)(2,1)S(1)}, u32[]{:S(2)}, u32[]{:S(2)}) %collective-permute-start.12) | collective-permute-done | bytes 1048608 | tf_op jit(solution)/shard_map/ppermute | solution.py:323
  109.1 1.2 %add_convert_fusion = bf16[128,4096]{1,0:T(8,128)(2,1)} fusion(f32[128,4096]{1,0:T(8,128)S(1)} %shard_map.49, bf16[128,4096]{1,0:T(8,128)(2,1)S(1)} %collective-permute-done.12), kind=kLoop, calls=%fused_computation | loop fusion | flops 1572864 | bytes 4194304 | tf_op jit(solution)/shard_map/convert_element_type | solution.py:325
Async XLA Ops:
  0.0 73.1 %collective-permute-start.7 = (bf16[1024,4096]{1,0:T(8,128)(2,1)}, bf16[1024,4096]{1,0:T(8,128)(2,1)}, u32[]{:S(2)}, u32[]{:S(2)}) collective-permute-start(bf16[1024,4096]{1,0:T(8,128)(2,1)} %refs_2_.7), channel_id=1, source_target_pairs={{0,1},{1,0},{2,3},{3,2},{4,5},{5,4},{6,7},{7,6},{8,9},{9,8},{10,11... | collective-permute-start | bytes 25165832 | tf_op jit(solution)/shard_map/ppermute | solution.py:256
  0.0 5.6 %copy-start.2 = (bf16[512,1024]{1,0:T(8,128)(2,1)S(1)}, bf16[512,1024]{1,0:T(8,128)(2,1)}, u32[]{:S(2)}) copy-start(bf16[512,1024]{1,0:T(8,128)(2,1)} %param.4) | copy-start | bytes 3145732
  2.8 28.5 %copy-start.3 = (s32[4096]{0:T(1024)S(1)}, s32[4096]{0:T(1024)}, u32[]{:S(2)}) copy-start(s32[4096]{0:T(1024)} %param.7) | copy-start | bytes 49156
  2.8 25.7 %collective-permute-start = (bf16[2,512,512]{2,1,0:T(8,128)(2,1)S(1)}, bf16[2,512,512]{2,1,0:T(8,128)(2,1)}, u32[]{:S(2)}, u32[]{:S(2)}) collective-permute-start(bf16[2,512,512]{2,1,0:T(8,128)(2,1)S(1)} %get-tuple-element.30), channel_id=1, source_target_pairs={{0,4},{4,0},{8,12},{12,8},{16,20},{20,16},{24,28},{28,24},{1,5},{5... | collective-permute-start | bytes 3145736 | tf_op jit(solution)/shard_map/ppermute | solution.py:254
  4.3 49.3 %collective-permute-start.2 = (bf16[2,512,512]{2,1,0:T(8,128)(2,1)}, bf16[2,512,512]{2,1,0:T(8,128)(2,1)S(1)}, u32[]{:S(2)}, u32[]{:S(2)}) collective-permute-start(bf16[2,512,512]{2,1,0:T(8,128)(2,1)} %get-tuple-element.29.kv_own), channel_id=1, source_target_pairs={{0,8},{4,12},{8,16},{12,20},{16,24},{20,28},{1,9},{5,13},{9,17},{1... | collective-permute-start | bytes 3145736 | tf_op jit(solution)/shard_map/ppermute | solution.py:255
  28.5 38.0 %collective-permute-start.3 = (bf16[2,512,512]{2,1,0:T(8,128)(2,1)}, bf16[2,512,512]{2,1,0:T(8,128)(2,1)S(1)}, u32[]{:S(2)}, u32[]{:S(2)}) collective-permute-start(bf16[2,512,512]{2,1,0:T(8,128)(2,1)} %collective-permute-done.kv_other), channel_id=1, source_target_pairs={{0,8},{4,12},{8,16},{12,20},{16,24},{20,28},{1,9},{5,13},{9,17},{1... | collective-permute-start | bytes 3145736 | tf_op jit(solution)/shard_map/ppermute | solution.py:259
  29.8 13.9 %collective-permute-start.1 = (bf16[512,512]{1,0:T(8,128)(2,1)}, bf16[512,512]{1,0:T(8,128)(2,1)}, u32[]{:S(2)}, u32[]{:S(2)}) collective-permute-start(bf16[512,512]{1,0:T(8,128)(2,1)} %get-tuple-element.17), channel_id=1, source_target_pairs={{0,4},{4,0},{8,12},{12,8},{16,20},{20,16},{24,28},{28,24},{1,5},{5... | collective-permute-start | bytes 1572872 | tf_op jit(solution)/shard_map/ppermute | solution.py:258
  33.2 33.3 %collective-permute-start.4 = (bf16[2,128,512]{2,1,0:T(8,128)(2,1)}, bf16[2,128,512]{2,1,0:T(8,128)(2,1)S(1)}, u32[]{:S(2)}, u32[]{:S(2)}) collective-permute-start(bf16[2,128,512]{2,1,0:T(8,128)(2,1)} %dynamic-slice_select_fusion), channel_id=1, source_target_pairs={{0,16},{4,20},{8,24},{12,28},{1,17},{5,21},{9,25},{13,29},{2,18},{... | collective-permute-start | bytes 786440 | tf_op jit(solution)/shard_map/ppermute | solution.py:261
  43.7 1.0 copy-start.1
  44.8 28.3 %copy-start = (bf16[1024,4096]{1,0:T(8,128)(2,1)S(1)}, bf16[1024,4096]{1,0:T(8,128)(2,1)}, u32[]{:S(2)}) copy-start(bf16[1024,4096]{1,0:T(8,128)(2,1)} %refs_2_.7) | copy-start | bytes 25165828
  71.1 1.9 %collective-permute-start.11 = (bf16[128,512]{1,0:T(8,128)(2,1)S(1)}, bf16[128,512]{1,0:T(8,128)(2,1)S(1)}, u32[]{:S(2)}, u32[]{:S(2)}) collective-permute-start(bf16[128,512]{1,0:T(8,128)(2,1)S(1)} %get-tuple-element.28), channel_id=1, source_target_pairs={{0,1},{1,0},{2,3},{3,2},{4,5},{5,4},{6,7},{7,6},{8,9},{9,8},{10,11... | collective-permute-start | bytes 393224 | tf_op jit(solution)/shard_map/ppermute | solution.py:316
  71.2 6.4 %collective-permute-start.9 = (bf16[128,512]{1,0:T(8,128)(2,1)S(1)}, bf16[128,512]{1,0:T(8,128)(2,1)S(1)}, u32[]{:S(2)}, u32[]{:S(2)}) collective-permute-start(bf16[128,512]{1,0:T(8,128)(2,1)S(1)} %get-tuple-element.25), channel_id=1, source_target_pairs={{0,4},{4,0},{8,12},{12,8},{16,20},{20,16},{24,28},{28,24},{1,5},{5... | collective-permute-start | bytes 393224 | tf_op jit(solution)/shard_map/ppermute | solution.py:317
  72.8 6.7 %collective-permute-start.10 = (bf16[128,512]{1,0:T(8,128)(2,1)S(1)}, bf16[128,512]{1,0:T(8,128)(2,1)S(1)}, u32[]{:S(2)}, u32[]{:S(2)}) collective-permute-start(bf16[128,512]{1,0:T(8,128)(2,1)S(1)} %get-tuple-element.26), channel_id=1, source_target_pairs={{0,5},{1,4},{2,7},{3,6},{4,1},{5,0},{6,3},{7,2},{8,13},{9,12},{10,... | collective-permute-start | bytes 393224 | tf_op jit(solution)/shard_map/ppermute | solution.py:318
  83.7 25.4 %collective-permute-start.12 = (bf16[128,4096]{1,0:T(8,128)(2,1)S(1)}, bf16[128,4096]{1,0:T(8,128)(2,1)S(1)}, u32[]{:S(2)}, u32[]{:S(2)}) collective-permute-start(bf16[128,4096]{1,0:T(8,128)(2,1)S(1)} %shard_map.51), channel_id=1, source_target_pairs={{0,2},{1,3},{2,0},{3,1},{4,6},{5,7},{6,4},{7,5},{8,10},{9,11},{10,... | collective-permute-start | bytes 3145736 | tf_op jit(solution)/shard_map/ppermute | solution.py:323
  85.3 1.9 %collective-permute-start.8 = (bf16[128,512]{1,0:T(8,128)(2,1)S(1)}, bf16[128,512]{1,0:T(8,128)(2,1)S(1)}, u32[]{:S(2)}, u32[]{:S(2)}) collective-permute-start(bf16[128,512]{1,0:T(8,128)(2,1)S(1)} %get-tuple-element.24), channel_id=1, source_target_pairs={{0,1},{1,0},{2,3},{3,2},{4,5},{5,4},{6,7},{7,6},{8,9},{9,8},{10,11... | collective-permute-start | bytes 393224 | tf_op jit(solution)/shard_map/ppermute | solution.py:316
  85.3 6.3 %collective-permute-start.5 = (bf16[128,512]{1,0:T(8,128)(2,1)S(1)}, bf16[128,512]{1,0:T(8,128)(2,1)S(1)}, u32[]{:S(2)}, u32[]{:S(2)}) collective-permute-start(bf16[128,512]{1,0:T(8,128)(2,1)S(1)} %get-tuple-element.21), channel_id=1, source_target_pairs={{0,4},{4,0},{8,12},{12,8},{16,20},{20,16},{24,28},{28,24},{1,5},{5... | collective-permute-start | bytes 393224 | tf_op jit(solution)/shard_map/ppermute | solution.py:317
  86.8 6.8 %collective-permute-start.6 = (bf16[128,512]{1,0:T(8,128)(2,1)S(1)}, bf16[128,512]{1,0:T(8,128)(2,1)S(1)}, u32[]{:S(2)}, u32[]{:S(2)}) collective-permute-start(bf16[128,512]{1,0:T(8,128)(2,1)S(1)} %get-tuple-element.22), channel_id=1, source_target_pairs={{0,5},{1,4},{2,7},{3,6},{4,1},{5,0},{6,3},{7,2},{8,13},{9,12},{10,... | collective-permute-start | bytes 393224 | tf_op jit(solution)/shard_map/ppermute | solution.py:318

commit v3 on v0

v3 whole, which is shorter than its diff:
```python
import functools
import math

import jax
import jax.numpy as jnp
from jax import lax
from jax.experimental import pallas as pl
from jax.experimental.pallas import tpu as pltpu
from jax.sharding import PartitionSpec as P

HD = 128
COST = 1000
HOLD = 0.5
TILE = 256
FAR_ROWS = 128
NEG = -1e30
VMEM_BYTES = 16 << 20
SCALE = HD ** (-0.5) * math.log2(math.e)
F32, BF16 = jnp.float32, jnp.bfloat16
IN_HBM = pl.BlockSpec(memory_space=pltpu.HBM)
IN_VMEM = pl.BlockSpec(memory_space=pltpu.VMEM)
IN_SMEM = pl.BlockSpec(memory_space=pltpu.SMEM)
ANYWHERE = pl.BlockSpec(memory_space=pl.ANY)


def tile_bias(key_docs, query_docs, causal_from=None):
    column = jnp.broadcast_to(key_docs, (8, key_docs.shape[1])).T[:, :1]
    allowed = column == query_docs
    if causal_from is not None:
        keys = lax.broadcasted_iota(jnp.int32, allowed.shape, 0)
        queries = lax.broadcasted_iota(jnp.int32, allowed.shape, 1) + causal_from
        allowed = allowed & (keys <= queries)
    return jnp.where(allowed, jnp.float32(0), jnp.float32(NEG))


def scores_of(key, query, bias):
    raw = lax.dot_general(key, query, (((1,), (1,)), ((), ())), preferred_element_type=F32)
    return raw * SCALE + bias


def head_cols(head):
    return pl.ds(head * HD, HD)


def multiple(value, of):
    return pl.multiple_of(value, of)


def fresh_tiles(heads, jobs, summed, stats):
    entries = [scores_of(k, q, bias) for k, q, v, bias, span in jobs]
    tops = [jnp.max(e, axis=0, keepdims=True) for e in entries]
    weights = [jnp.exp2(e - t) for e, t in zip(entries, tops)]
    totals = [jnp.sum(w, axis=0, keepdims=True) for w in weights]
    sums = [
        jnp.dot(job[2], w.astype(BF16), preferred_element_type=F32) for job, w in zip(jobs, weights)
    ]
    for first in range(0, len(jobs), heads):
        span, these = jobs[first][4], slice(first, first + heads)
        stats[:, span] = jnp.concatenate(tops[these] + totals[these], axis=0)
        for h in range(heads):
            summed[head_cols(h), span] = sums[first + h]


def fold_tiles(heads, keys, queries, values, bias, span, summed, stats):
    before = stats[:, span]
    olds = [summed[head_cols(h), span] for h in range(heads)]
    entries = [scores_of(k, q, bias) for k, q in zip(keys, queries)]
    tops = [
        jnp.maximum(before[h : h + 1], jnp.max(e, axis=0, keepdims=True))
        for h, e in enumerate(entries)
    ]
    shrinks = [jnp.exp2(before[h : h + 1] - t) for h, t in enumerate(tops)]
    weights = [jnp.exp2(e - t) for e, t in zip(entries, tops)]
    totals = [
        before[heads + h : heads + h + 1] * shrinks[h] + jnp.sum(w, axis=0, keepdims=True)
        for h, w in enumerate(weights)
    ]
    sums = [
        o * s + jnp.dot(v, w.astype(BF16), preferred_element_type=F32)
        for o, s, v, w in zip(olds, shrinks, values, weights)
    ]
    stats[:, span] = jnp.concatenate(tops + totals, axis=0)
    for h in range(heads):
        summed[head_cols(h), span] = sums[h]


def transposed(heads, values, target, at):
    for head in range(heads):
        target[head_cols(head), at] = values[:, head_cols(head)].T


def started(copies):
    for copy in copies:
        copy.start()
    return copies


def waited(copies):
    for copy in copies:
        copy.wait()


def fold_keys(heads, ks, qs, vts, docs_row, query_docs, count, nearest, shift, span, summed, stats):
    def one(at, size):
        there = pl.ds(multiple(at, TILE), size)
        bias = tile_bias(docs_row[:, pl.ds(multiple(shift + at, TILE), size)], query_docs)
        fold_tiles(
            heads,
            [ks[there, head_cols(h)] for h in range(heads)],
            [qs[:, head_cols(h)] for h in range(heads)],
            [vts[head_cols(h), there] for h in range(heads)],
            bias, span, summed, stats,
        )

    def two_back(step, _):
        one(nearest - (step + 1) * 2 * TILE, 2 * TILE)
        return 0

    lax.fori_loop(0, count // 2, two_back, 0)

    @pl.when(lax.rem(count, 2) == 1)
    def _():
        one(nearest - count * TILE, TILE)


def pair_kernel(heads, shard, pad, ids, docs, docs_row, q_own, kv_own, q_other, k_other, v_other,
                summed, stats, qs, ks, vts):
    side = lax.rem(ids[0], 2)
    own = pl.ds(multiple(side * shard, shard), shard)
    other = pl.ds(multiple((1 - side) * shard, shard), shard)
    ks[own, :] = kv_own[0]
    ks[other, :] = k_other[...]
    qs[own, :] = q_own[...]
    qs[other, :] = q_other[...]
    transposed(heads, kv_own.at[1], vts, own)
    transposed(heads, v_other, vts, other)

    for step in range(shard // TILE):
        jobs = []
        for start in (0, shard):
            at = start + step * TILE
            keys, span = pl.ds(start, (step + 1) * TILE), pl.ds(at, TILE)
            bias = tile_bias(
                docs_row[:, pad + start : pad + at + TILE], docs_row[:, pad + at : pad + at + TILE],
                step * TILE,
            )
            jobs += [
                (ks[keys, head_cols(h)], qs[span, head_cols(h)], vts[head_cols(h), keys], bias, span)
                for h in range(heads)
            ]
        fresh_tiles(heads, jobs, summed, stats)

    @pl.when(docs[pad + shard - 1] == docs[pad + shard])
    def _():
        def one_tile(step, _):
            start = multiple(shard + step * TILE, TILE)
            span = pl.ds(start, TILE)
            first_doc = docs[pad + start]
            live = jnp.int32(0)
            for back in range(shard // TILE):
                live += (docs[pad + shard - back * TILE - 1] == first_doc).astype(jnp.int32)
            query_docs = docs_row[:, pl.ds(multiple(pad + start, TILE), TILE)]
            fold_keys(
                heads, ks, qs.at[span], vts, docs_row, query_docs, live, shard, pad, span, summed, stats
            )
            return 0

        lax.fori_loop(0, shard // TILE, one_tile, 0)


def remote_kernel(heads, shard, pad, wave, ids, docs, docs_row, q_own, q_other, summed_in, stats_in, *rest):
    (same, k_cross, v_cross, kv_far), rest = rest[:4], rest[4:]
    sources = ((k_cross, v_cross), (same.at[0], same.at[1]))
    outs, (qs, ks, vts, done, summed, stats, sems) = rest[:4], rest[4:]
    half = heads * HD
    side = lax.rem(ids[0], 2)
    core, y_own = lax.rem(ids[1], 2), ids[1] // 2
    y_part = 1 - y_own if wave == 0 else y_own
    part_at = multiple(y_part * TILE, TILE)
    rows = pl.ds(part_at, TILE)
    copies = [
        pltpu.make_async_copy(a, b, sems.at[i])
        for i, (a, b) in enumerate(
            (
                (q_own.at[rows, :], qs.at[side]),
                (q_other.at[rows, :], qs.at[1 - side]),
                (summed_in.at[:, rows], summed.at[0]),
                (stats_in.at[:, rows], stats.at[0]),
                (summed_in.at[:, pl.ds(multiple(shard + part_at, TILE), TILE)], summed.at[1]),
                (stats_in.at[:, pl.ds(multiple(shard + part_at, TILE), TILE)], stats.at[1]),
            )
        )
    ]
    started(copies)

    def reach(query_at):
        first_doc = docs[pad + query_at]
        live = jnp.int32(0)
        for back in range(pad // TILE):
            live += (docs[pad - back * TILE - 1] == first_doc).astype(jnp.int32)
        return live

    most = reach(part_at)

    def place_keys(keys, values, at, size):
        ks[pl.ds(at, size), :] = keys[...]
        transposed(heads, values, vts, pl.ds(at, size))

    for back in range(pad // TILE):
        at = pad - (back + 1) * TILE

        @pl.when(most > back)
        def _():
            if back == 4:
                blank = TILE - FAR_ROWS
                ks[at : at + blank, :] = jnp.zeros((blank, half), BF16)
                vts[:, at : at + blank] = jnp.zeros((half, blank), BF16)
                place_keys(kv_far.at[0], kv_far.at[1], at + blank, FAR_ROWS)
            else:
                part = pl.ds((1 - back % 2) * TILE, TILE)
                for which, (keys, values) in enumerate(sources if back < 2 else sources[::-1]):

                    @pl.when(side == which)
                    def _():
                        place_keys(keys.at[part], values.at[part], at, TILE)

    waited(copies)
    whole = pl.ds(0, TILE)

    def one_tile(step, _):
        here = multiple(step * shard + part_at, TILE)
        mine = pl.ds(multiple(step * TILE, TILE), TILE)
        query_docs = docs_row[:, pl.ds(multiple(pad + here, TILE), TILE)]

        fold_keys(
            heads, ks, qs.at[step], vts, docs_row, query_docs, reach(here), pad, 0, whole,
            summed.at[step], stats.at[step],
        )
        for head in range(heads):
            part = summed[step, head_cols(head), :] / stats[step, heads + head : heads + head + 1, :]
            done[mine, head_cols(head)] = part.astype(BF16).T
        return 0

    lax.fori_loop(0, 2, one_tile, 0)
    block = outs[0].shape[0]
    for turn, out in enumerate(outs):
        to_side = 1 - side if turn // 2 else side
        to_core = 1 - core if turn % 2 else core
        out[...] = done[pl.ds(multiple((to_side * 2 + to_core) * block, block), block), :]


def project_kernel(count, turns, ring, part, chunk, begun, ids, *refs):
    pieces, (w_near, w_other) = refs[:count], refs[count : count + 2]
    out, held, sems = refs[-3:]
    side = lax.rem(ids[0], 2)
    width = pieces[0].shape[1]
    steps = out.shape[1] // chunk
    first = part * out.shape[1]

    def copies(step):
        made = []
        for number, turn in enumerate(turns):
            source = w_other if turn % 2 else w_near
            to_side = 1 - side if turn // 2 else side
            made.append(
                pltpu.make_async_copy(
                    source.at[
                        pl.ds(multiple(to_side * width, width), width),
                        pl.ds(first + step * chunk, chunk),
                    ],
                    held.at[step % ring, number],
                    sems.at[step % ring, number],
                )
            )
        return made

    for step in range(min(ring, steps)):
        started(copies(step))
    for step in range(steps):
        waited(copies(step))
        here = slice(step * chunk, (step + 1) * chunk)
        term = refs[count + 2][:, first + step * chunk : first + (step + 1) * chunk] if begun else None
        for number in range(count):
            more = jnp.dot(pieces[number][...], held[step % ring, number], preferred_element_type=F32)
            term = more if term is None else term + more
        out[:, here] = term.astype(out.dtype)
        if step + ring < steps:
            started(copies(step + ring))


def add_kernel(staying, *refs):
    arrived, out = refs[:-1], refs[-1]
    width = arrived[0].shape[1]
    for number, part in enumerate(arrived):
        here = slice(number * width, (number + 1) * width)
        out[:, here] = (staying[:, here] + part[...].astype(F32)).astype(out.dtype)


def pass_kernel(ids, *refs):
    refs[-1][0] = ids[0]
    refs[-1][1] = ids[1]


def after(ids, arrays, micros):
    return pl.pallas_call(
        pass_kernel,
        in_specs=[IN_SMEM] + [ANYWHERE] * len(arrays),
        out_specs=IN_SMEM,
        out_shape=jax.ShapeDtypeStruct(ids.shape, ids.dtype),
        compiler_params=pltpu.CompilerParams(vmem_limit_bytes=VMEM_BYTES),
        cost_estimate=pl.CostEstimate(
            flops=int(micros * 1.1e9), bytes_accessed=1024, transcendentals=0
        ),
    )(ids, *arrays)


def call(kernel, outs, scratch, micros, specs, arrays, limit=VMEM_BYTES):
    return pl.pallas_call(
        kernel,
        in_specs=specs,
        out_specs=[IN_VMEM] * len(outs),
        out_shape=[jax.ShapeDtypeStruct(shape, kind) for shape, kind in outs],
        scratch_shapes=scratch,
        compiler_params=pltpu.CompilerParams(vmem_limit_bytes=limit),
        cost_estimate=pl.CostEstimate(
            flops=int(micros * COST), bytes_accessed=1024, transcendentals=0
        ),
    )(*arrays)


def per_device(queries, keys_values, w_out, doc_index):
    shard, width = queries.shape
    n_ctx, n_head = lax.axis_size("ctx"), lax.axis_size("head")
    me, group = lax.axis_index("ctx"), lax.axis_index("head")
    half = width // 2
    heads = half // HD
    rows = 2 * shard
    pad = rows + TILE
    block = shard // n_head

    ids = jnp.stack([me, group]).astype(jnp.int32)
    padded = jnp.concatenate([jnp.full((pad,), -1, jnp.int32), doc_index])
    docs = lax.dynamic_slice_in_dim(padded, (me // 2) * rows, pad + rows)
    docs_row = docs.reshape(1, pad + rows)

    swap = [(c, c ^ 1) for c in range(n_ctx)]
    hop = [(c, c + 2) for c in range(n_ctx - 2)]
    far = [(c, c + 4) for c in range(n_ctx - 4)]
    core = [(h, h ^ 1) for h in range(n_head)]
    both = [
        (c * n_head + h, (c ^ 1) * n_head + (h ^ 1)) for c in range(n_ctx) for h in range(n_head)
    ]
    far_y = [(h, h ^ 2) for h in range(n_head)]
    sems = pltpu.SemaphoreType.DMA
    vmem = pltpu.VMEM

    side = lax.rem(me, 2)

    def mine(array, axis):
        return lax.dynamic_slice_in_dim(array, side * half, half, axis)

    def theirs(array, axis):
        return lax.dynamic_slice_in_dim(array, (1 - side) * half, half, axis)

    kv_own = mine(keys_values, 2)
    queries, keys_values, kv_own = lax.optimization_barrier((queries, keys_values, kv_own))
    same = lax.ppermute(kv_own, "ctx", hop)
    k_other = lax.ppermute(theirs(keys_values[0], 1), "ctx", swap)
    v_other = lax.ppermute(theirs(keys_values[1], 1), "ctx", swap)
    w_other = lax.ppermute(w_out, "head", core)
    q_send, q_own = theirs(queries, 1), mine(queries, 1)
    q_send, k_other, w_other = lax.optimization_barrier((q_send, k_other, w_other))
    q_other = lax.ppermute(q_send, "ctx", swap)
    late_k = lax.ppermute(k_other, "ctx", hop)
    late_v = lax.ppermute(v_other, "ctx", hop)

    last = shard - FAR_ROWS
    tails = [kv_own[:, last:], k_other[last:], v_other[last:]]
    late_v, tails = lax.optimization_barrier((late_v, tails))

    def far_hop(own, k, v):
        return lax.ppermute(jnp.where(side == 1, own, jnp.stack([k, v])), "ctx", far)

    blocks = doc_index.reshape(-1, rows)
    kv_far = lax.cond(
        jnp.any(blocks[:-2, -1] == blocks[2:, 0]),
        far_hop,
        lambda own, k, v: jnp.zeros_like(own),
        *tails,
    )
    arrivals = [same, late_k, late_v, kv_far]
    ids_late = after(ids, [late_k], HOLD)

    summed, stats = call(
        functools.partial(pair_kernel, heads, shard, pad),
        [((half, rows), F32), ((2 * heads, rows), F32)],
        [vmem((rows, half), BF16)] * 2 + [vmem((half, rows), BF16)],
        7,
        [IN_SMEM, IN_SMEM] + [IN_VMEM] * 6,
        [ids, docs, docs_row, q_own, kv_own, q_other, k_other, v_other],
    )

    def finished(wave, stats):
        return call(
            functools.partial(remote_kernel, heads, shard, pad, wave),
            [((block, half), BF16)] * 4,
            [
                vmem((2, TILE, half), BF16),
                vmem((pad, half), BF16),
                vmem((half, pad), BF16),
                vmem((2 * TILE, half), BF16),
                vmem((2, half, TILE), F32),
                vmem((2, 2 * heads, TILE), F32),
                sems((6,)),
            ],
            5e6 if wave == 0 else 1,
            [IN_SMEM, IN_SMEM, IN_VMEM] + [IN_HBM] * 4 + [IN_VMEM] * len(arrivals),
            [ids_late, docs, docs_row, q_own, q_other, summed, stats, *arrivals],
        )

    def exchanged(pieces):
        return [
            pieces[0],
            lax.ppermute(pieces[1], "head", core),
            lax.ppermute(pieces[2], "ctx", swap),
            lax.ppermute(pieces[3], ("ctx", "head"), both),
        ]

    def project(pieces, turns, begun, kind, part, parts):
        columns = w_out.shape[1] // parts
        chunk, ring = 512, 16 // len(pieces)
        more = [] if begun is None else [begun]
        (out,) = call(
            functools.partial(
                project_kernel, len(pieces), turns, ring, part, chunk, begun is not None
            ),
            [((block, columns), kind)],
            [vmem((ring, len(pieces), half, chunk), BF16), sems((ring, len(pieces)))],
            2 * len(pieces) // parts,
            [IN_SMEM] + [IN_VMEM] * len(pieces) + [IN_HBM] * 2 + [IN_VMEM] * len(more),
            [ids, *pieces, w_out, w_other, *more],
        )
        return out

    parts = 2
    pieces = exchanged(finished(0, stats))
    begun = project(pieces[:2], (0, 1), None, F32, 0, 1)
    leaving = [project(pieces[2:], (2, 3), begun, BF16, part, parts) for part in range(parts)]
    arrived = [lax.ppermute(part, "head", far_y) for part in leaving]
    stats, leaving = lax.optimization_barrier((stats, leaving))
    pieces = exchanged(finished(1, stats))
    staying = project(pieces, (0, 1, 2, 3), None, F32, 0, 1)
    (out,) = call(
        add_kernel,
        [((block, w_out.shape[1]), BF16)],
        [],
        1,
        [IN_VMEM] * (1 + parts),
        [staying, *arrived],
    )
    return out


def solution(mesh):
    in_specs = (P("ctx", "head"), P(None, "ctx", "head"), P("head", None), P())
    out_specs = P(("ctx", "head"), None)
    return jax.shard_map(
        per_device, mesh=mesh, in_specs=in_specs, out_specs=out_specs, check_vma=False
    )
```

time: 273 us -> 98.3 us (0.36)
  the two profiles are of different devices: /device:TPU:24 before, /device:TPU:19 now
where the time goes in v3:
time: 98.3 us; the launch traced here: 99.1 us
  waiting for transfers between devices  35.2 us (36%)
  Pallas kernels  34.3 us (35%)
  starting transfers between devices  21.4 us (22%)
  local copies, waits for them, and re-layouts  6.44 us (7%)
    pallas_call x8, Pallas kernels, call(): pl.pallas_call(kernel, in_specs=specs, out_specs=[IN_VMEM] * len(outs), o...  33.1 us
    ppermute x1, waiting for transfers between devices, per_device(): v_other = lax.ppermute(theirs(keys_values[1], 1), 'ctx', swap)  8.22 us
    ppermute x1, waiting for transfers between devices, per_device(): k_other = lax.ppermute(theirs(keys_values[0], 1), 'ctx', swap)  7.12 us
    ppermute x1, waiting for transfers between devices, per_device(): late_v = lax.ppermute(v_other, 'ctx', hop)  5.87 us
    ppermute x1, waiting for transfers between devices, per_device(): late_k = lax.ppermute(k_other, 'ctx', hop)  5.39 us
    ppermute x2, waiting for transfers between devices, exchanged(): lax.ppermute(pieces[3], ('ctx', 'head'), both)  5.26 us
    ppermute x2, waiting for transfers between devices, exchanged(): lax.ppermute(pieces[2], 'ctx', swap)  3.37 us
    ppermute x1, starting transfers between devices, per_device(): late_v = lax.ppermute(v_other, 'ctx', hop)  3.19 us
  transfers between devices with their start and end apart: 15, of which 7 were waited for; matrix products, arithmetic and copies ran while one was open for 7% of the time, Pallas kernels for 26%

profile of v3, /device:TPU:19, one launch (start us, length us, event | category | flops | bytes accessed | tf_op | source)
XLA Modules:
  0.0 99.1 jit_solution(1636610333141741762)
XLA Ops:
  0.0 0.0 copy-start
  0.0 0.7 collective-permute-start.2
  0.7 1.3 %constant_dynamic-slice_fusion.2.kv_own = bf16[2,512,512]{2,1,0:T(8,128)(2,1)S(1)} fusion(bf16[2,512,1024]{2,1,0:T(8,128)(2,1)} %param.7, s32[]{:T(128)S(6)} %select_n.25), kind=kLoop, calls=%fused_computation.7 | loop fusion | bytes 2097156 | tf_op jit(solution)/shard_map/dynamic_slice | solution.py:360
  2.0 0.0 copy-done
  2.0 0.2 fusion
  2.2 0.0 copy-start.1
  2.2 0.0 copy-start.2
  2.2 0.3 collective-permute-start.5
  2.6 1.3 %collective-permute-start.1 = (bf16[512,512]{1,0:T(8,128)(2,1)S(1)}, bf16[512,512]{1,0:T(8,128)(2,1)}, u32[]{:S(2)}, u32[]{:S(2)}) collective-permute-start(bf16[512,512]{1,0:T(8,128)(2,1)S(1)} %dynamic-slice_bitcast_fusion.1), channel_id=1, source_target_pairs={{0,4},{4,0},{8,12},{12,8},{16,20},{20,16},{24,28},{28,24},{1,5},{5... | collective-permute-start | bytes 1572872 | tf_op jit(solution)/shard_map/ppermute | solution.py:368
  3.9 3.2 %collective-permute-start.6 = (bf16[2,512,512]{2,1,0:T(8,128)(2,1)S(1)}, bf16[2,512,512]{2,1,0:T(8,128)(2,1)S(1)}, u32[]{:S(2)}, u32[]{:S(2)}) collective-permute-start(bf16[2,512,512]{2,1,0:T(8,128)(2,1)S(1)} %constant_dynamic-slice_fusion.2.kv_own), channel_id=1, source_target_pairs={{0,8},{4,12},{8,16},{12,20},{16,24},{20,28},{1,9},{5,13},{9,17},{1... | collective-permute-start | bytes 3145736 | tf_op jit(solution)/shard_map/ppermute | solution.py:367
  7.1 8.2 %collective-permute-done.5.v_other = bf16[512,512]{1,0:T(8,128)(2,1)} collective-permute-done((bf16[512,512]{1,0:T(8,128)(2,1)S(1)}, bf16[512,512]{1,0:T(8,128)(2,1)}, u32[]{:S(2)}, u32[]{:S(2)}) %collective-permute-start.5) | collective-permute-done | bytes 524320 | tf_op jit(solution)/shard_map/ppermute | solution.py:369
  15.3 3.2 %collective-permute-start.7 = (bf16[512,512]{1,0:T(8,128)(2,1)}, bf16[512,512]{1,0:T(8,128)(2,1)}, u32[]{:S(2)}, u32[]{:S(2)}) collective-permute-start(bf16[512,512]{1,0:T(8,128)(2,1)} %collective-permute-done.5.v_other), channel_id=1, source_target_pairs={{0,8},{4,12},{8,16},{12,20},{16,24},{20,28},{1,9},{5,13},{9,17},{1... | collective-permute-start | bytes 1572872 | tf_op jit(solution)/shard_map/ppermute | solution.py:375
  18.5 0.0 copy-done.1
  18.5 0.9 constant_dynamic-slice_fusion
  19.4 7.1 %collective-permute-done.1.k_other = bf16[512,512]{1,0:T(8,128)(2,1)} collective-permute-done((bf16[512,512]{1,0:T(8,128)(2,1)S(1)}, bf16[512,512]{1,0:T(8,128)(2,1)}, u32[]{:S(2)}, u32[]{:S(2)}) %collective-permute-start.1) | collective-permute-done | bytes 524320 | tf_op jit(solution)/shard_map/ppermute | solution.py:368
  26.5 0.0 collective-permute-done.2.refs_3_.refs_5_
  26.5 0.3 collective-permute-start.4
  26.8 3.2 %collective-permute-start.3 = (bf16[512,512]{1,0:T(8,128)(2,1)}, bf16[512,512]{1,0:T(8,128)(2,1)}, u32[]{:S(2)}, u32[]{:S(2)}) collective-permute-start(bf16[512,512]{1,0:T(8,128)(2,1)} %collective-permute-done.1.k_other), channel_id=1, source_target_pairs={{0,8},{4,12},{8,16},{12,20},{16,24},{20,28},{1,9},{5,13},{9,17},{1... | collective-permute-start | bytes 1572872 | tf_op jit(solution)/shard_map/ppermute | solution.py:374
  30.0 0.0 copy-done.2
  30.1 0.1 pad_dynamic-slice_fusion.docs
  30.2 0.7 compare_reduce_fusion
  31.5 0.1 pad_add_fusion.ids
  31.6 1.6 %slice.28 = bf16[128,512]{1,0:T(8,128)(2,1)} slice(bf16[512,512]{1,0:T(8,128)(2,1)} %collective-permute-done.5.v_other), slice={[384:512], [0:512]} | slice | bytes 262144 | tf_op jit(solution)/shard_map/slice | solution.py:378
  33.2 1.5 %slice.24 = bf16[128,512]{1,0:T(8,128)(2,1)} slice(bf16[512,512]{1,0:T(8,128)(2,1)} %collective-permute-done.1.k_other), slice={[384:512], [0:512]} | slice | bytes 262144 | tf_op jit(solution)/shard_map/slice | solution.py:378
  34.7 5.9 %collective-permute-done.7.rest_2_ = bf16[512,512]{1,0:T(8,128)(2,1)} collective-permute-done((bf16[512,512]{1,0:T(8,128)(2,1)}, bf16[512,512]{1,0:T(8,128)(2,1)}, u32[]{:S(2)}, u32[]{:S(2)}) %collective-permute-start.7) | collective-permute-done | bytes 524320 | tf_op jit(solution)/shard_map/ppermute | solution.py:375
  40.6 0.7 conditional.1
  40.6 0.7 broadcast.3
  41.3 0.0 collective-permute-done.4.q_other
  41.3 5.1 %shard_map.47 = (f32[512,1024]{1,0:T(8,128)S(1)}, f32[8,1024]{1,0:T(8,128)S(1)}) custom-call(s32[2]{0:T(128)S(1)} %pad_add_fusion.ids, s32[2304]{0:T(1024)S(1)} %pad_dynamic-slice_fusion.docs, s32[1,2304]{1,0:T(1,128)S(1)} %reshape.9.docs_row, bf16[512,512]{1,0:T(8,128)(2,1)S(1)} %get-tuple-element.64.q_own, ...), custom_call_target="tpu_custom_call" | custom-call | flops 7000 | bytes 1024 | tf_op jit(solution)/shard_map/pallas_call | solution.py:318
  46.4 5.4 %collective-permute-done.3.refs_0_.rest_1_ = bf16[512,512]{1,0:T(8,128)(2,1)} collective-permute-done((bf16[512,512]{1,0:T(8,128)(2,1)}, bf16[512,512]{1,0:T(8,128)(2,1)}, u32[]{:S(2)}, u32[]{:S(2)}) %collective-permute-start.3) | collective-permute-done | bytes 524320 | tf_op jit(solution)/shard_map/ppermute | solution.py:374
  51.8 1.1 %shard_map.46.ids = s32[2]{0:T(128)S(1)} custom-call(s32[2]{0:T(128)S(1)} %pad_add_fusion.ids, bf16[512,512]{1,0:T(8,128)(2,1)} %collective-permute-done.3.refs_0_.rest_1_), custom_call_target="tpu_custom_call" | custom-call | flops 550000000 | bytes 1024 | tf_op jit(solution)/shard_map/pallas_call | solution.py:305
  53.0 0.0 collective-permute-done.6.rest_0_
  53.0 0.0 slice-start
  53.0 0.0 slice-start.1
  53.0 4.4 %shard_map.48 = (bf16[128,512]{1,0:T(8,128)(2,1)S(1)}, bf16[128,512]{1,0:T(8,128)(2,1)S(1)}, bf16[128,512]{1,0:T(8,128)(2,1)S(1)}, bf16[128,512]{1,0:T(8,128)(2,1)S(1)}) custom-call(s32[2]{0:T(128)S(1)} %shard_map.46.ids, s32[2304]{0:T(1024)S(1)} %pad_dynamic-slice_fusion.docs, s32[1,2304]{1,0:T(1,128)S(1)} %reshape.9.docs_row, ...), custom_call_target="tpu_custom_call" | custom-call | flops 5000000000 | bytes 1024 | tf_op jit(solution)/shard_map/pallas_call | solution.py:318
  57.4 2.1 %collective-permute-start.10 = (bf16[128,512]{1,0:T(8,128)(2,1)S(1)}, bf16[128,512]{1,0:T(8,128)(2,1)S(1)}, u32[]{:S(2)}, u32[]{:S(2)}) collective-permute-start(bf16[128,512]{1,0:T(8,128)(2,1)S(1)} %get-tuple-element.56), channel_id=1, source_target_pairs={{0,1},{1,0},{2,3},{3,2},{4,5},{5,4},{6,7},{7,6},{8,9},{9,8},{10,11... | collective-permute-start | bytes 393224 | tf_op jit(solution)/shard_map/ppermute | solution.py:424
  59.5 0.3 collective-permute-start.8
  59.8 1.4 %collective-permute-start.9 = (bf16[128,512]{1,0:T(8,128)(2,1)S(1)}, bf16[128,512]{1,0:T(8,128)(2,1)S(1)}, u32[]{:S(2)}, u32[]{:S(2)}) collective-permute-start(bf16[128,512]{1,0:T(8,128)(2,1)S(1)} %get-tuple-element.53), channel_id=1, source_target_pairs={{0,5},{1,4},{2,7},{3,6},{4,1},{5,0},{6,3},{7,2},{8,13},{9,12},{10,... | collective-permute-start | bytes 393224 | tf_op jit(solution)/shard_map/ppermute | solution.py:426
  61.2 0.0 collective-permute-done.10.refs_1_
  61.2 0.0 slice-done
  61.3 0.0 slice-done.1
  61.3 4.3 %shard_map.49.refs_4_ = f32[128,4096]{1,0:T(8,128)S(1)} custom-call(s32[2]{0:T(128)S(1)} %pad_add_fusion.ids, bf16[128,512]{1,0:T(8,128)(2,1)S(1)} %get-tuple-element.55.refs_0_, bf16[128,512]{1,0:T(8,128)(2,1)S(1)} %collective-permute-done.10.refs_1_, bf16[1024,4096]{1,0:T(8,128)(2,1)S(1)} %bitcast.9, bf16[1024,4096]{1,0:T(8,128)(2,1)} %collective-permute-done.2.refs_3_.refs_5_), custom_call_target="tpu_custom_call" | custom-call | flops 4000 | bytes 1024 | tf_op jit(solution)/shard_map/pallas_call | solution.py:318
  65.6 0.0 collective-permute-done.8.refs_0_
  65.6 2.0 %collective-permute-done.9.refs_1_ = bf16[128,512]{1,0:T(8,128)(2,1)S(1)} collective-permute-done((bf16[128,512]{1,0:T(8,128)(2,1)S(1)}, bf16[128,512]{1,0:T(8,128)(2,1)S(1)}, u32[]{:S(2)}, u32[]{:S(2)}) %collective-permute-start.9) | collective-permute-done | bytes 131104 | tf_op jit(solution)/shard_map/ppermute | solution.py:426
  67.6 3.1 %shard_map.50 = bf16[128,2048]{1,0:T(8,128)(2,1)S(1)} custom-call(s32[2]{0:T(128)S(1)} %pad_add_fusion.ids, bf16[128,512]{1,0:T(8,128)(2,1)S(1)} %collective-permute-done.8.refs_0_, bf16[128,512]{1,0:T(8,128)(2,1)S(1)} %collective-permute-done.9.refs_1_, bf16[1024,4096]{1,0:T(8,128)(2,1)S(1)} %bitcast.9, ...), custom_call_target="tpu_custom_call" | custom-call | flops 2000 | bytes 1024 | tf_op jit(solution)/shard_map/pallas_call | solution.py:318
  70.7 3.0 %collective-permute-start.14 = (bf16[128,2048]{1,0:T(8,128)(2,1)S(1)}, bf16[128,2048]{1,0:T(8,128)(2,1)S(1)}, u32[]{:S(2)}, u32[]{:S(2)}) collective-permute-start(bf16[128,2048]{1,0:T(8,128)(2,1)S(1)} %shard_map.50), channel_id=1, source_target_pairs={{0,2},{1,3},{2,0},{3,1},{4,6},{5,7},{6,4},{7,5},{8,10},{9,11},{10,... | collective-permute-start | bytes 1572872 | tf_op jit(solution)/shard_map/ppermute | solution.py:449
  73.7 3.1 %shard_map.51 = bf16[128,2048]{1,0:T(8,128)(2,1)S(1)} custom-call(s32[2]{0:T(128)S(1)} %pad_add_fusion.ids, bf16[128,512]{1,0:T(8,128)(2,1)S(1)} %collective-permute-done.8.refs_0_, bf16[128,512]{1,0:T(8,128)(2,1)S(1)} %collective-permute-done.9.refs_1_, bf16[1024,4096]{1,0:T(8,128)(2,1)S(1)} %bitcast.9, ...), custom_call_target="tpu_custom_call" | custom-call | flops 2000 | bytes 1024 | tf_op jit(solution)/shard_map/pallas_call | solution.py:318
  76.8 0.1 collective-permute-start.15
  76.9 5.8 %shard_map.52 = (bf16[128,512]{1,0:T(8,128)(2,1)S(1)}, bf16[128,512]{1,0:T(8,128)(2,1)S(1)}, bf16[128,512]{1,0:T(8,128)(2,1)S(1)}, bf16[128,512]{1,0:T(8,128)(2,1)S(1)}) custom-call(s32[2]{0:T(128)S(1)} %shard_map.46.ids, s32[2304]{0:T(1024)S(1)} %pad_dynamic-slice_fusion.docs, s32[1,2304]{1,0:T(1,128)S(1)} %reshape.9.docs_row, ...), custom_call_target="tpu_custom_call" | custom-call | flops 1000 | bytes 1024 | tf_op jit(solution)/shard_map/pallas_call | solution.py:318
  82.7 0.6 collective-permute-start.11
  83.3 0.3 collective-permute-start.12
  83.5 1.4 %collective-permute-start.13 = (bf16[128,512]{1,0:T(8,128)(2,1)S(1)}, bf16[128,512]{1,0:T(8,128)(2,1)S(1)}, u32[]{:S(2)}, u32[]{:S(2)}) collective-permute-start(bf16[128,512]{1,0:T(8,128)(2,1)S(1)} %get-tuple-element.61), channel_id=1, source_target_pairs={{0,5},{1,4},{2,7},{3,6},{4,1},{5,0},{6,3},{7,2},{8,13},{9,12},{10,... | collective-permute-start | bytes 393224 | tf_op jit(solution)/shard_map/ppermute | solution.py:426
  85.0 0.0 collective-permute-done.11.refs_1_
  85.0 3.4 %collective-permute-done.12.refs_2_ = bf16[128,512]{1,0:T(8,128)(2,1)S(1)} collective-permute-done((bf16[128,512]{1,0:T(8,128)(2,1)S(1)}, bf16[128,512]{1,0:T(8,128)(2,1)S(1)}, u32[]{:S(2)}, u32[]{:S(2)}) %collective-permute-start.12) | collective-permute-done | bytes 131104 | tf_op jit(solution)/shard_map/ppermute | solution.py:425
  88.3 3.3 %collective-permute-done.13.refs_3_ = bf16[128,512]{1,0:T(8,128)(2,1)S(1)} collective-permute-done((bf16[128,512]{1,0:T(8,128)(2,1)S(1)}, bf16[128,512]{1,0:T(8,128)(2,1)S(1)}, u32[]{:S(2)}, u32[]{:S(2)}) %collective-permute-start.13) | collective-permute-done | bytes 131104 | tf_op jit(solution)/shard_map/ppermute | solution.py:426
  91.6 6.2 %shard_map.53.staying = f32[128,4096]{1,0:T(8,128)S(1)} custom-call(s32[2]{0:T(128)S(1)} %pad_add_fusion.ids, bf16[128,512]{1,0:T(8,128)(2,1)S(1)} %get-tuple-element.58.refs_0_, bf16[128,512]{1,0:T(8,128)(2,1)S(1)} %collective-permute-done.11.refs_1_, bf16[128,512]{1,0:T(8,128)(2,1)S(1)} %collective-permute-done.12.refs_2_, ...), custom_call_target="tpu_custom_call" | custom-call | flops 8000 | bytes 1024 | tf_op jit(solution)/shard_map/pallas_call | solution.py:318
  97.8 0.0 collective-permute-done.14.refs_0_
  97.8 0.0 collective-permute-done.15.refs_1_
  97.9 1.2 %shard_map.54 = bf16[128,4096]{1,0:T(8,128)(2,1)} custom-call(f32[128,4096]{1,0:T(8,128)S(1)} %shard_map.53.staying, bf16[128,2048]{1,0:T(8,128)(2,1)S(1)} %collective-permute-done.14.refs_0_, bf16[128,2048]{1,0:T(8,128)(2,1)S(1)} %collective-permute-done.15.refs_1_), custom_call_target="tpu_custom_call" | custom-call | flops 1000 | bytes 1024 | tf_op jit(solution)/shard_map/pallas_call | solution.py:318
  (6 shorter events, 0.1 us)
Async XLA Ops:
  0.0 2.0 %copy-start = (bf16[2,512,1024]{2,1,0:T(8,128)(2,1)S(1)}, bf16[2,512,1024]{2,1,0:T(8,128)(2,1)}, u32[]{:S(2)}) copy-start(bf16[2,512,1024]{2,1,0:T(8,128)(2,1)} %param.7) | copy-start | bytes 6291460
  0.0 26.5 %collective-permute-start.2 = (bf16[1024,4096]{1,0:T(8,128)(2,1)}, bf16[1024,4096]{1,0:T(8,128)(2,1)}, u32[]{:S(2)}, u32[]{:S(2)}) collective-permute-start(bf16[1024,4096]{1,0:T(8,128)(2,1)} %refs_4_.1), channel_id=1, source_target_pairs={{0,1},{1,0},{2,3},{3,2},{4,5},{5,4},{6,7},{7,6},{8,9},{9,8},{10,11... | collective-permute-start | bytes 25165832 | tf_op jit(solution)/shard_map/ppermute | solution.py:370
  2.2 16.3 %copy-start.1 = (bf16[512,1024]{1,0:T(8,128)(2,1)S(1)}, bf16[512,1024]{1,0:T(8,128)(2,1)}, u32[]{:S(2)}) copy-start(bf16[512,1024]{1,0:T(8,128)(2,1)} %param.6) | copy-start | bytes 3145732
  2.2 27.8 %copy-start.2 = (s32[4096]{0:T(1024)S(1)}, s32[4096]{0:T(1024)}, u32[]{:S(2)}) copy-start(s32[4096]{0:T(1024)} %param.9) | copy-start | bytes 49156
  2.2 13.1 %collective-permute-start.5 = (bf16[512,512]{1,0:T(8,128)(2,1)S(1)}, bf16[512,512]{1,0:T(8,128)(2,1)}, u32[]{:S(2)}, u32[]{:S(2)}) collective-permute-start(bf16[512,512]{1,0:T(8,128)(2,1)S(1)} %dynamic-slice_bitcast_fusion), channel_id=1, source_target_pairs={{0,4},{4,0},{8,12},{12,8},{16,20},{20,16},{24,28},{28,24},{1,5},{5... | collective-permute-start | bytes 1572872 | tf_op jit(solution)/shard_map/ppermute | solution.py:369
  2.6 23.9 %collective-permute-start.1 = (bf16[512,512]{1,0:T(8,128)(2,1)S(1)}, bf16[512,512]{1,0:T(8,128)(2,1)}, u32[]{:S(2)}, u32[]{:S(2)}) collective-permute-start(bf16[512,512]{1,0:T(8,128)(2,1)S(1)} %dynamic-slice_bitcast_fusion.1), channel_id=1, source_target_pairs={{0,4},{4,0},{8,12},{12,8},{16,20},{20,16},{24,28},{28,24},{1,5},{5... | collective-permute-start | bytes 1572872 | tf_op jit(solution)/shard_map/ppermute | solution.py:368
  3.9 49.1 %collective-permute-start.6 = (bf16[2,512,512]{2,1,0:T(8,128)(2,1)S(1)}, bf16[2,512,512]{2,1,0:T(8,128)(2,1)S(1)}, u32[]{:S(2)}, u32[]{:S(2)}) collective-permute-start(bf16[2,512,512]{2,1,0:T(8,128)(2,1)S(1)} %constant_dynamic-slice_fusion.2.kv_own), channel_id=1, source_target_pairs={{0,8},{4,12},{8,16},{12,20},{16,24},{20,28},{1,9},{5,13},{9,17},{1... | collective-permute-start | bytes 3145736 | tf_op jit(solution)/shard_map/ppermute | solution.py:367
  15.3 25.3 %collective-permute-start.7 = (bf16[512,512]{1,0:T(8,128)(2,1)}, bf16[512,512]{1,0:T(8,128)(2,1)}, u32[]{:S(2)}, u32[]{:S(2)}) collective-permute-start(bf16[512,512]{1,0:T(8,128)(2,1)} %collective-permute-done.5.v_other), channel_id=1, source_target_pairs={{0,8},{4,12},{8,16},{12,20},{16,24},{20,28},{1,9},{5,13},{9,17},{1... | collective-permute-start | bytes 1572872 | tf_op jit(solution)/shard_map/ppermute | solution.py:375
  26.5 14.8 %collective-permute-start.4 = (bf16[512,512]{1,0:T(8,128)(2,1)}, bf16[512,512]{1,0:T(8,128)(2,1)S(1)}, u32[]{:S(2)}, u32[]{:S(2)}) collective-permute-start(bf16[512,512]{1,0:T(8,128)(2,1)} %get-tuple-element.44), channel_id=1, source_target_pairs={{0,4},{4,0},{8,12},{12,8},{16,20},{20,16},{24,28},{28,24},{1,5},{5... | collective-permute-start | bytes 1572872 | tf_op jit(solution)/shard_map/ppermute | solution.py:373
  26.8 25.0 %collective-permute-start.3 = (bf16[512,512]{1,0:T(8,128)(2,1)}, bf16[512,512]{1,0:T(8,128)(2,1)}, u32[]{:S(2)}, u32[]{:S(2)}) collective-permute-start(bf16[512,512]{1,0:T(8,128)(2,1)} %collective-permute-done.1.k_other), channel_id=1, source_target_pairs={{0,8},{4,12},{8,16},{12,20},{16,24},{20,28},{1,9},{5,13},{9,17},{1... | collective-permute-start | bytes 1572872 | tf_op jit(solution)/shard_map/ppermute | solution.py:374
  53.0 8.3 %slice-start = ((s8[8388608]{0:T(1024)(128)(4,1)}), s8[4194304]{0:T(1024)(128)(4,1)S(1)}, s32[]{:S(2)}) async-start(s8[8388608]{0:T(1024)(128)(4,1)} %bitcast.8), calls=%async_computation | async-start | bytes 8388608
  53.0 8.3 %slice-start.1 = ((s8[8388608]{0:T(1024)(128)(4,1)}), s8[4194304]{0:T(1024)(128)(4,1)S(1)}, s32[]{:S(2)}) async-start(s8[8388608]{0:T(1024)(128)(4,1)} %bitcast.8), calls=%async_computation.1 | async-start | bytes 8388608
  57.4 3.9 %collective-permute-start.10 = (bf16[128,512]{1,0:T(8,128)(2,1)S(1)}, bf16[128,512]{1,0:T(8,128)(2,1)S(1)}, u32[]{:S(2)}, u32[]{:S(2)}) collective-permute-start(bf16[128,512]{1,0:T(8,128)(2,1)S(1)} %get-tuple-element.56), channel_id=1, source_target_pairs={{0,1},{1,0},{2,3},{3,2},{4,5},{5,4},{6,7},{7,6},{8,9},{9,8},{10,11... | collective-permute-start | bytes 393224 | tf_op jit(solution)/shard_map/ppermute | solution.py:424
  59.5 6.0 %collective-permute-start.8 = (bf16[128,512]{1,0:T(8,128)(2,1)S(1)}, bf16[128,512]{1,0:T(8,128)(2,1)S(1)}, u32[]{:S(2)}, u32[]{:S(2)}) collective-permute-start(bf16[128,512]{1,0:T(8,128)(2,1)S(1)} %get-tuple-element.52), channel_id=1, source_target_pairs={{0,4},{4,0},{8,12},{12,8},{16,20},{20,16},{24,28},{28,24},{1,5},{5... | collective-permute-start | bytes 393224 | tf_op jit(solution)/shard_map/ppermute | solution.py:425
  59.8 7.8 %collective-permute-start.9 = (bf16[128,512]{1,0:T(8,128)(2,1)S(1)}, bf16[128,512]{1,0:T(8,128)(2,1)S(1)}, u32[]{:S(2)}, u32[]{:S(2)}) collective-permute-start(bf16[128,512]{1,0:T(8,128)(2,1)S(1)} %get-tuple-element.53), channel_id=1, source_target_pairs={{0,5},{1,4},{2,7},{3,6},{4,1},{5,0},{6,3},{7,2},{8,13},{9,12},{10,... | collective-permute-start | bytes 393224 | tf_op jit(solution)/shard_map/ppermute | solution.py:426
  70.7 27.2 %collective-permute-start.14 = (bf16[128,2048]{1,0:T(8,128)(2,1)S(1)}, bf16[128,2048]{1,0:T(8,128)(2,1)S(1)}, u32[]{:S(2)}, u32[]{:S(2)}) collective-permute-start(bf16[128,2048]{1,0:T(8,128)(2,1)S(1)} %shard_map.50), channel_id=1, source_target_pairs={{0,2},{1,3},{2,0},{3,1},{4,6},{5,7},{6,4},{7,5},{8,10},{9,11},{10,... | collective-permute-start | bytes 1572872 | tf_op jit(solution)/shard_map/ppermute | solution.py:449
  76.8 21.1 %collective-permute-start.15 = (bf16[128,2048]{1,0:T(8,128)(2,1)S(1)}, bf16[128,2048]{1,0:T(8,128)(2,1)S(1)}, u32[]{:S(2)}, u32[]{:S(2)}) collective-permute-start(bf16[128,2048]{1,0:T(8,128)(2,1)S(1)} %shard_map.51), channel_id=1, source_target_pairs={{0,2},{1,3},{2,0},{3,1},{4,6},{5,7},{6,4},{7,5},{8,10},{9,11},{10,... | collective-permute-start | bytes 1572872 | tf_op jit(solution)/shard_map/ppermute | solution.py:449
  82.7 2.3 %collective-permute-start.11 = (bf16[128,512]{1,0:T(8,128)(2,1)S(1)}, bf16[128,512]{1,0:T(8,128)(2,1)S(1)}, u32[]{:S(2)}, u32[]{:S(2)}) collective-permute-start(bf16[128,512]{1,0:T(8,128)(2,1)S(1)} %get-tuple-element.59), channel_id=1, source_target_pairs={{0,1},{1,0},{2,3},{3,2},{4,5},{5,4},{6,7},{7,6},{8,9},{9,8},{10,11... | collective-permute-start | bytes 393224 | tf_op jit(solution)/shard_map/ppermute | solution.py:424
  83.3 5.1 %collective-permute-start.12 = (bf16[128,512]{1,0:T(8,128)(2,1)S(1)}, bf16[128,512]{1,0:T(8,128)(2,1)S(1)}, u32[]{:S(2)}, u32[]{:S(2)}) collective-permute-start(bf16[128,512]{1,0:T(8,128)(2,1)S(1)} %get-tuple-element.60), channel_id=1, source_target_pairs={{0,4},{4,0},{8,12},{12,8},{16,20},{20,16},{24,28},{28,24},{1,5},{5... | collective-permute-start | bytes 393224 | tf_op jit(solution)/shard_map/ppermute | solution.py:425
  83.5 8.1 %collective-permute-start.13 = (bf16[128,512]{1,0:T(8,128)(2,1)S(1)}, bf16[128,512]{1,0:T(8,128)(2,1)S(1)}, u32[]{:S(2)}, u32[]{:S(2)}) collective-permute-start(bf16[128,512]{1,0:T(8,128)(2,1)S(1)} %get-tuple-element.61), channel_id=1, source_target_pairs={{0,5},{1,4},{2,7},{3,6},{4,1},{5,0},{6,3},{7,2},{8,13},{9,12},{10,... | collective-permute-start | bytes 393224 | tf_op jit(solution)/shard_map/ppermute | solution.py:426

commit v4 on v3

--- a/solution.py
+++ b/solution.py
@@ -46,6 +46,17 @@
     return pl.multiple_of(value, of)
 
 
+def top_row(head):
+    return head // 2 * 4 + head % 2
+
+
+def stacked(tops, totals):
+    rows = []
+    for first in range(0, len(tops), 2):
+        rows += tops[first : first + 2] + totals[first : first + 2]
+    return jnp.concatenate(rows, axis=0)
+
+
 def fresh_tiles(heads, jobs, summed, stats):
     entries = [scores_of(k, q, bias) for k, q, v, bias, span in jobs]
     tops = [jnp.max(e, axis=0, keepdims=True) for e in entries]
@@ -56,7 +67,7 @@
     ]
     for first in range(0, len(jobs), heads):
         span, these = jobs[first][4], slice(first, first + heads)
-        stats[:, span] = jnp.concatenate(tops[these] + totals[these], axis=0)
+        stats[:, span] = stacked(tops[these], totals[these])
         for h in range(heads):
             summed[head_cols(h), span] = sums[first + h]
 
@@ -64,22 +75,23 @@
 def fold_tiles(heads, keys, queries, values, bias, span, summed, stats):
     before = stats[:, span]
     olds = [summed[head_cols(h), span] for h in range(heads)]
+    old_tops = [before[top_row(h) : top_row(h) + 1] for h in range(heads)]
+    old_totals = [before[top_row(h) + 2 : top_row(h) + 3] for h in range(heads)]
     entries = [scores_of(k, q, bias) for k, q in zip(keys, queries)]
     tops = [
-        jnp.maximum(before[h : h + 1], jnp.max(e, axis=0, keepdims=True))
-        for h, e in enumerate(entries)
-    ]
-    shrinks = [jnp.exp2(before[h : h + 1] - t) for h, t in enumerate(tops)]
+        jnp.maximum(old, jnp.max(e, axis=0, keepdims=True)) for old, e in zip(old_tops, entries)
+    ]
+    shrinks = [jnp.exp2(old - t) for old, t in zip(old_tops, tops)]
     weights = [jnp.exp2(e - t) for e, t in zip(entries, tops)]
     totals = [
-        before[heads + h : heads + h + 1] * shrinks[h] + jnp.sum(w, axis=0, keepdims=True)
-        for h, w in enumerate(weights)
+        old * s + jnp.sum(w, axis=0, keepdims=True)
+        for old, s, w in zip(old_totals, shrinks, weights)
     ]
     sums = [
         o * s + jnp.dot(v, w.astype(BF16), preferred_element_type=F32)
         for o, s, v, w in zip(olds, shrinks, values, weights)
     ]
-    stats[:, span] = jnp.concatenate(tops + totals, axis=0)
+    stats[:, span] = stacked(tops, totals)
     for h in range(heads):
         summed[head_cols(h), span] = sums[h]
 
@@ -123,17 +135,19 @@
         one(nearest - count * TILE, TILE)
 
 
-def pair_kernel(heads, shard, pad, ids, docs, docs_row, q_own, kv_own, q_other, k_other, v_other,
+def pair_kernel(heads, shard, pad, ids, docs, docs_row, q_own, kv_own, q_other, kv_other_a, kv_other_b,
                 summed, stats, qs, ks, vts):
     side = lax.rem(ids[0], 2)
     own = pl.ds(multiple(side * shard, shard), shard)
     other = pl.ds(multiple((1 - side) * shard, shard), shard)
     ks[own, :] = kv_own[0]
-    ks[other, :] = k_other[...]
+    for number, part in enumerate((kv_other_a, kv_other_b)):
+        cols = pl.ds(number * 2 * HD, 2 * HD)
+        ks[other, cols] = part[0]
+        transposed(2, part.at[1], vts.at[cols], other)
     qs[own, :] = q_own[...]
     qs[other, :] = q_other[...]
     transposed(heads, kv_own.at[1], vts, own)
-    transposed(heads, v_other, vts, other)
 
     for step in range(shard // TILE):
         jobs = []
@@ -168,26 +182,29 @@
         lax.fori_loop(0, shard // TILE, one_tile, 0)
 
 
-def remote_kernel(heads, shard, pad, wave, ids, docs, docs_row, q_own, q_other, summed_in, stats_in, *rest):
-    (same, k_cross, v_cross, kv_far), rest = rest[:4], rest[4:]
-    sources = ((k_cross, v_cross), (same.at[0], same.at[1]))
-    outs, (qs, ks, vts, done, summed, stats, sems) = rest[:4], rest[4:]
-    half = heads * HD
+def remote_kernel(groups, shard, pad, wave, ids, docs, docs_row, q_own, q_other, summed_in, stats_in, same,
+                  kv_far, *rest):
+    crossed, rest = rest[: len(groups)], rest[len(groups) :]
+    outs, (qs, ks, vts, done, summed, stats_all, stats, sems) = rest[:4], rest[4:]
+    heads = 2 * len(groups)
+    width = heads * HD
     side = lax.rem(ids[0], 2)
     core, y_own = lax.rem(ids[1], 2), ids[1] // 2
     y_part = 1 - y_own if wave == 0 else y_own
     part_at = multiple(y_part * TILE, TILE)
     rows = pl.ds(part_at, TILE)
+    later = pl.ds(multiple(shard + part_at, TILE), TILE)
+    cols = pl.ds(groups[0] * 2 * HD, width)
     copies = [
         pltpu.make_async_copy(a, b, sems.at[i])
         for i, (a, b) in enumerate(
             (
-                (q_own.at[rows, :], qs.at[side]),
-                (q_other.at[rows, :], qs.at[1 - side]),
-                (summed_in.at[:, rows], summed.at[0]),
-                (stats_in.at[:, rows], stats.at[0]),
-                (summed_in.at[:, pl.ds(multiple(shard + part_at, TILE), TILE)], summed.at[1]),
-                (stats_in.at[:, pl.ds(multiple(shard + part_at, TILE), TILE)], stats.at[1]),
+                (q_own.at[rows, cols], qs.at[side]),
+                (q_other.at[rows, cols], qs.at[1 - side]),
+                (summed_in.at[cols, rows], summed.at[0]),
+                (stats_in.at[:, rows], stats_all.at[0]),
+                (summed_in.at[cols, later], summed.at[1]),
+                (stats_in.at[:, later], stats_all.at[1]),
             )
         )
     ]
@@ -202,9 +219,10 @@
 
     most = reach(part_at)
 
-    def place_keys(keys, values, at, size):
-        ks[pl.ds(at, size), :] = keys[...]
-        transposed(heads, values, vts, pl.ds(at, size))
+    def place_keys(keys, values, number, at, size):
+        cols = pl.ds(number * 2 * HD, 2 * HD)
+        ks[pl.ds(at, size), cols] = keys[...]
+        transposed(2, values, vts.at[cols], pl.ds(at, size))
 
     for back in range(pad // TILE):
         at = pad - (back + 1) * TILE
@@ -213,31 +231,45 @@
         def _():
             if back == 4:
                 blank = TILE - FAR_ROWS
-                ks[at : at + blank, :] = jnp.zeros((blank, half), BF16)
-                vts[:, at : at + blank] = jnp.zeros((half, blank), BF16)
-                place_keys(kv_far.at[0], kv_far.at[1], at + blank, FAR_ROWS)
+                ks[at : at + blank, :] = jnp.zeros((blank, width), BF16)
+                vts[:, at : at + blank] = jnp.zeros((width, blank), BF16)
+                for number, group in enumerate(groups):
+                    mine = pl.ds(group * 2 * HD, 2 * HD)
+                    place_keys(
+                        kv_far.at[0, :, mine], kv_far.at[1, :, mine], number, at + blank, FAR_ROWS
+                    )
             else:
                 part = pl.ds((1 - back % 2) * TILE, TILE)
-                for which, (keys, values) in enumerate(sources if back < 2 else sources[::-1]):
-
-                    @pl.when(side == which)
-                    def _():
-                        place_keys(keys.at[part], values.at[part], at, TILE)
+
+                @pl.when(side == back // 2)
+                def _():
+                    for number in range(len(groups)):
+                        place_keys(
+                            crossed[number].at[0, part], crossed[number].at[1, part], number, at, TILE
+                        )
+
+                @pl.when(side == 1 - back // 2)
+                def _():
+                    for number, group in enumerate(groups):
+                        mine = pl.ds(group * 2 * HD, 2 * HD)
+                        place_keys(same.at[0, part, mine], same.at[1, part, mine], number, at, TILE)
 
     waited(copies)
+    for step in range(2):
+        stats[step] = stats_all[step, 4 * groups[0] : 4 * groups[0] + 2 * heads, :]
     whole = pl.ds(0, TILE)
 
     def one_tile(step, _):
         here = multiple(step * shard + part_at, TILE)
-        mine = pl.ds(multiple(step * TILE, TILE), TILE)
         query_docs = docs_row[:, pl.ds(multiple(pad + here, TILE), TILE)]
-
         fold_keys(
             heads, ks, qs.at[step], vts, docs_row, query_docs, reach(here), pad, 0, whole,
             summed.at[step], stats.at[step],
         )
+        mine = pl.ds(multiple(step * TILE, TILE), TILE)
         for head in range(heads):
-            part = summed[step, head_cols(head), :] / stats[step, heads + head : heads + head + 1, :]
+            total = stats[step, top_row(head) + 2 : top_row(head) + 3, :]
+            part = summed[step, head_cols(head), :] / total
             done[mine, head_cols(head)] = part.astype(BF16).T
         return 0
 
@@ -249,7 +281,8 @@
         out[...] = done[pl.ds(multiple((to_side * 2 + to_core) * block, block), block), :]
 
 
-def project_kernel(count, turns, ring, part, chunk, begun, ids, *refs):
+def project_kernel(places, half, ring, part, chunk, begun, ids, *refs):
+    count = len(places)
     pieces, (w_near, w_other) = refs[:count], refs[count : count + 2]
     out, held, sems = refs[-3:]
     side = lax.rem(ids[0], 2)
@@ -259,13 +292,13 @@
 
     def copies(step):
         made = []
-        for number, turn in enumerate(turns):
+        for number, (turn, row) in enumerate(places):
             source = w_other if turn % 2 else w_near
             to_side = 1 - side if turn // 2 else side
             made.append(
                 pltpu.make_async_copy(
                     source.at[
-                        pl.ds(multiple(to_side * width, width), width),
+                        pl.ds(multiple(to_side * half + row, width), width),
                         pl.ds(first + step * chunk, chunk),
                     ],
                     held.at[step % ring, number],
@@ -365,31 +398,22 @@
     kv_own = mine(keys_values, 2)
     queries, keys_values, kv_own = lax.optimization_barrier((queries, keys_values, kv_own))
     same = lax.ppermute(kv_own, "ctx", hop)
-    k_other = lax.ppermute(theirs(keys_values[0], 1), "ctx", swap)
-    v_other = lax.ppermute(theirs(keys_values[1], 1), "ctx", swap)
+    quarter = half // 2
+    kv_other = [
+        lax.ppermute(
+            lax.dynamic_slice_in_dim(keys_values, (1 - side) * half + group * quarter, quarter, 2),
+            "ctx",
+            swap,
+        )
+        for group in range(2)
+    ]
     w_other = lax.ppermute(w_out, "head", core)
     q_send, q_own = theirs(queries, 1), mine(queries, 1)
-    q_send, k_other, w_other = lax.optimization_barrier((q_send, k_other, w_other))
+    q_send, kv_other[0], w_other = lax.optimization_barrier((q_send, kv_other[0], w_other))
     q_other = lax.ppermute(q_send, "ctx", swap)
-    late_k = lax.ppermute(k_other, "ctx", hop)
-    late_v = lax.ppermute(v_other, "ctx", hop)
-
-    last = shard - FAR_ROWS
-    tails = [kv_own[:, last:], k_other[last:], v_other[last:]]
-    late_v, tails = lax.optimization_barrier((late_v, tails))
-
-    def far_hop(own, k, v):
-        return lax.ppermute(jnp.where(side == 1, own, jnp.stack([k, v])), "ctx", far)
-
-    blocks = doc_index.reshape(-1, rows)
-    kv_far = lax.cond(
-        jnp.any(blocks[:-2, -1] == blocks[2:, 0]),
-        far_hop,
-        lambda own, k, v: jnp.zeros_like(own),
-        *tails,
-    )
-    arrivals = [same, late_k, late_v, kv_far]
-    ids_late = after(ids, [late_k], HOLD)
+    crossed = [lax.ppermute(part, "ctx", hop) for part in kv_other]
+
+    ids_late = after(ids, crossed[:1], HOLD)
 
     summed, stats = call(
         functools.partial(pair_kernel, heads, shard, pad),
@@ -397,25 +421,55 @@
         [vmem((rows, half), BF16)] * 2 + [vmem((half, rows), BF16)],
         7,
         [IN_SMEM, IN_SMEM] + [IN_VMEM] * 6,
-        [ids, docs, docs_row, q_own, kv_own, q_other, k_other, v_other],
+        [ids, docs, docs_row, q_own, kv_own, q_other, *kv_other],
     )
 
-    def finished(wave, stats):
+    def far_hop(own, *parts):
+        tail = jnp.where(side == 1, own, jnp.concatenate(parts, axis=2))
+        turn = me // 4 % 2
+
+        def pairs(first):
+            groups = [[c, (c + 4) % n_ctx] for c in range(n_ctx) if c // 4 % 2 == first]
+            return lax.all_to_all(
+                jnp.stack([tail, tail]), "ctx", 0, 0, axis_index_groups=groups
+            )[0]
+
+        got = pairs(0)
+        if n_ctx > 8:
+            got = jnp.where(turn == 1, got, pairs(1))
+        return got
+
+    last = shard - FAR_ROWS
+    blocks = doc_index.reshape(-1, rows)
+    tails = [kv_own[:, last:]] + [part[:, last:] for part in kv_other]
+    stats, tails = lax.optimization_barrier((stats, tails))
+    kv_far = lax.cond(
+        jnp.any(blocks[:-2, -1] == blocks[2:, 0]),
+        far_hop,
+        lambda own, *parts: jnp.zeros_like(own),
+        *tails,
+    )
+
+    def finished(wave, groups, ids, stats):
+        heads = 2 * len(groups)
+        width = heads * HD
         return call(
-            functools.partial(remote_kernel, heads, shard, pad, wave),
-            [((block, half), BF16)] * 4,
+            functools.partial(remote_kernel, groups, shard, pad, wave),
+            [((block, width), BF16)] * 4,
             [
-                vmem((2, TILE, half), BF16),
-                vmem((pad, half), BF16),
-                vmem((half, pad), BF16),
-                vmem((2 * TILE, half), BF16),
-                vmem((2, half, TILE), F32),
+                vmem((2, TILE, width), BF16),
+                vmem((pad, width), BF16),
+                vmem((width, pad), BF16),
+                vmem((2 * TILE, width), BF16),
+                vmem((2, width, TILE), F32),
+                vmem((2, 8, TILE), F32),
                 vmem((2, 2 * heads, TILE), F32),
                 sems((6,)),
             ],
-            5e6 if wave == 0 else 1,
-            [IN_SMEM, IN_SMEM, IN_VMEM] + [IN_HBM] * 4 + [IN_VMEM] * len(arrivals),
-            [ids_late, docs, docs_row, q_own, q_other, summed, stats, *arrivals],
+            5e6 if wave == 0 and groups == (1,) else 1,
+            [IN_SMEM, IN_SMEM, IN_VMEM] + [IN_HBM] * 4 + [IN_VMEM] * (2 + len(groups)),
+            [ids, docs, docs_row, q_own, q_other, summed, stats, same, kv_far]
+            + [crossed[group] for group in groups],
         )
 
     def exchanged(pieces):
@@ -426,30 +480,37 @@
             lax.ppermute(pieces[3], ("ctx", "head"), both),
         ]
 
-    def project(pieces, turns, begun, kind, part, parts):
+    def project(pieces, places, begun, kind, part, parts):
         columns = w_out.shape[1] // parts
-        chunk, ring = 512, 16 // len(pieces)
+        width = pieces[0].shape[1]
+        chunk, ring = 512, min(8, 8192 // (width * len(pieces)))
         more = [] if begun is None else [begun]
         (out,) = call(
-            functools.partial(
-                project_kernel, len(pieces), turns, ring, part, chunk, begun is not None
-            ),
+            functools.partial(project_kernel, places, half, ring, part, chunk, begun is not None),
             [((block, columns), kind)],
-            [vmem((ring, len(pieces), half, chunk), BF16), sems((ring, len(pieces)))],
-            2 * len(pieces) // parts,
+            [vmem((ring, len(pieces), width, chunk), BF16), sems((ring, len(pieces)))],
+            1,
             [IN_SMEM] + [IN_VMEM] * len(pieces) + [IN_HBM] * 2 + [IN_VMEM] * len(more),
             [ids, *pieces, w_out, w_other, *more],
         )
         return out
 
     parts = 2
-    pieces = exchanged(finished(0, stats))
-    begun = project(pieces[:2], (0, 1), None, F32, 0, 1)
-    leaving = [project(pieces[2:], (2, 3), begun, BF16, part, parts) for part in range(parts)]
+    early = exchanged(finished(0, (0,), ids, stats))
+    late = exchanged(finished(0, (1,), ids_late, stats))
+    begun = project(
+        early[:2] + late[:2] + early[2:],
+        ((0, 0), (1, 0), (0, quarter), (1, quarter), (2, 0), (3, 0)),
+        None, F32, 0, 1,
+    )
+    leaving = [
+        project(late[2:], ((2, quarter), (3, quarter)), begun, BF16, part, parts)
+        for part in range(parts)
+    ]
     arrived = [lax.ppermute(part, "head", far_y) for part in leaving]
     stats, leaving = lax.optimization_barrier((stats, leaving))
-    pieces = exchanged(finished(1, stats))
-    staying = project(pieces, (0, 1, 2, 3), None, F32, 0, 1)
+    pieces = exchanged(finished(1, (0, 1), ids_late, stats))
+    staying = project(pieces, tuple((turn, 0) for turn in range(4)), None, F32, 0, 1)
     (out,) = call(
         add_kernel,
         [((block, w_out.shape[1]), BF16)],

time: 98.3 us -> 95 us (0.966)
  the two profiles are of different devices: /device:TPU:19 before, /device:TPU:24 now
where the time goes in v4:
time: 95 us; the launch traced here: 93.7 us
  Pallas kernels  34.4 us (36%)
  waiting for transfers between devices  33.2 us (35%)
  starting transfers between devices  15.6 us (16%)
  local copies, waits for them, and re-layouts  8.78 us (9%)
    pallas_call x9, Pallas kernels, call(): pl.pallas_call(kernel, in_specs=specs, out_specs=[IN_VMEM] * len(outs), o...  33.3 us
    ppermute x2, waiting for transfers between devices, per_device(): lax.ppermute(lax.dynamic_slice_in_dim(keys_values, (1 - side) * half + gr...  18.6 us
    slice x3, local copies, waits for them, and re-layouts, per_device(): tails = [kv_own[:, last:]] + [part[:, last:] for part in kv_other]  4.82 us
    ppermute x3, waiting for transfers between devices, exchanged(): lax.ppermute(pieces[2], 'ctx', swap)  4.5 us
    dynamic_slice x2, local copies, waits for them, and re-layouts, mine(): return lax.dynamic_slice_in_dim(array, side * half, half, axis)  3.68 us
    ppermute x2, waiting for transfers between devices, per_device(): crossed = [lax.ppermute(part, 'ctx', hop) for part in kv_other]  3.39 us
    ppermute x1, waiting for transfers between devices, per_device(): q_other = lax.ppermute(q_send, 'ctx', swap)  2.84 us
    ppermute x3, starting transfers between devices, exchanged(): lax.ppermute(pieces[3], ('ctx', 'head'), both)  2.81 us
  transfers between devices with their start and end apart: 18, of which 7 were waited for; matrix products, arithmetic and copies ran while one was open for 10% of the time, Pallas kernels for 33%

profile of v4, /device:TPU:24, one launch (start us, length us, event | category | flops | bytes accessed | tf_op | source)
XLA Modules:
  0.0 93.7 jit_solution(2752416716215544679)
XLA Ops:
  0.0 0.0 copy-start
  0.0 0.0 collective-permute-start.1
  0.0 2.4 %constant_dynamic-slice_fusion.4.kv_own = bf16[2,512,512]{2,1,0:T(8,128)(2,1)} fusion(bf16[2,512,1024]{2,1,0:T(8,128)(2,1)} %param.7, s32[]{:T(128)S(6)} %select_n.27), kind=kLoop, calls=%fused_computation.10 | loop fusion | bytes 2097156 | tf_op jit(solution)/shard_map/dynamic_slice | solution.py:393
  2.4 0.0 copy-done
  2.4 0.0 copy-start.1
  2.4 0.1 constant_dynamic-slice_fusion
  2.6 1.6 %collective-permute-start = (bf16[2,512,256]{2,1,0:T(8,128)(2,1)S(1)}, bf16[2,512,256]{2,1,0:T(8,128)(2,1)}, u32[]{:S(2)}, u32[]{:S(2)}) collective-permute-start(bf16[2,512,256]{2,1,0:T(8,128)(2,1)S(1)} %get-tuple-element.71), channel_id=1, source_target_pairs={{0,4},{4,0},{8,12},{12,8},{16,20},{20,16},{24,28},{28,24},{1,5},{5... | collective-permute-start | bytes 1572872 | tf_op jit(solution)/shard_map/ppermute | solution.py:403
  4.1 1.3 %collective-permute-start.5 = (bf16[2,512,512]{2,1,0:T(8,128)(2,1)}, bf16[2,512,512]{2,1,0:T(8,128)(2,1)}, u32[]{:S(2)}, u32[]{:S(2)}) collective-permute-start(bf16[2,512,512]{2,1,0:T(8,128)(2,1)} %constant_dynamic-slice_fusion.4.kv_own), channel_id=1, source_target_pairs={{0,8},{4,12},{8,16},{12,20},{16,24},{20,28},{1,9},{5,13},{9,17},{1... | collective-permute-start | bytes 3145736 | tf_op jit(solution)/shard_map/ppermute | solution.py:400
  5.4 0.6 collective-permute-start.4
  6.0 1.3 %constant_dynamic-slice_fusion.1 = (bf16[512,512]{1,0:T(8,128)(2,1)S(1)}, bf16[512,512]{1,0:T(8,128)(2,1)S(1)}) fusion(bf16[512,1024]{1,0:T(8,128)(2,1)} %param.6, s32[]{:T(128)S(6)} %select_n.27, s32[]{:T(128)S(6)} %select_n.28), kind=kLoop, calls=%fused_computation.7 | loop fusion | bytes 2097160 | tf_op jit(solution)/shard_map/dynamic_slice | solution.py:393
  7.3 10.2 %collective-permute-done.kv_other_a = bf16[2,512,256]{2,1,0:T(8,128)(2,1)} collective-permute-done((bf16[2,512,256]{2,1,0:T(8,128)(2,1)S(1)}, bf16[2,512,256]{2,1,0:T(8,128)(2,1)}, u32[]{:S(2)}, u32[]{:S(2)}) %collective-permute-start) | collective-permute-done | bytes 524320 | tf_op jit(solution)/shard_map/ppermute | solution.py:403
  17.5 0.0 collective-permute-done.1.refs_7_.refs_3_.refs_5_
  17.5 1.5 %collective-permute-start.3 = (bf16[512,512]{1,0:T(8,128)(2,1)S(1)}, bf16[512,512]{1,0:T(8,128)(2,1)S(1)}, u32[]{:S(2)}, u32[]{:S(2)}) collective-permute-start(bf16[512,512]{1,0:T(8,128)(2,1)S(1)} %get-tuple-element.48), channel_id=1, source_target_pairs={{0,4},{4,0},{8,12},{12,8},{16,20},{20,16},{24,28},{28,24},{1,5},{5... | collective-permute-start | bytes 1572872 | tf_op jit(solution)/shard_map/ppermute | solution.py:413
  19.0 1.3 %collective-permute-start.2 = (bf16[2,512,256]{2,1,0:T(8,128)(2,1)}, bf16[2,512,256]{2,1,0:T(8,128)(2,1)}, u32[]{:S(2)}, u32[]{:S(2)}) collective-permute-start(bf16[2,512,256]{2,1,0:T(8,128)(2,1)} %collective-permute-done.kv_other_a), channel_id=1, source_target_pairs={{0,8},{4,12},{8,16},{12,20},{16,24},{20,28},{1,9},{5,13},{9,17},{1... | collective-permute-start | bytes 1572872 | tf_op jit(solution)/shard_map/ppermute | solution.py:414
  20.3 8.5 %collective-permute-done.4.kv_other_b = bf16[2,512,256]{2,1,0:T(8,128)(2,1)} collective-permute-done((bf16[2,512,256]{2,1,0:T(8,128)(2,1)S(1)}, bf16[2,512,256]{2,1,0:T(8,128)(2,1)}, u32[]{:S(2)}, u32[]{:S(2)}) %collective-permute-start.4) | collective-permute-done | bytes 524320 | tf_op jit(solution)/shard_map/ppermute | solution.py:403
  28.7 1.3 %collective-permute-start.6 = (bf16[2,512,256]{2,1,0:T(8,128)(2,1)}, bf16[2,512,256]{2,1,0:T(8,128)(2,1)}, u32[]{:S(2)}, u32[]{:S(2)}) collective-permute-start(bf16[2,512,256]{2,1,0:T(8,128)(2,1)} %collective-permute-done.4.kv_other_b), channel_id=1, source_target_pairs={{0,8},{4,12},{8,16},{12,20},{16,24},{20,28},{1,9},{5,13},{9,17},{1... | collective-permute-start | bytes 1572872 | tf_op jit(solution)/shard_map/ppermute | solution.py:414
  30.0 1.7 %slice.18 = bf16[2,128,512]{2,1,0:T(8,128)(2,1)} slice(bf16[2,512,512]{2,1,0:T(8,128)(2,1)} %constant_dynamic-slice_fusion.4.kv_own), slice={[0:2], [384:512], [0:512]} | slice | bytes 524288 | tf_op jit(solution)/shard_map/slice | solution.py:444
  31.7 0.0 copy-done.1
  31.7 0.1 pad_dynamic-slice_fusion.docs
  31.8 0.8 compare_reduce_fusion
  33.2 0.1 pad_add_fusion.ids
  33.3 1.6 %slice.24 = bf16[2,128,256]{2,1,0:T(8,128)(2,1)} slice(bf16[2,512,256]{2,1,0:T(8,128)(2,1)} %collective-permute-done.4.kv_other_b), slice={[0:2], [384:512], [0:256]} | slice | bytes 262144 | tf_op jit(solution)/shard_map/slice | solution.py:444
  34.9 1.6 %slice.19 = bf16[2,128,256]{2,1,0:T(8,128)(2,1)} slice(bf16[2,512,256]{2,1,0:T(8,128)(2,1)} %collective-permute-done.kv_other_a), slice={[0:2], [384:512], [0:256]} | slice | bytes 262144 | tf_op jit(solution)/shard_map/slice | solution.py:444
  36.4 2.8 %collective-permute-done.3.q_other = bf16[512,512]{1,0:T(8,128)(2,1)S(1)} collective-permute-done((bf16[512,512]{1,0:T(8,128)(2,1)S(1)}, bf16[512,512]{1,0:T(8,128)(2,1)S(1)}, u32[]{:S(2)}, u32[]{:S(2)}) %collective-permute-start.3) | collective-permute-done | bytes 524320 | tf_op jit(solution)/shard_map/ppermute | solution.py:413
  39.3 5.4 %shard_map.47 = (f32[512,1024]{1,0:T(8,128)S(1)}, f32[8,1024]{1,0:T(8,128)S(1)}) custom-call(s32[2]{0:T(128)S(1)} %pad_add_fusion.ids, s32[2304]{0:T(1024)S(1)} %pad_dynamic-slice_fusion.docs, s32[1,2304]{1,0:T(1,128)S(1)} %reshape.7.docs_row, bf16[512,512]{1,0:T(8,128)(2,1)S(1)} %get-tuple-element.72.q_own, ...), custom_call_target="tpu_custom_call" | custom-call | flops 7000 | bytes 1024 | tf_op jit(solution)/shard_map/pallas_call | solution.py:351
  44.8 0.0 collective-permute-done.5.same
  44.8 0.0 collective-permute-done.2.refs_0_.rest_0_
  44.8 2.7 %shard_map.49 = (bf16[128,256]{1,0:T(8,128)(2,1)S(1)}, bf16[128,256]{1,0:T(8,128)(2,1)S(1)}, bf16[128,256]{1,0:T(8,128)(2,1)S(1)}, bf16[128,256]{1,0:T(8,128)(2,1)S(1)}) custom-call(s32[2]{0:T(128)S(1)} %pad_add_fusion.ids, s32[2304]{0:T(1024)S(1)} %pad_dynamic-slice_fusion.docs, s32[1,2304]{1,0:T(1,128)S(1)} %reshape.7.docs_row, ...), custom_call_target="tpu_custom_call" | custom-call | flops 1000 | bytes 1024 | tf_op jit(solution)/shard_map/pallas_call | solution.py:351
  47.4 0.1 collective-permute-start.9
  47.5 1.6 %collective-permute-start.11 = (bf16[128,256]{1,0:T(8,128)(2,1)S(1)}, bf16[128,256]{1,0:T(8,128)(2,1)S(1)}, u32[]{:S(2)}, u32[]{:S(2)}) collective-permute-start(bf16[128,256]{1,0:T(8,128)(2,1)S(1)} %get-tuple-element.63), channel_id=1, source_target_pairs={{0,4},{4,0},{8,12},{12,8},{16,20},{20,16},{24,28},{28,24},{1,5},{5... | collective-permute-start | bytes 196616 | tf_op jit(solution)/shard_map/ppermute | solution.py:479
  49.1 0.3 collective-permute-start.12
  49.4 0.0 slice-start
  49.4 1.1 %shard_map.46.ids = s32[2]{0:T(128)S(1)} custom-call(s32[2]{0:T(128)S(1)} %pad_add_fusion.ids, bf16[2,512,256]{2,1,0:T(8,128)(2,1)} %collective-permute-done.2.refs_0_.rest_0_), custom_call_target="tpu_custom_call" | custom-call | flops 550000000 | bytes 1024 | tf_op jit(solution)/shard_map/pallas_call | solution.py:338
  50.5 0.0 slice-start.1
  50.5 3.4 %collective-permute-done.6.rest_0_.rest_1_ = bf16[2,512,256]{2,1,0:T(8,128)(2,1)} collective-permute-done((bf16[2,512,256]{2,1,0:T(8,128)(2,1)}, bf16[2,512,256]{2,1,0:T(8,128)(2,1)}, u32[]{:S(2)}, u32[]{:S(2)}) %collective-permute-start.6) | collective-permute-done | bytes 524320 | tf_op jit(solution)/shard_map/ppermute | solution.py:414
  53.9 2.8 %shard_map.48 = (bf16[128,256]{1,0:T(8,128)(2,1)S(1)}, bf16[128,256]{1,0:T(8,128)(2,1)S(1)}, bf16[128,256]{1,0:T(8,128)(2,1)S(1)}, bf16[128,256]{1,0:T(8,128)(2,1)S(1)}) custom-call(s32[2]{0:T(128)S(1)} %shard_map.46.ids, s32[2304]{0:T(1024)S(1)} %pad_dynamic-slice_fusion.docs, s32[1,2304]{1,0:T(1,128)S(1)} %reshape.7.docs_row, ...), custom_call_target="tpu_custom_call" | custom-call | flops 5000000000 | bytes 1024 | tf_op jit(solution)/shard_map/pallas_call | solution.py:351
  56.8 0.1 collective-permute-start.10
  56.9 0.6 collective-permute-start.7
  57.5 0.0 collective-permute-done.9.refs_1_
  57.5 1.3 %collective-permute-start.8 = (bf16[128,256]{1,0:T(8,128)(2,1)S(1)}, bf16[128,256]{1,0:T(8,128)(2,1)S(1)}, u32[]{:S(2)}, u32[]{:S(2)}) collective-permute-start(bf16[128,256]{1,0:T(8,128)(2,1)S(1)} %get-tuple-element.57), channel_id=1, source_target_pairs={{0,5},{1,4},{2,7},{3,6},{4,1},{5,0},{6,3},{7,2},{8,13},{9,12},{10,... | collective-permute-start | bytes 196616 | tf_op jit(solution)/shard_map/ppermute | solution.py:480
  58.7 0.0 collective-permute-done.11.refs_4_
  58.7 0.0 collective-permute-done.12.refs_5_
  58.7 0.0 collective-permute-done.10.refs_3_
  58.7 0.0 slice-done
  58.7 0.0 slice-done.1
  58.8 5.2 %shard_map.50.refs_4_ = f32[128,4096]{1,0:T(8,128)S(1)} custom-call(s32[2]{0:T(128)S(1)} %pad_add_fusion.ids, bf16[128,256]{1,0:T(8,128)(2,1)S(1)} %get-tuple-element.59.refs_0_, bf16[128,256]{1,0:T(8,128)(2,1)S(1)} %collective-permute-done.9.refs_1_, bf16[128,256]{1,0:T(8,128)(2,1)S(1)} %get-tuple-element.61.refs_2_, ...), custom_call_target="tpu_custom_call" | custom-call | flops 1000 | bytes 1024 | tf_op jit(solution)/shard_map/pallas_call | solution.py:351
  64.0 0.0 collective-permute-done.7.refs_0_
  64.0 0.0 collective-permute-done.8.refs_1_
  64.0 2.6 %shard_map.51 = bf16[128,2048]{1,0:T(8,128)(2,1)S(1)} custom-call(s32[2]{0:T(128)S(1)} %pad_add_fusion.ids, bf16[128,256]{1,0:T(8,128)(2,1)S(1)} %collective-permute-done.7.refs_0_, bf16[128,256]{1,0:T(8,128)(2,1)S(1)} %collective-permute-done.8.refs_1_, bf16[1024,4096]{1,0:T(8,128)(2,1)S(1)} %bitcast.7, ...), custom_call_target="tpu_custom_call" | custom-call | flops 1000 | bytes 1024 | tf_op jit(solution)/shard_map/pallas_call | solution.py:351
  66.6 2.2 %collective-permute-start.16 = (bf16[128,2048]{1,0:T(8,128)(2,1)S(1)}, bf16[128,2048]{1,0:T(8,128)(2,1)S(1)}, u32[]{:S(2)}, u32[]{:S(2)}) collective-permute-start(bf16[128,2048]{1,0:T(8,128)(2,1)S(1)} %shard_map.51), channel_id=1, source_target_pairs={{0,2},{1,3},{2,0},{3,1},{4,6},{5,7},{6,4},{7,5},{8,10},{9,11},{10,... | collective-permute-start | bytes 1572872 | tf_op jit(solution)/shard_map/ppermute | solution.py:510
  68.9 2.6 %shard_map.52 = bf16[128,2048]{1,0:T(8,128)(2,1)S(1)} custom-call(s32[2]{0:T(128)S(1)} %pad_add_fusion.ids, bf16[128,256]{1,0:T(8,128)(2,1)S(1)} %collective-permute-done.7.refs_0_, bf16[128,256]{1,0:T(8,128)(2,1)S(1)} %collective-permute-done.8.refs_1_, bf16[1024,4096]{1,0:T(8,128)(2,1)S(1)} %bitcast.7, ...), custom_call_target="tpu_custom_call" | custom-call | flops 1000 | bytes 1024 | tf_op jit(solution)/shard_map/pallas_call | solution.py:351
  71.5 0.1 collective-permute-start.17
  71.6 4.5 %shard_map.53 = (bf16[128,512]{1,0:T(8,128)(2,1)S(1)}, bf16[128,512]{1,0:T(8,128)(2,1)S(1)}, bf16[128,512]{1,0:T(8,128)(2,1)S(1)}, bf16[128,512]{1,0:T(8,128)(2,1)S(1)}) custom-call(s32[2]{0:T(128)S(1)} %shard_map.46.ids, s32[2304]{0:T(1024)S(1)} %pad_dynamic-slice_fusion.docs, s32[1,2304]{1,0:T(1,128)S(1)} %reshape.7.docs_row, ...), custom_call_target="tpu_custom_call" | custom-call | flops 1000 | bytes 1024 | tf_op jit(solution)/shard_map/pallas_call | solution.py:351
  76.1 0.1 collective-permute-start.13
  76.2 0.6 collective-permute-start.14
  76.8 1.2 %collective-permute-start.15 = (bf16[128,512]{1,0:T(8,128)(2,1)S(1)}, bf16[128,512]{1,0:T(8,128)(2,1)S(1)}, u32[]{:S(2)}, u32[]{:S(2)}) collective-permute-start(bf16[128,512]{1,0:T(8,128)(2,1)S(1)} %get-tuple-element.69), channel_id=1, source_target_pairs={{0,5},{1,4},{2,7},{3,6},{4,1},{5,0},{6,3},{7,2},{8,13},{9,12},{10,... | collective-permute-start | bytes 393224 | tf_op jit(solution)/shard_map/ppermute | solution.py:480
  78.0 0.0 collective-permute-done.13.refs_1_
  78.0 4.5 %collective-permute-done.14.refs_2_ = bf16[128,512]{1,0:T(8,128)(2,1)S(1)} collective-permute-done((bf16[128,512]{1,0:T(8,128)(2,1)S(1)}, bf16[128,512]{1,0:T(8,128)(2,1)S(1)}, u32[]{:S(2)}, u32[]{:S(2)}) %collective-permute-start.14) | collective-permute-done | bytes 131104 | tf_op jit(solution)/shard_map/ppermute | solution.py:479
  82.5 1.9 %collective-permute-done.15.refs_3_ = bf16[128,512]{1,0:T(8,128)(2,1)S(1)} collective-permute-done((bf16[128,512]{1,0:T(8,128)(2,1)S(1)}, bf16[128,512]{1,0:T(8,128)(2,1)S(1)}, u32[]{:S(2)}, u32[]{:S(2)}) %collective-permute-start.15) | collective-permute-done | bytes 131104 | tf_op jit(solution)/shard_map/ppermute | solution.py:480
  84.4 6.3 %shard_map.54.staying = f32[128,4096]{1,0:T(8,128)S(1)} custom-call(s32[2]{0:T(128)S(1)} %pad_add_fusion.ids, bf16[128,512]{1,0:T(8,128)(2,1)S(1)} %get-tuple-element.66.refs_0_, bf16[128,512]{1,0:T(8,128)(2,1)S(1)} %collective-permute-done.13.refs_1_, bf16[128,512]{1,0:T(8,128)(2,1)S(1)} %collective-permute-done.14.refs_2_, ...), custom_call_target="tpu_custom_call" | custom-call | flops 1000 | bytes 1024 | tf_op jit(solution)/shard_map/pallas_call | solution.py:351
  90.7 0.0 collective-permute-done.16.refs_0_
  90.7 1.8 %collective-permute-done.17.refs_1_ = bf16[128,2048]{1,0:T(8,128)(2,1)S(1)} collective-permute-done((bf16[128,2048]{1,0:T(8,128)(2,1)S(1)}, bf16[128,2048]{1,0:T(8,128)(2,1)S(1)}, u32[]{:S(2)}, u32[]{:S(2)}) %collective-permute-start.17) | collective-permute-done | bytes 524320 | tf_op jit(solution)/shard_map/ppermute | solution.py:510
  92.6 1.1 %shard_map.55 = bf16[128,4096]{1,0:T(8,128)(2,1)} custom-call(f32[128,4096]{1,0:T(8,128)S(1)} %shard_map.54.staying, bf16[128,2048]{1,0:T(8,128)(2,1)S(1)} %collective-permute-done.16.refs_0_, bf16[128,2048]{1,0:T(8,128)(2,1)S(1)} %collective-permute-done.17.refs_1_), custom_call_target="tpu_custom_call" | custom-call | flops 1000 | bytes 1024 | tf_op jit(solution)/shard_map/pallas_call | solution.py:351
  (5 shorter events, 0.1 us)
Async XLA Ops:
  0.0 2.4 %copy-start = (bf16[2,512,1024]{2,1,0:T(8,128)(2,1)S(1)}, bf16[2,512,1024]{2,1,0:T(8,128)(2,1)}, u32[]{:S(2)}) copy-start(bf16[2,512,1024]{2,1,0:T(8,128)(2,1)} %param.7) | copy-start | bytes 6291460
  0.0 17.5 %collective-permute-start.1 = (bf16[1024,4096]{1,0:T(8,128)(2,1)}, bf16[1024,4096]{1,0:T(8,128)(2,1)}, u32[]{:S(2)}, u32[]{:S(2)}) collective-permute-start(bf16[1024,4096]{1,0:T(8,128)(2,1)} %refs_4_.1), channel_id=1, source_target_pairs={{0,1},{1,0},{2,3},{3,2},{4,5},{5,4},{6,7},{7,6},{8,9},{9,8},{10,11... | collective-permute-start | bytes 25165832 | tf_op jit(solution)/shard_map/ppermute | solution.py:410
  2.4 29.3 %copy-start.1 = (s32[4096]{0:T(1024)S(1)}, s32[4096]{0:T(1024)}, u32[]{:S(2)}) copy-start(s32[4096]{0:T(1024)} %param.9) | copy-start | bytes 49156
  2.6 14.9 %collective-permute-start = (bf16[2,512,256]{2,1,0:T(8,128)(2,1)S(1)}, bf16[2,512,256]{2,1,0:T(8,128)(2,1)}, u32[]{:S(2)}, u32[]{:S(2)}) collective-permute-start(bf16[2,512,256]{2,1,0:T(8,128)(2,1)S(1)} %get-tuple-element.71), channel_id=1, source_target_pairs={{0,4},{4,0},{8,12},{12,8},{16,20},{20,16},{24,28},{28,24},{1,5},{5... | collective-permute-start | bytes 1572872 | tf_op jit(solution)/shard_map/ppermute | solution.py:403
  4.1 40.6 %collective-permute-start.5 = (bf16[2,512,512]{2,1,0:T(8,128)(2,1)}, bf16[2,512,512]{2,1,0:T(8,128)(2,1)}, u32[]{:S(2)}, u32[]{:S(2)}) collective-permute-start(bf16[2,512,512]{2,1,0:T(8,128)(2,1)} %constant_dynamic-slice_fusion.4.kv_own), channel_id=1, source_target_pairs={{0,8},{4,12},{8,16},{12,20},{16,24},{20,28},{1,9},{5,13},{9,17},{1... | collective-permute-start | bytes 3145736 | tf_op jit(solution)/shard_map/ppermute | solution.py:400
  5.4 23.3 %collective-permute-start.4 = (bf16[2,512,256]{2,1,0:T(8,128)(2,1)S(1)}, bf16[2,512,256]{2,1,0:T(8,128)(2,1)}, u32[]{:S(2)}, u32[]{:S(2)}) collective-permute-start(bf16[2,512,256]{2,1,0:T(8,128)(2,1)S(1)} %get-tuple-element.70), channel_id=1, source_target_pairs={{0,4},{4,0},{8,12},{12,8},{16,20},{20,16},{24,28},{28,24},{1,5},{5... | collective-permute-start | bytes 1572872 | tf_op jit(solution)/shard_map/ppermute | solution.py:403
  17.5 21.8 %collective-permute-start.3 = (bf16[512,512]{1,0:T(8,128)(2,1)S(1)}, bf16[512,512]{1,0:T(8,128)(2,1)S(1)}, u32[]{:S(2)}, u32[]{:S(2)}) collective-permute-start(bf16[512,512]{1,0:T(8,128)(2,1)S(1)} %get-tuple-element.48), channel_id=1, source_target_pairs={{0,4},{4,0},{8,12},{12,8},{16,20},{20,16},{24,28},{28,24},{1,5},{5... | collective-permute-start | bytes 1572872 | tf_op jit(solution)/shard_map/ppermute | solution.py:413
  19.0 25.8 %collective-permute-start.2 = (bf16[2,512,256]{2,1,0:T(8,128)(2,1)}, bf16[2,512,256]{2,1,0:T(8,128)(2,1)}, u32[]{:S(2)}, u32[]{:S(2)}) collective-permute-start(bf16[2,512,256]{2,1,0:T(8,128)(2,1)} %collective-permute-done.kv_other_a), channel_id=1, source_target_pairs={{0,8},{4,12},{8,16},{12,20},{16,24},{20,28},{1,9},{5,13},{9,17},{1... | collective-permute-start | bytes 1572872 | tf_op jit(solution)/shard_map/ppermute | solution.py:414
  28.7 25.2 %collective-permute-start.6 = (bf16[2,512,256]{2,1,0:T(8,128)(2,1)}, bf16[2,512,256]{2,1,0:T(8,128)(2,1)}, u32[]{:S(2)}, u32[]{:S(2)}) collective-permute-start(bf16[2,512,256]{2,1,0:T(8,128)(2,1)} %collective-permute-done.4.kv_other_b), channel_id=1, source_target_pairs={{0,8},{4,12},{8,16},{12,20},{16,24},{20,28},{1,9},{5,13},{9,17},{1... | collective-permute-start | bytes 1572872 | tf_op jit(solution)/shard_map/ppermute | solution.py:414
  47.4 10.0 %collective-permute-start.9 = (bf16[128,256]{1,0:T(8,128)(2,1)S(1)}, bf16[128,256]{1,0:T(8,128)(2,1)S(1)}, u32[]{:S(2)}, u32[]{:S(2)}) collective-permute-start(bf16[128,256]{1,0:T(8,128)(2,1)S(1)} %get-tuple-element.60), channel_id=1, source_target_pairs={{0,1},{1,0},{2,3},{3,2},{4,5},{5,4},{6,7},{7,6},{8,9},{9,8},{10,11... | collective-permute-start | bytes 196616 | tf_op jit(solution)/shard_map/ppermute | solution.py:478
  47.5 11.2 %collective-permute-start.11 = (bf16[128,256]{1,0:T(8,128)(2,1)S(1)}, bf16[128,256]{1,0:T(8,128)(2,1)S(1)}, u32[]{:S(2)}, u32[]{:S(2)}) collective-permute-start(bf16[128,256]{1,0:T(8,128)(2,1)S(1)} %get-tuple-element.63), channel_id=1, source_target_pairs={{0,4},{4,0},{8,12},{12,8},{16,20},{20,16},{24,28},{28,24},{1,5},{5... | collective-permute-start | bytes 196616 | tf_op jit(solution)/shard_map/ppermute | solution.py:479
  49.1 9.6 %collective-permute-start.12 = (bf16[128,256]{1,0:T(8,128)(2,1)S(1)}, bf16[128,256]{1,0:T(8,128)(2,1)S(1)}, u32[]{:S(2)}, u32[]{:S(2)}) collective-permute-start(bf16[128,256]{1,0:T(8,128)(2,1)S(1)} %get-tuple-element.64), channel_id=1, source_target_pairs={{0,5},{1,4},{2,7},{3,6},{4,1},{5,0},{6,3},{7,2},{8,13},{9,12},{10,... | collective-permute-start | bytes 196616 | tf_op jit(solution)/shard_map/ppermute | solution.py:480
  49.4 9.4 %slice-start = ((s8[8388608]{0:T(1024)(128)(4,1)}), s8[4194304]{0:T(1024)(128)(4,1)S(1)}, s32[]{:S(2)}) async-start(s8[8388608]{0:T(1024)(128)(4,1)} %bitcast.6), calls=%async_computation.1 | async-start | bytes 8388608
  50.5 8.2 %slice-start.1 = ((s8[8388608]{0:T(1024)(128)(4,1)}), s8[4194304]{0:T(1024)(128)(4,1)S(1)}, s32[]{:S(2)}) async-start(s8[8388608]{0:T(1024)(128)(4,1)} %bitcast.6), calls=%async_computation.2 | async-start | bytes 8388608
  56.8 2.0 %collective-permute-start.10 = (bf16[128,256]{1,0:T(8,128)(2,1)S(1)}, bf16[128,256]{1,0:T(8,128)(2,1)S(1)}, u32[]{:S(2)}, u32[]{:S(2)}) collective-permute-start(bf16[128,256]{1,0:T(8,128)(2,1)S(1)} %get-tuple-element.62), channel_id=1, source_target_pairs={{0,1},{1,0},{2,3},{3,2},{4,5},{5,4},{6,7},{7,6},{8,9},{9,8},{10,11... | collective-permute-start | bytes 196616 | tf_op jit(solution)/shard_map/ppermute | solution.py:478
  56.9 7.2 %collective-permute-start.7 = (bf16[128,256]{1,0:T(8,128)(2,1)S(1)}, bf16[128,256]{1,0:T(8,128)(2,1)S(1)}, u32[]{:S(2)}, u32[]{:S(2)}) collective-permute-start(bf16[128,256]{1,0:T(8,128)(2,1)S(1)} %get-tuple-element.56), channel_id=1, source_target_pairs={{0,4},{4,0},{8,12},{12,8},{16,20},{20,16},{24,28},{28,24},{1,5},{5... | collective-permute-start | bytes 196616 | tf_op jit(solution)/shard_map/ppermute | solution.py:479
  57.5 6.6 %collective-permute-start.8 = (bf16[128,256]{1,0:T(8,128)(2,1)S(1)}, bf16[128,256]{1,0:T(8,128)(2,1)S(1)}, u32[]{:S(2)}, u32[]{:S(2)}) collective-permute-start(bf16[128,256]{1,0:T(8,128)(2,1)S(1)} %get-tuple-element.57), channel_id=1, source_target_pairs={{0,5},{1,4},{2,7},{3,6},{4,1},{5,0},{6,3},{7,2},{8,13},{9,12},{10,... | collective-permute-start | bytes 196616 | tf_op jit(solution)/shard_map/ppermute | solution.py:480
  66.6 24.1 %collective-permute-start.16 = (bf16[128,2048]{1,0:T(8,128)(2,1)S(1)}, bf16[128,2048]{1,0:T(8,128)(2,1)S(1)}, u32[]{:S(2)}, u32[]{:S(2)}) collective-permute-start(bf16[128,2048]{1,0:T(8,128)(2,1)S(1)} %shard_map.51), channel_id=1, source_target_pairs={{0,2},{1,3},{2,0},{3,1},{4,6},{5,7},{6,4},{7,5},{8,10},{9,11},{10,... | collective-permute-start | bytes 1572872 | tf_op jit(solution)/shard_map/ppermute | solution.py:510
  71.5 21.1 %collective-permute-start.17 = (bf16[128,2048]{1,0:T(8,128)(2,1)S(1)}, bf16[128,2048]{1,0:T(8,128)(2,1)S(1)}, u32[]{:S(2)}, u32[]{:S(2)}) collective-permute-start(bf16[128,2048]{1,0:T(8,128)(2,1)S(1)} %shard_map.52), channel_id=1, source_target_pairs={{0,2},{1,3},{2,0},{3,1},{4,6},{5,7},{6,4},{7,5},{8,10},{9,11},{10,... | collective-permute-start | bytes 1572872 | tf_op jit(solution)/shard_map/ppermute | solution.py:510
  76.1 1.9 %collective-permute-start.13 = (bf16[128,512]{1,0:T(8,128)(2,1)S(1)}, bf16[128,512]{1,0:T(8,128)(2,1)S(1)}, u32[]{:S(2)}, u32[]{:S(2)}) collective-permute-start(bf16[128,512]{1,0:T(8,128)(2,1)S(1)} %get-tuple-element.67), channel_id=1, source_target_pairs={{0,1},{1,0},{2,3},{3,2},{4,5},{5,4},{6,7},{7,6},{8,9},{9,8},{10,11... | collective-permute-start | bytes 393224 | tf_op jit(solution)/shard_map/ppermute | solution.py:478
  76.2 6.3 %collective-permute-start.14 = (bf16[128,512]{1,0:T(8,128)(2,1)S(1)}, bf16[128,512]{1,0:T(8,128)(2,1)S(1)}, u32[]{:S(2)}, u32[]{:S(2)}) collective-permute-start(bf16[128,512]{1,0:T(8,128)(2,1)S(1)} %get-tuple-element.68), channel_id=1, source_target_pairs={{0,4},{4,0},{8,12},{12,8},{16,20},{20,16},{24,28},{28,24},{1,5},{5... | collective-permute-start | bytes 393224 | tf_op jit(solution)/shard_map/ppermute | solution.py:479
  76.8 7.7 %collective-permute-start.15 = (bf16[128,512]{1,0:T(8,128)(2,1)S(1)}, bf16[128,512]{1,0:T(8,128)(2,1)S(1)}, u32[]{:S(2)}, u32[]{:S(2)}) collective-permute-start(bf16[128,512]{1,0:T(8,128)(2,1)S(1)} %get-tuple-element.69), channel_id=1, source_target_pairs={{0,5},{1,4},{2,7},{3,6},{4,1},{5,0},{6,3},{7,2},{8,13},{9,12},{10,... | collective-permute-start | bytes 393224 | tf_op jit(solution)/shard_map/ppermute | solution.py:480

commit v5 on v4

--- a/solution.py
+++ b/solution.py
@@ -483,7 +483,8 @@
     def project(pieces, places, begun, kind, part, parts):
         columns = w_out.shape[1] // parts
         width = pieces[0].shape[1]
-        chunk, ring = 512, min(8, 8192 // (width * len(pieces)))
+        chunk = 512 if begun is None else 1024
+        ring = max(2, min(8, (4 << 20) // (width * len(pieces) * chunk)))
         more = [] if begun is None else [begun]
         (out,) = call(
             functools.partial(project_kernel, places, half, ring, part, chunk, begun is not None),

time: 95 us -> 94.4 us (level)
    ppermute x2, waiting for transfers between devices: 3.39 us -> 2.07 us  [per_device(): crossed = [lax.ppermute(part, 'ctx', hop) for part in kv_other]]
where the time goes in v5:
time: 94.4 us; the launch traced here: 93.4 us
  Pallas kernels  34.9 us (37%)
  waiting for transfers between devices  32.5 us (34%)
  starting transfers between devices  15.5 us (16%)
  local copies, waits for them, and re-layouts  8.78 us (9%)
    pallas_call x9, Pallas kernels, call(): pl.pallas_call(kernel, in_specs=specs, out_specs=[IN_VMEM] * len(outs), o...  33.7 us
    ppermute x2, waiting for transfers between devices, per_device(): lax.ppermute(lax.dynamic_slice_in_dim(keys_values, (1 - side) * half + gr...  18.6 us
    slice x3, local copies, waits for them, and re-layouts, per_device(): tails = [kv_own[:, last:]] + [part[:, last:] for part in kv_other]  4.82 us
    ppermute x3, waiting for transfers between devices, exchanged(): lax.ppermute(pieces[2], 'ctx', swap)  4.5 us
    dynamic_slice x2, local copies, waits for them, and re-layouts, mine(): return lax.dynamic_slice_in_dim(array, side * half, half, axis)  3.68 us
    ppermute x3, starting transfers between devices, exchanged(): lax.ppermute(pieces[2], 'ctx', swap)  3.11 us
    ppermute x1, waiting for transfers between devices, per_device(): q_other = lax.ppermute(q_send, 'ctx', swap)  2.84 us
    ppermute x2, starting transfers between devices, per_device(): crossed = [lax.ppermute(part, 'ctx', hop) for part in kv_other]  2.56 us
  transfers between devices with their start and end apart: 18, of which 7 were waited for; matrix products, arithmetic and copies ran while one was open for 10% of the time, Pallas kernels for 33%

profile of v5, /device:TPU:24, one launch (start us, length us, event | category | flops | bytes accessed | tf_op | source)
XLA Modules:
  0.0 93.4 jit_solution(13572030582893573139)
XLA Ops:
  0.0 0.0 copy-start
  0.0 0.0 collective-permute-start.1
  0.0 2.4 %constant_dynamic-slice_fusion.4.kv_own = bf16[2,512,512]{2,1,0:T(8,128)(2,1)} fusion(bf16[2,512,1024]{2,1,0:T(8,128)(2,1)} %param.7, s32[]{:T(128)S(6)} %select_n.27), kind=kLoop, calls=%fused_computation.10 | loop fusion | bytes 2097156 | tf_op jit(solution)/shard_map/dynamic_slice | solution.py:393
  2.4 0.0 copy-done
  2.4 0.0 copy-start.1
  2.4 0.1 constant_dynamic-slice_fusion
  2.6 1.6 %collective-permute-start = (bf16[2,512,256]{2,1,0:T(8,128)(2,1)S(1)}, bf16[2,512,256]{2,1,0:T(8,128)(2,1)}, u32[]{:S(2)}, u32[]{:S(2)}) collective-permute-start(bf16[2,512,256]{2,1,0:T(8,128)(2,1)S(1)} %get-tuple-element.71), channel_id=1, source_target_pairs={{0,4},{4,0},{8,12},{12,8},{16,20},{20,16},{24,28},{28,24},{1,5},{5... | collective-permute-start | bytes 1572872 | tf_op jit(solution)/shard_map/ppermute | solution.py:403
  4.1 1.3 %collective-permute-start.5 = (bf16[2,512,512]{2,1,0:T(8,128)(2,1)}, bf16[2,512,512]{2,1,0:T(8,128)(2,1)}, u32[]{:S(2)}, u32[]{:S(2)}) collective-permute-start(bf16[2,512,512]{2,1,0:T(8,128)(2,1)} %constant_dynamic-slice_fusion.4.kv_own), channel_id=1, source_target_pairs={{0,8},{4,12},{8,16},{12,20},{16,24},{20,28},{1,9},{5,13},{9,17},{1... | collective-permute-start | bytes 3145736 | tf_op jit(solution)/shard_map/ppermute | solution.py:400
  5.4 0.6 collective-permute-start.4
  6.0 1.3 %constant_dynamic-slice_fusion.1 = (bf16[512,512]{1,0:T(8,128)(2,1)S(1)}, bf16[512,512]{1,0:T(8,128)(2,1)S(1)}) fusion(bf16[512,1024]{1,0:T(8,128)(2,1)} %param.6, s32[]{:T(128)S(6)} %select_n.27, s32[]{:T(128)S(6)} %select_n.28), kind=kLoop, calls=%fused_computation.7 | loop fusion | bytes 2097160 | tf_op jit(solution)/shard_map/dynamic_slice | solution.py:393
  7.3 10.2 %collective-permute-done.kv_other_a = bf16[2,512,256]{2,1,0:T(8,128)(2,1)} collective-permute-done((bf16[2,512,256]{2,1,0:T(8,128)(2,1)S(1)}, bf16[2,512,256]{2,1,0:T(8,128)(2,1)}, u32[]{:S(2)}, u32[]{:S(2)}) %collective-permute-start) | collective-permute-done | bytes 524320 | tf_op jit(solution)/shard_map/ppermute | solution.py:403
  17.5 0.0 collective-permute-done.1.refs_7_.refs_3_.refs_5_
  17.5 1.5 %collective-permute-start.3 = (bf16[512,512]{1,0:T(8,128)(2,1)S(1)}, bf16[512,512]{1,0:T(8,128)(2,1)S(1)}, u32[]{:S(2)}, u32[]{:S(2)}) collective-permute-start(bf16[512,512]{1,0:T(8,128)(2,1)S(1)} %get-tuple-element.48), channel_id=1, source_target_pairs={{0,4},{4,0},{8,12},{12,8},{16,20},{20,16},{24,28},{28,24},{1,5},{5... | collective-permute-start | bytes 1572872 | tf_op jit(solution)/shard_map/ppermute | solution.py:413
  19.0 1.3 %collective-permute-start.2 = (bf16[2,512,256]{2,1,0:T(8,128)(2,1)}, bf16[2,512,256]{2,1,0:T(8,128)(2,1)}, u32[]{:S(2)}, u32[]{:S(2)}) collective-permute-start(bf16[2,512,256]{2,1,0:T(8,128)(2,1)} %collective-permute-done.kv_other_a), channel_id=1, source_target_pairs={{0,8},{4,12},{8,16},{12,20},{16,24},{20,28},{1,9},{5,13},{9,17},{1... | collective-permute-start | bytes 1572872 | tf_op jit(solution)/shard_map/ppermute | solution.py:414
  20.3 8.5 %collective-permute-done.4.kv_other_b = bf16[2,512,256]{2,1,0:T(8,128)(2,1)} collective-permute-done((bf16[2,512,256]{2,1,0:T(8,128)(2,1)S(1)}, bf16[2,512,256]{2,1,0:T(8,128)(2,1)}, u32[]{:S(2)}, u32[]{:S(2)}) %collective-permute-start.4) | collective-permute-done | bytes 524320 | tf_op jit(solution)/shard_map/ppermute | solution.py:403
  28.7 1.3 %collective-permute-start.6 = (bf16[2,512,256]{2,1,0:T(8,128)(2,1)}, bf16[2,512,256]{2,1,0:T(8,128)(2,1)}, u32[]{:S(2)}, u32[]{:S(2)}) collective-permute-start(bf16[2,512,256]{2,1,0:T(8,128)(2,1)} %collective-permute-done.4.kv_other_b), channel_id=1, source_target_pairs={{0,8},{4,12},{8,16},{12,20},{16,24},{20,28},{1,9},{5,13},{9,17},{1... | collective-permute-start | bytes 1572872 | tf_op jit(solution)/shard_map/ppermute | solution.py:414
  30.0 1.7 %slice.18 = bf16[2,128,512]{2,1,0:T(8,128)(2,1)} slice(bf16[2,512,512]{2,1,0:T(8,128)(2,1)} %constant_dynamic-slice_fusion.4.kv_own), slice={[0:2], [384:512], [0:512]} | slice | bytes 524288 | tf_op jit(solution)/shard_map/slice | solution.py:444
  31.7 0.0 copy-done.1
  31.7 0.1 pad_dynamic-slice_fusion.docs
  31.8 0.8 compare_reduce_fusion
  33.2 0.1 pad_add_fusion.ids
  33.3 1.6 %slice.24 = bf16[2,128,256]{2,1,0:T(8,128)(2,1)} slice(bf16[2,512,256]{2,1,0:T(8,128)(2,1)} %collective-permute-done.4.kv_other_b), slice={[0:2], [384:512], [0:256]} | slice | bytes 262144 | tf_op jit(solution)/shard_map/slice | solution.py:444
  34.9 1.6 %slice.19 = bf16[2,128,256]{2,1,0:T(8,128)(2,1)} slice(bf16[2,512,256]{2,1,0:T(8,128)(2,1)} %collective-permute-done.kv_other_a), slice={[0:2], [384:512], [0:256]} | slice | bytes 262144 | tf_op jit(solution)/shard_map/slice | solution.py:444
  36.4 2.8 %collective-permute-done.3.q_other = bf16[512,512]{1,0:T(8,128)(2,1)S(1)} collective-permute-done((bf16[512,512]{1,0:T(8,128)(2,1)S(1)}, bf16[512,512]{1,0:T(8,128)(2,1)S(1)}, u32[]{:S(2)}, u32[]{:S(2)}) %collective-permute-start.3) | collective-permute-done | bytes 524320 | tf_op jit(solution)/shard_map/ppermute | solution.py:413
  39.3 6.4 %shard_map.47 = (f32[512,1024]{1,0:T(8,128)S(1)}, f32[8,1024]{1,0:T(8,128)S(1)}) custom-call(s32[2]{0:T(128)S(1)} %pad_add_fusion.ids, s32[2304]{0:T(1024)S(1)} %pad_dynamic-slice_fusion.docs, s32[1,2304]{1,0:T(1,128)S(1)} %reshape.7.docs_row, bf16[512,512]{1,0:T(8,128)(2,1)S(1)} %get-tuple-element.72.q_own, ...), custom_call_target="tpu_custom_call" | custom-call | flops 7000 | bytes 1024 | tf_op jit(solution)/shard_map/pallas_call | solution.py:351
  45.8 0.0 collective-permute-done.5.same
  45.8 0.0 collective-permute-done.2.refs_0_.rest_0_
  45.8 3.0 %shard_map.49 = (bf16[128,256]{1,0:T(8,128)(2,1)S(1)}, bf16[128,256]{1,0:T(8,128)(2,1)S(1)}, bf16[128,256]{1,0:T(8,128)(2,1)S(1)}, bf16[128,256]{1,0:T(8,128)(2,1)S(1)}) custom-call(s32[2]{0:T(128)S(1)} %pad_add_fusion.ids, s32[2304]{0:T(1024)S(1)} %pad_dynamic-slice_fusion.docs, s32[1,2304]{1,0:T(1,128)S(1)} %reshape.7.docs_row, ...), custom_call_target="tpu_custom_call" | custom-call | flops 1000 | bytes 1024 | tf_op jit(solution)/shard_map/pallas_call | solution.py:351
  48.8 0.1 collective-permute-start.9
  48.8 1.6 %collective-permute-start.11 = (bf16[128,256]{1,0:T(8,128)(2,1)S(1)}, bf16[128,256]{1,0:T(8,128)(2,1)S(1)}, u32[]{:S(2)}, u32[]{:S(2)}) collective-permute-start(bf16[128,256]{1,0:T(8,128)(2,1)S(1)} %get-tuple-element.63), channel_id=1, source_target_pairs={{0,4},{4,0},{8,12},{12,8},{16,20},{20,16},{24,28},{28,24},{1,5},{5... | collective-permute-start | bytes 196616 | tf_op jit(solution)/shard_map/ppermute | solution.py:479
  50.4 0.3 collective-permute-start.12
  50.7 0.0 slice-start
  50.7 1.1 %shard_map.46.ids = s32[2]{0:T(128)S(1)} custom-call(s32[2]{0:T(128)S(1)} %pad_add_fusion.ids, bf16[2,512,256]{2,1,0:T(8,128)(2,1)} %collective-permute-done.2.refs_0_.rest_0_), custom_call_target="tpu_custom_call" | custom-call | flops 550000000 | bytes 1024 | tf_op jit(solution)/shard_map/pallas_call | solution.py:338
  51.9 0.0 slice-start.1
  51.9 2.1 %collective-permute-done.6.rest_0_.rest_1_ = bf16[2,512,256]{2,1,0:T(8,128)(2,1)} collective-permute-done((bf16[2,512,256]{2,1,0:T(8,128)(2,1)}, bf16[2,512,256]{2,1,0:T(8,128)(2,1)}, u32[]{:S(2)}, u32[]{:S(2)}) %collective-permute-start.6) | collective-permute-done | bytes 524320 | tf_op jit(solution)/shard_map/ppermute | solution.py:414
  53.9 3.1 %shard_map.48 = (bf16[128,256]{1,0:T(8,128)(2,1)S(1)}, bf16[128,256]{1,0:T(8,128)(2,1)S(1)}, bf16[128,256]{1,0:T(8,128)(2,1)S(1)}, bf16[128,256]{1,0:T(8,128)(2,1)S(1)}) custom-call(s32[2]{0:T(128)S(1)} %shard_map.46.ids, s32[2304]{0:T(1024)S(1)} %pad_dynamic-slice_fusion.docs, s32[1,2304]{1,0:T(1,128)S(1)} %reshape.7.docs_row, ...), custom_call_target="tpu_custom_call" | custom-call | flops 5000000000 | bytes 1024 | tf_op jit(solution)/shard_map/pallas_call | solution.py:351
  57.1 0.1 collective-permute-start.10
  57.1 0.8 collective-permute-start.7
  57.9 0.0 collective-permute-done.9.refs_1_
  57.9 1.1 %collective-permute-start.8 = (bf16[128,256]{1,0:T(8,128)(2,1)S(1)}, bf16[128,256]{1,0:T(8,128)(2,1)S(1)}, u32[]{:S(2)}, u32[]{:S(2)}) collective-permute-start(bf16[128,256]{1,0:T(8,128)(2,1)S(1)} %get-tuple-element.57), channel_id=1, source_target_pairs={{0,5},{1,4},{2,7},{3,6},{4,1},{5,0},{6,3},{7,2},{8,13},{9,12},{10,... | collective-permute-start | bytes 196616 | tf_op jit(solution)/shard_map/ppermute | solution.py:480
  59.0 0.0 collective-permute-done.11.refs_4_
  59.0 0.0 collective-permute-done.12.refs_5_
  59.0 0.0 collective-permute-done.10.refs_3_
  59.0 0.0 slice-done
  59.0 0.0 slice-done.1
  59.0 5.2 %shard_map.50.refs_4_ = f32[128,4096]{1,0:T(8,128)S(1)} custom-call(s32[2]{0:T(128)S(1)} %pad_add_fusion.ids, bf16[128,256]{1,0:T(8,128)(2,1)S(1)} %get-tuple-element.59.refs_0_, bf16[128,256]{1,0:T(8,128)(2,1)S(1)} %collective-permute-done.9.refs_1_, bf16[128,256]{1,0:T(8,128)(2,1)S(1)} %get-tuple-element.61.refs_2_, ...), custom_call_target="tpu_custom_call" | custom-call | flops 1000 | bytes 1024 | tf_op jit(solution)/shard_map/pallas_call | solution.py:351
  64.3 0.0 collective-permute-done.7.refs_0_
  64.3 0.0 collective-permute-done.8.refs_1_
  64.3 2.4 %shard_map.51 = bf16[128,2048]{1,0:T(8,128)(2,1)S(1)} custom-call(s32[2]{0:T(128)S(1)} %pad_add_fusion.ids, bf16[128,256]{1,0:T(8,128)(2,1)S(1)} %collective-permute-done.7.refs_0_, bf16[128,256]{1,0:T(8,128)(2,1)S(1)} %collective-permute-done.8.refs_1_, bf16[1024,4096]{1,0:T(8,128)(2,1)S(1)} %bitcast.7, ...), custom_call_target="tpu_custom_call" | custom-call | flops 1000 | bytes 1024 | tf_op jit(solution)/shard_map/pallas_call | solution.py:351
  66.8 1.6 %collective-permute-start.16 = (bf16[128,2048]{1,0:T(8,128)(2,1)S(1)}, bf16[128,2048]{1,0:T(8,128)(2,1)S(1)}, u32[]{:S(2)}, u32[]{:S(2)}) collective-permute-start(bf16[128,2048]{1,0:T(8,128)(2,1)S(1)} %shard_map.51), channel_id=1, source_target_pairs={{0,2},{1,3},{2,0},{3,1},{4,6},{5,7},{6,4},{7,5},{8,10},{9,11},{10,... | collective-permute-start | bytes 1572872 | tf_op jit(solution)/shard_map/ppermute | solution.py:511
  68.4 2.4 %shard_map.52 = bf16[128,2048]{1,0:T(8,128)(2,1)S(1)} custom-call(s32[2]{0:T(128)S(1)} %pad_add_fusion.ids, bf16[128,256]{1,0:T(8,128)(2,1)S(1)} %collective-permute-done.7.refs_0_, bf16[128,256]{1,0:T(8,128)(2,1)S(1)} %collective-permute-done.8.refs_1_, bf16[1024,4096]{1,0:T(8,128)(2,1)S(1)} %bitcast.7, ...), custom_call_target="tpu_custom_call" | custom-call | flops 1000 | bytes 1024 | tf_op jit(solution)/shard_map/pallas_call | solution.py:351
  70.8 0.6 collective-permute-start.17
  71.4 3.7 %shard_map.53 = (bf16[128,512]{1,0:T(8,128)(2,1)S(1)}, bf16[128,512]{1,0:T(8,128)(2,1)S(1)}, bf16[128,512]{1,0:T(8,128)(2,1)S(1)}, bf16[128,512]{1,0:T(8,128)(2,1)S(1)}) custom-call(s32[2]{0:T(128)S(1)} %shard_map.46.ids, s32[2304]{0:T(1024)S(1)} %pad_dynamic-slice_fusion.docs, s32[1,2304]{1,0:T(1,128)S(1)} %reshape.7.docs_row, ...), custom_call_target="tpu_custom_call" | custom-call | flops 1000 | bytes 1024 | tf_op jit(solution)/shard_map/pallas_call | solution.py:351
  75.1 0.1 collective-permute-start.13
  75.2 0.8 collective-permute-start.14
  76.0 1.1 %collective-permute-start.15 = (bf16[128,512]{1,0:T(8,128)(2,1)S(1)}, bf16[128,512]{1,0:T(8,128)(2,1)S(1)}, u32[]{:S(2)}, u32[]{:S(2)}) collective-permute-start(bf16[128,512]{1,0:T(8,128)(2,1)S(1)} %get-tuple-element.69), channel_id=1, source_target_pairs={{0,5},{1,4},{2,7},{3,6},{4,1},{5,0},{6,3},{7,2},{8,13},{9,12},{10,... | collective-permute-start | bytes 393224 | tf_op jit(solution)/shard_map/ppermute | solution.py:480
  77.0 0.0 collective-permute-done.13.refs_1_
  77.1 4.5 %collective-permute-done.14.refs_2_ = bf16[128,512]{1,0:T(8,128)(2,1)S(1)} collective-permute-done((bf16[128,512]{1,0:T(8,128)(2,1)S(1)}, bf16[128,512]{1,0:T(8,128)(2,1)S(1)}, u32[]{:S(2)}, u32[]{:S(2)}) %collective-permute-start.14) | collective-permute-done | bytes 131104 | tf_op jit(solution)/shard_map/ppermute | solution.py:479
  81.5 1.9 %collective-permute-done.15.refs_3_ = bf16[128,512]{1,0:T(8,128)(2,1)S(1)} collective-permute-done((bf16[128,512]{1,0:T(8,128)(2,1)S(1)}, bf16[128,512]{1,0:T(8,128)(2,1)S(1)}, u32[]{:S(2)}, u32[]{:S(2)}) %collective-permute-start.15) | collective-permute-done | bytes 131104 | tf_op jit(solution)/shard_map/ppermute | solution.py:480
  83.5 6.2 %shard_map.54.staying = f32[128,4096]{1,0:T(8,128)S(1)} custom-call(s32[2]{0:T(128)S(1)} %pad_add_fusion.ids, bf16[128,512]{1,0:T(8,128)(2,1)S(1)} %get-tuple-element.66.refs_0_, bf16[128,512]{1,0:T(8,128)(2,1)S(1)} %collective-permute-done.13.refs_1_, bf16[128,512]{1,0:T(8,128)(2,1)S(1)} %collective-permute-done.14.refs_2_, ...), custom_call_target="tpu_custom_call" | custom-call | flops 1000 | bytes 1024 | tf_op jit(solution)/shard_map/pallas_call | solution.py:351
  89.7 0.0 collective-permute-done.16.refs_0_
  89.7 2.5 %collective-permute-done.17.refs_1_ = bf16[128,2048]{1,0:T(8,128)(2,1)S(1)} collective-permute-done((bf16[128,2048]{1,0:T(8,128)(2,1)S(1)}, bf16[128,2048]{1,0:T(8,128)(2,1)S(1)}, u32[]{:S(2)}, u32[]{:S(2)}) %collective-permute-start.17) | collective-permute-done | bytes 524320 | tf_op jit(solution)/shard_map/ppermute | solution.py:511
  92.2 1.1 %shard_map.55 = bf16[128,4096]{1,0:T(8,128)(2,1)} custom-call(f32[128,4096]{1,0:T(8,128)S(1)} %shard_map.54.staying, bf16[128,2048]{1,0:T(8,128)(2,1)S(1)} %collective-permute-done.16.refs_0_, bf16[128,2048]{1,0:T(8,128)(2,1)S(1)} %collective-permute-done.17.refs_1_), custom_call_target="tpu_custom_call" | custom-call | flops 1000 | bytes 1024 | tf_op jit(solution)/shard_map/pallas_call | solution.py:351
  (5 shorter events, 0.1 us)
Async XLA Ops:
  0.0 2.4 %copy-start = (bf16[2,512,1024]{2,1,0:T(8,128)(2,1)S(1)}, bf16[2,512,1024]{2,1,0:T(8,128)(2,1)}, u32[]{:S(2)}) copy-start(bf16[2,512,1024]{2,1,0:T(8,128)(2,1)} %param.7) | copy-start | bytes 6291460
  0.0 17.5 %collective-permute-start.1 = (bf16[1024,4096]{1,0:T(8,128)(2,1)}, bf16[1024,4096]{1,0:T(8,128)(2,1)}, u32[]{:S(2)}, u32[]{:S(2)}) collective-permute-start(bf16[1024,4096]{1,0:T(8,128)(2,1)} %refs_4_.1), channel_id=1, source_target_pairs={{0,1},{1,0},{2,3},{3,2},{4,5},{5,4},{6,7},{7,6},{8,9},{9,8},{10,11... | collective-permute-start | bytes 25165832 | tf_op jit(solution)/shard_map/ppermute | solution.py:410
  2.4 29.3 %copy-start.1 = (s32[4096]{0:T(1024)S(1)}, s32[4096]{0:T(1024)}, u32[]{:S(2)}) copy-start(s32[4096]{0:T(1024)} %param.9) | copy-start | bytes 49156
  2.6 14.9 %collective-permute-start = (bf16[2,512,256]{2,1,0:T(8,128)(2,1)S(1)}, bf16[2,512,256]{2,1,0:T(8,128)(2,1)}, u32[]{:S(2)}, u32[]{:S(2)}) collective-permute-start(bf16[2,512,256]{2,1,0:T(8,128)(2,1)S(1)} %get-tuple-element.71), channel_id=1, source_target_pairs={{0,4},{4,0},{8,12},{12,8},{16,20},{20,16},{24,28},{28,24},{1,5},{5... | collective-permute-start | bytes 1572872 | tf_op jit(solution)/shard_map/ppermute | solution.py:403
  4.1 41.7 %collective-permute-start.5 = (bf16[2,512,512]{2,1,0:T(8,128)(2,1)}, bf16[2,512,512]{2,1,0:T(8,128)(2,1)}, u32[]{:S(2)}, u32[]{:S(2)}) collective-permute-start(bf16[2,512,512]{2,1,0:T(8,128)(2,1)} %constant_dynamic-slice_fusion.4.kv_own), channel_id=1, source_target_pairs={{0,8},{4,12},{8,16},{12,20},{16,24},{20,28},{1,9},{5,13},{9,17},{1... | collective-permute-start | bytes 3145736 | tf_op jit(solution)/shard_map/ppermute | solution.py:400
  5.4 23.3 %collective-permute-start.4 = (bf16[2,512,256]{2,1,0:T(8,128)(2,1)S(1)}, bf16[2,512,256]{2,1,0:T(8,128)(2,1)}, u32[]{:S(2)}, u32[]{:S(2)}) collective-permute-start(bf16[2,512,256]{2,1,0:T(8,128)(2,1)S(1)} %get-tuple-element.70), channel_id=1, source_target_pairs={{0,4},{4,0},{8,12},{12,8},{16,20},{20,16},{24,28},{28,24},{1,5},{5... | collective-permute-start | bytes 1572872 | tf_op jit(solution)/shard_map/ppermute | solution.py:403
  17.5 21.8 %collective-permute-start.3 = (bf16[512,512]{1,0:T(8,128)(2,1)S(1)}, bf16[512,512]{1,0:T(8,128)(2,1)S(1)}, u32[]{:S(2)}, u32[]{:S(2)}) collective-permute-start(bf16[512,512]{1,0:T(8,128)(2,1)S(1)} %get-tuple-element.48), channel_id=1, source_target_pairs={{0,4},{4,0},{8,12},{12,8},{16,20},{20,16},{24,28},{28,24},{1,5},{5... | collective-permute-start | bytes 1572872 | tf_op jit(solution)/shard_map/ppermute | solution.py:413
  19.0 26.8 %collective-permute-start.2 = (bf16[2,512,256]{2,1,0:T(8,128)(2,1)}, bf16[2,512,256]{2,1,0:T(8,128)(2,1)}, u32[]{:S(2)}, u32[]{:S(2)}) collective-permute-start(bf16[2,512,256]{2,1,0:T(8,128)(2,1)} %collective-permute-done.kv_other_a), channel_id=1, source_target_pairs={{0,8},{4,12},{8,16},{12,20},{16,24},{20,28},{1,9},{5,13},{9,17},{1... | collective-permute-start | bytes 1572872 | tf_op jit(solution)/shard_map/ppermute | solution.py:414
  28.7 25.2 %collective-permute-start.6 = (bf16[2,512,256]{2,1,0:T(8,128)(2,1)}, bf16[2,512,256]{2,1,0:T(8,128)(2,1)}, u32[]{:S(2)}, u32[]{:S(2)}) collective-permute-start(bf16[2,512,256]{2,1,0:T(8,128)(2,1)} %collective-permute-done.4.kv_other_b), channel_id=1, source_target_pairs={{0,8},{4,12},{8,16},{12,20},{16,24},{20,28},{1,9},{5,13},{9,17},{1... | collective-permute-start | bytes 1572872 | tf_op jit(solution)/shard_map/ppermute | solution.py:414
  48.8 9.2 %collective-permute-start.9 = (bf16[128,256]{1,0:T(8,128)(2,1)S(1)}, bf16[128,256]{1,0:T(8,128)(2,1)S(1)}, u32[]{:S(2)}, u32[]{:S(2)}) collective-permute-start(bf16[128,256]{1,0:T(8,128)(2,1)S(1)} %get-tuple-element.60), channel_id=1, source_target_pairs={{0,1},{1,0},{2,3},{3,2},{4,5},{5,4},{6,7},{7,6},{8,9},{9,8},{10,11... | collective-permute-start | bytes 196616 | tf_op jit(solution)/shard_map/ppermute | solution.py:478
  48.8 10.2 %collective-permute-start.11 = (bf16[128,256]{1,0:T(8,128)(2,1)S(1)}, bf16[128,256]{1,0:T(8,128)(2,1)S(1)}, u32[]{:S(2)}, u32[]{:S(2)}) collective-permute-start(bf16[128,256]{1,0:T(8,128)(2,1)S(1)} %get-tuple-element.63), channel_id=1, source_target_pairs={{0,4},{4,0},{8,12},{12,8},{16,20},{20,16},{24,28},{28,24},{1,5},{5... | collective-permute-start | bytes 196616 | tf_op jit(solution)/shard_map/ppermute | solution.py:479
  50.4 8.6 %collective-permute-start.12 = (bf16[128,256]{1,0:T(8,128)(2,1)S(1)}, bf16[128,256]{1,0:T(8,128)(2,1)S(1)}, u32[]{:S(2)}, u32[]{:S(2)}) collective-permute-start(bf16[128,256]{1,0:T(8,128)(2,1)S(1)} %get-tuple-element.64), channel_id=1, source_target_pairs={{0,5},{1,4},{2,7},{3,6},{4,1},{5,0},{6,3},{7,2},{8,13},{9,12},{10,... | collective-permute-start | bytes 196616 | tf_op jit(solution)/shard_map/ppermute | solution.py:480
  50.7 8.3 %slice-start = ((s8[8388608]{0:T(1024)(128)(4,1)}), s8[4194304]{0:T(1024)(128)(4,1)S(1)}, s32[]{:S(2)}) async-start(s8[8388608]{0:T(1024)(128)(4,1)} %bitcast.6), calls=%async_computation.1 | async-start | bytes 8388608
  51.9 7.2 %slice-start.1 = ((s8[8388608]{0:T(1024)(128)(4,1)}), s8[4194304]{0:T(1024)(128)(4,1)S(1)}, s32[]{:S(2)}) async-start(s8[8388608]{0:T(1024)(128)(4,1)} %bitcast.6), calls=%async_computation.2 | async-start | bytes 8388608
  57.1 2.0 %collective-permute-start.10 = (bf16[128,256]{1,0:T(8,128)(2,1)S(1)}, bf16[128,256]{1,0:T(8,128)(2,1)S(1)}, u32[]{:S(2)}, u32[]{:S(2)}) collective-permute-start(bf16[128,256]{1,0:T(8,128)(2,1)S(1)} %get-tuple-element.62), channel_id=1, source_target_pairs={{0,1},{1,0},{2,3},{3,2},{4,5},{5,4},{6,7},{7,6},{8,9},{9,8},{10,11... | collective-permute-start | bytes 196616 | tf_op jit(solution)/shard_map/ppermute | solution.py:478
  57.1 7.2 %collective-permute-start.7 = (bf16[128,256]{1,0:T(8,128)(2,1)S(1)}, bf16[128,256]{1,0:T(8,128)(2,1)S(1)}, u32[]{:S(2)}, u32[]{:S(2)}) collective-permute-start(bf16[128,256]{1,0:T(8,128)(2,1)S(1)} %get-tuple-element.56), channel_id=1, source_target_pairs={{0,4},{4,0},{8,12},{12,8},{16,20},{20,16},{24,28},{28,24},{1,5},{5... | collective-permute-start | bytes 196616 | tf_op jit(solution)/shard_map/ppermute | solution.py:479
  57.9 6.4 %collective-permute-start.8 = (bf16[128,256]{1,0:T(8,128)(2,1)S(1)}, bf16[128,256]{1,0:T(8,128)(2,1)S(1)}, u32[]{:S(2)}, u32[]{:S(2)}) collective-permute-start(bf16[128,256]{1,0:T(8,128)(2,1)S(1)} %get-tuple-element.57), channel_id=1, source_target_pairs={{0,5},{1,4},{2,7},{3,6},{4,1},{5,0},{6,3},{7,2},{8,13},{9,12},{10,... | collective-permute-start | bytes 196616 | tf_op jit(solution)/shard_map/ppermute | solution.py:480
  66.8 22.9 %collective-permute-start.16 = (bf16[128,2048]{1,0:T(8,128)(2,1)S(1)}, bf16[128,2048]{1,0:T(8,128)(2,1)S(1)}, u32[]{:S(2)}, u32[]{:S(2)}) collective-permute-start(bf16[128,2048]{1,0:T(8,128)(2,1)S(1)} %shard_map.51), channel_id=1, source_target_pairs={{0,2},{1,3},{2,0},{3,1},{4,6},{5,7},{6,4},{7,5},{8,10},{9,11},{10,... | collective-permute-start | bytes 1572872 | tf_op jit(solution)/shard_map/ppermute | solution.py:511
  70.8 21.4 %collective-permute-start.17 = (bf16[128,2048]{1,0:T(8,128)(2,1)S(1)}, bf16[128,2048]{1,0:T(8,128)(2,1)S(1)}, u32[]{:S(2)}, u32[]{:S(2)}) collective-permute-start(bf16[128,2048]{1,0:T(8,128)(2,1)S(1)} %shard_map.52), channel_id=1, source_target_pairs={{0,2},{1,3},{2,0},{3,1},{4,6},{5,7},{6,4},{7,5},{8,10},{9,11},{10,... | collective-permute-start | bytes 1572872 | tf_op jit(solution)/shard_map/ppermute | solution.py:511
  75.1 1.9 %collective-permute-start.13 = (bf16[128,512]{1,0:T(8,128)(2,1)S(1)}, bf16[128,512]{1,0:T(8,128)(2,1)S(1)}, u32[]{:S(2)}, u32[]{:S(2)}) collective-permute-start(bf16[128,512]{1,0:T(8,128)(2,1)S(1)} %get-tuple-element.67), channel_id=1, source_target_pairs={{0,1},{1,0},{2,3},{3,2},{4,5},{5,4},{6,7},{7,6},{8,9},{9,8},{10,11... | collective-permute-start | bytes 393224 | tf_op jit(solution)/shard_map/ppermute | solution.py:478
  75.2 6.4 %collective-permute-start.14 = (bf16[128,512]{1,0:T(8,128)(2,1)S(1)}, bf16[128,512]{1,0:T(8,128)(2,1)S(1)}, u32[]{:S(2)}, u32[]{:S(2)}) collective-permute-start(bf16[128,512]{1,0:T(8,128)(2,1)S(1)} %get-tuple-element.68), channel_id=1, source_target_pairs={{0,4},{4,0},{8,12},{12,8},{16,20},{20,16},{24,28},{28,24},{1,5},{5... | collective-permute-start | bytes 393224 | tf_op jit(solution)/shard_map/ppermute | solution.py:479
  76.0 7.5 %collective-permute-start.15 = (bf16[128,512]{1,0:T(8,128)(2,1)S(1)}, bf16[128,512]{1,0:T(8,128)(2,1)S(1)}, u32[]{:S(2)}, u32[]{:S(2)}) collective-permute-start(bf16[128,512]{1,0:T(8,128)(2,1)S(1)} %get-tuple-element.69), channel_id=1, source_target_pairs={{0,5},{1,4},{2,7},{3,6},{4,1},{5,0},{6,3},{7,2},{8,13},{9,12},{10,... | collective-permute-start | bytes 393224 | tf_op jit(solution)/shard_map/ppermute | solution.py:480

commit v6 on v5

--- a/solution.py
+++ b/solution.py
@@ -15,6 +15,8 @@
 FAR_ROWS = 128
 NEG = -1e30
 VMEM_BYTES = 16 << 20
+PROJECT_BYTES = 24 << 20
+RING_VALUES = 13 << 19
 SCALE = HD ** (-0.5) * math.log2(math.e)
 F32, BF16 = jnp.float32, jnp.bfloat16
 IN_HBM = pl.BlockSpec(memory_space=pltpu.HBM)
@@ -484,7 +486,7 @@
         columns = w_out.shape[1] // parts
         width = pieces[0].shape[1]
         chunk = 512 if begun is None else 1024
-        ring = max(2, min(8, (4 << 20) // (width * len(pieces) * chunk)))
+        ring = max(2, min(8, RING_VALUES // (width * len(pieces) * chunk)))
         more = [] if begun is None else [begun]
         (out,) = call(
             functools.partial(project_kernel, places, half, ring, part, chunk, begun is not None),
@@ -493,6 +495,7 @@
             1,
             [IN_SMEM] + [IN_VMEM] * len(pieces) + [IN_HBM] * 2 + [IN_VMEM] * len(more),
             [ids, *pieces, w_out, w_other, *more],
+            PROJECT_BYTES,
         )
         return out
 

time: 94.4 us -> 94.2 us (level)
    ppermute x2, waiting for transfers between devices: 2.07 us -> 3.12 us  [per_device(): crossed = [lax.ppermute(part, 'ctx', hop) for part in kv_other]]
where the time goes in v6:
time: 94.2 us; the launch traced here: 93.7 us
  Pallas kernels  34.4 us (37%)
  waiting for transfers between devices  33.2 us (35%)
  starting transfers between devices  15.5 us (16%)
  local copies, waits for them, and re-layouts  8.78 us (9%)
    pallas_call x9, Pallas kernels, call(): pl.pallas_call(kernel, in_specs=specs, out_specs=[IN_VMEM] * len(outs), o...  33.3 us
    ppermute x2, waiting for transfers between devices, per_device(): lax.ppermute(lax.dynamic_slice_in_dim(keys_values, (1 - side) * half + gr...  18.6 us
    slice x3, local copies, waits for them, and re-layouts, per_device(): tails = [kv_own[:, last:]] + [part[:, last:] for part in kv_other]  4.82 us
    ppermute x3, waiting for transfers between devices, exchanged(): lax.ppermute(pieces[2], 'ctx', swap)  4.5 us
    dynamic_slice x2, local copies, waits for them, and re-layouts, mine(): return lax.dynamic_slice_in_dim(array, side * half, half, axis)  3.68 us
    ppermute x2, waiting for transfers between devices, per_device(): crossed = [lax.ppermute(part, 'ctx', hop) for part in kv_other]  3.12 us
    ppermute x1, waiting for transfers between devices, per_device(): q_other = lax.ppermute(q_send, 'ctx', swap)  2.84 us
    ppermute x3, starting transfers between devices, exchanged(): lax.ppermute(pieces[3], ('ctx', 'head'), both)  2.81 us
  transfers between devices with their start and end apart: 18, of which 7 were waited for; matrix products, arithmetic and copies ran while one was open for 10% of the time, Pallas kernels for 33%

profile of v6, /device:TPU:24, one launch (start us, length us, event | category | flops | bytes accessed | tf_op | source)
XLA Modules:
  0.0 93.7 jit_solution(14915649663556625693)
XLA Ops:
  0.0 0.0 copy-start
  0.0 0.0 collective-permute-start.1
  0.0 2.4 %constant_dynamic-slice_fusion.4.kv_own = bf16[2,512,512]{2,1,0:T(8,128)(2,1)} fusion(bf16[2,512,1024]{2,1,0:T(8,128)(2,1)} %param.7, s32[]{:T(128)S(6)} %select_n.27), kind=kLoop, calls=%fused_computation.10 | loop fusion | bytes 2097156 | tf_op jit(solution)/shard_map/dynamic_slice | solution.py:395
  2.4 0.0 copy-done
  2.4 0.0 copy-start.1
  2.4 0.1 constant_dynamic-slice_fusion
  2.6 1.6 %collective-permute-start = (bf16[2,512,256]{2,1,0:T(8,128)(2,1)S(1)}, bf16[2,512,256]{2,1,0:T(8,128)(2,1)}, u32[]{:S(2)}, u32[]{:S(2)}) collective-permute-start(bf16[2,512,256]{2,1,0:T(8,128)(2,1)S(1)} %get-tuple-element.71), channel_id=1, source_target_pairs={{0,4},{4,0},{8,12},{12,8},{16,20},{20,16},{24,28},{28,24},{1,5},{5... | collective-permute-start | bytes 1572872 | tf_op jit(solution)/shard_map/ppermute | solution.py:405
  4.1 1.3 %collective-permute-start.5 = (bf16[2,512,512]{2,1,0:T(8,128)(2,1)}, bf16[2,512,512]{2,1,0:T(8,128)(2,1)}, u32[]{:S(2)}, u32[]{:S(2)}) collective-permute-start(bf16[2,512,512]{2,1,0:T(8,128)(2,1)} %constant_dynamic-slice_fusion.4.kv_own), channel_id=1, source_target_pairs={{0,8},{4,12},{8,16},{12,20},{16,24},{20,28},{1,9},{5,13},{9,17},{1... | collective-permute-start | bytes 3145736 | tf_op jit(solution)/shard_map/ppermute | solution.py:402
  5.4 0.6 collective-permute-start.4
  6.0 1.3 %constant_dynamic-slice_fusion.1 = (bf16[512,512]{1,0:T(8,128)(2,1)S(1)}, bf16[512,512]{1,0:T(8,128)(2,1)S(1)}) fusion(bf16[512,1024]{1,0:T(8,128)(2,1)} %param.6, s32[]{:T(128)S(6)} %select_n.27, s32[]{:T(128)S(6)} %select_n.28), kind=kLoop, calls=%fused_computation.7 | loop fusion | bytes 2097160 | tf_op jit(solution)/shard_map/dynamic_slice | solution.py:395
  7.3 10.2 %collective-permute-done.kv_other_a = bf16[2,512,256]{2,1,0:T(8,128)(2,1)} collective-permute-done((bf16[2,512,256]{2,1,0:T(8,128)(2,1)S(1)}, bf16[2,512,256]{2,1,0:T(8,128)(2,1)}, u32[]{:S(2)}, u32[]{:S(2)}) %collective-permute-start) | collective-permute-done | bytes 524320 | tf_op jit(solution)/shard_map/ppermute | solution.py:405
  17.5 0.0 collective-permute-done.1.refs_7_.refs_3_.refs_5_
  17.5 1.5 %collective-permute-start.3 = (bf16[512,512]{1,0:T(8,128)(2,1)S(1)}, bf16[512,512]{1,0:T(8,128)(2,1)S(1)}, u32[]{:S(2)}, u32[]{:S(2)}) collective-permute-start(bf16[512,512]{1,0:T(8,128)(2,1)S(1)} %get-tuple-element.48), channel_id=1, source_target_pairs={{0,4},{4,0},{8,12},{12,8},{16,20},{20,16},{24,28},{28,24},{1,5},{5... | collective-permute-start | bytes 1572872 | tf_op jit(solution)/shard_map/ppermute | solution.py:415
  19.0 1.3 %collective-permute-start.2 = (bf16[2,512,256]{2,1,0:T(8,128)(2,1)}, bf16[2,512,256]{2,1,0:T(8,128)(2,1)}, u32[]{:S(2)}, u32[]{:S(2)}) collective-permute-start(bf16[2,512,256]{2,1,0:T(8,128)(2,1)} %collective-permute-done.kv_other_a), channel_id=1, source_target_pairs={{0,8},{4,12},{8,16},{12,20},{16,24},{20,28},{1,9},{5,13},{9,17},{1... | collective-permute-start | bytes 1572872 | tf_op jit(solution)/shard_map/ppermute | solution.py:416
  20.3 8.5 %collective-permute-done.4.kv_other_b = bf16[2,512,256]{2,1,0:T(8,128)(2,1)} collective-permute-done((bf16[2,512,256]{2,1,0:T(8,128)(2,1)S(1)}, bf16[2,512,256]{2,1,0:T(8,128)(2,1)}, u32[]{:S(2)}, u32[]{:S(2)}) %collective-permute-start.4) | collective-permute-done | bytes 524320 | tf_op jit(solution)/shard_map/ppermute | solution.py:405
  28.7 1.3 %collective-permute-start.6 = (bf16[2,512,256]{2,1,0:T(8,128)(2,1)}, bf16[2,512,256]{2,1,0:T(8,128)(2,1)}, u32[]{:S(2)}, u32[]{:S(2)}) collective-permute-start(bf16[2,512,256]{2,1,0:T(8,128)(2,1)} %collective-permute-done.4.kv_other_b), channel_id=1, source_target_pairs={{0,8},{4,12},{8,16},{12,20},{16,24},{20,28},{1,9},{5,13},{9,17},{1... | collective-permute-start | bytes 1572872 | tf_op jit(solution)/shard_map/ppermute | solution.py:416
  30.0 1.7 %slice.18 = bf16[2,128,512]{2,1,0:T(8,128)(2,1)} slice(bf16[2,512,512]{2,1,0:T(8,128)(2,1)} %constant_dynamic-slice_fusion.4.kv_own), slice={[0:2], [384:512], [0:512]} | slice | bytes 524288 | tf_op jit(solution)/shard_map/slice | solution.py:446
  31.7 0.0 copy-done.1
  31.7 0.1 pad_dynamic-slice_fusion.docs
  31.8 0.8 compare_reduce_fusion
  33.2 0.1 pad_add_fusion.ids
  33.3 1.6 %slice.24 = bf16[2,128,256]{2,1,0:T(8,128)(2,1)} slice(bf16[2,512,256]{2,1,0:T(8,128)(2,1)} %collective-permute-done.4.kv_other_b), slice={[0:2], [384:512], [0:256]} | slice | bytes 262144 | tf_op jit(solution)/shard_map/slice | solution.py:446
  34.9 1.6 %slice.19 = bf16[2,128,256]{2,1,0:T(8,128)(2,1)} slice(bf16[2,512,256]{2,1,0:T(8,128)(2,1)} %collective-permute-done.kv_other_a), slice={[0:2], [384:512], [0:256]} | slice | bytes 262144 | tf_op jit(solution)/shard_map/slice | solution.py:446
  36.4 2.8 %collective-permute-done.3.q_other = bf16[512,512]{1,0:T(8,128)(2,1)S(1)} collective-permute-done((bf16[512,512]{1,0:T(8,128)(2,1)S(1)}, bf16[512,512]{1,0:T(8,128)(2,1)S(1)}, u32[]{:S(2)}, u32[]{:S(2)}) %collective-permute-start.3) | collective-permute-done | bytes 524320 | tf_op jit(solution)/shard_map/ppermute | solution.py:415
  39.3 5.1 %shard_map.47 = (f32[512,1024]{1,0:T(8,128)S(1)}, f32[8,1024]{1,0:T(8,128)S(1)}) custom-call(s32[2]{0:T(128)S(1)} %pad_add_fusion.ids, s32[2304]{0:T(1024)S(1)} %pad_dynamic-slice_fusion.docs, s32[1,2304]{1,0:T(1,128)S(1)} %reshape.7.docs_row, bf16[512,512]{1,0:T(8,128)(2,1)S(1)} %get-tuple-element.72.q_own, ...), custom_call_target="tpu_custom_call" | custom-call | flops 7000 | bytes 1024 | tf_op jit(solution)/shard_map/pallas_call | solution.py:353
  44.4 0.0 collective-permute-done.5.same
  44.4 0.0 collective-permute-done.2.refs_0_.rest_0_
  44.4 3.3 %shard_map.49 = (bf16[128,256]{1,0:T(8,128)(2,1)S(1)}, bf16[128,256]{1,0:T(8,128)(2,1)S(1)}, bf16[128,256]{1,0:T(8,128)(2,1)S(1)}, bf16[128,256]{1,0:T(8,128)(2,1)S(1)}) custom-call(s32[2]{0:T(128)S(1)} %pad_add_fusion.ids, s32[2304]{0:T(1024)S(1)} %pad_dynamic-slice_fusion.docs, s32[1,2304]{1,0:T(1,128)S(1)} %reshape.7.docs_row, ...), custom_call_target="tpu_custom_call" | custom-call | flops 1000 | bytes 1024 | tf_op jit(solution)/shard_map/pallas_call | solution.py:353
  47.7 0.1 collective-permute-start.9
  47.8 1.6 %collective-permute-start.11 = (bf16[128,256]{1,0:T(8,128)(2,1)S(1)}, bf16[128,256]{1,0:T(8,128)(2,1)S(1)}, u32[]{:S(2)}, u32[]{:S(2)}) collective-permute-start(bf16[128,256]{1,0:T(8,128)(2,1)S(1)} %get-tuple-element.63), channel_id=1, source_target_pairs={{0,4},{4,0},{8,12},{12,8},{16,20},{20,16},{24,28},{28,24},{1,5},{5... | collective-permute-start | bytes 196616 | tf_op jit(solution)/shard_map/ppermute | solution.py:481
  49.4 0.3 collective-permute-start.12
  49.7 0.0 slice-start
  49.7 1.1 %shard_map.46.ids = s32[2]{0:T(128)S(1)} custom-call(s32[2]{0:T(128)S(1)} %pad_add_fusion.ids, bf16[2,512,256]{2,1,0:T(8,128)(2,1)} %collective-permute-done.2.refs_0_.rest_0_), custom_call_target="tpu_custom_call" | custom-call | flops 550000000 | bytes 1024 | tf_op jit(solution)/shard_map/pallas_call | solution.py:340
  50.8 0.0 slice-start.1
  50.8 3.1 %collective-permute-done.6.rest_0_.rest_1_ = bf16[2,512,256]{2,1,0:T(8,128)(2,1)} collective-permute-done((bf16[2,512,256]{2,1,0:T(8,128)(2,1)}, bf16[2,512,256]{2,1,0:T(8,128)(2,1)}, u32[]{:S(2)}, u32[]{:S(2)}) %collective-permute-start.6) | collective-permute-done | bytes 524320 | tf_op jit(solution)/shard_map/ppermute | solution.py:416
  53.9 3.5 %shard_map.48 = (bf16[128,256]{1,0:T(8,128)(2,1)S(1)}, bf16[128,256]{1,0:T(8,128)(2,1)S(1)}, bf16[128,256]{1,0:T(8,128)(2,1)S(1)}, bf16[128,256]{1,0:T(8,128)(2,1)S(1)}) custom-call(s32[2]{0:T(128)S(1)} %shard_map.46.ids, s32[2304]{0:T(1024)S(1)} %pad_dynamic-slice_fusion.docs, s32[1,2304]{1,0:T(1,128)S(1)} %reshape.7.docs_row, ...), custom_call_target="tpu_custom_call" | custom-call | flops 5000000000 | bytes 1024 | tf_op jit(solution)/shard_map/pallas_call | solution.py:353
  57.4 0.1 collective-permute-start.10
  57.5 0.6 collective-permute-start.7
  58.1 0.0 collective-permute-done.9.refs_1_
  58.1 1.3 %collective-permute-start.8 = (bf16[128,256]{1,0:T(8,128)(2,1)S(1)}, bf16[128,256]{1,0:T(8,128)(2,1)S(1)}, u32[]{:S(2)}, u32[]{:S(2)}) collective-permute-start(bf16[128,256]{1,0:T(8,128)(2,1)S(1)} %get-tuple-element.57), channel_id=1, source_target_pairs={{0,5},{1,4},{2,7},{3,6},{4,1},{5,0},{6,3},{7,2},{8,13},{9,12},{10,... | collective-permute-start | bytes 196616 | tf_op jit(solution)/shard_map/ppermute | solution.py:482
  59.3 0.0 collective-permute-done.11.refs_4_
  59.3 0.0 collective-permute-done.12.refs_5_
  59.3 0.0 collective-permute-done.10.refs_3_
  59.4 0.0 slice-done
  59.4 0.0 slice-done.1
  59.4 5.2 %shard_map.50.refs_4_ = f32[128,4096]{1,0:T(8,128)S(1)} custom-call(s32[2]{0:T(128)S(1)} %pad_add_fusion.ids, bf16[128,256]{1,0:T(8,128)(2,1)S(1)} %get-tuple-element.59.refs_0_, bf16[128,256]{1,0:T(8,128)(2,1)S(1)} %collective-permute-done.9.refs_1_, bf16[128,256]{1,0:T(8,128)(2,1)S(1)} %get-tuple-element.61.refs_2_, ...), custom_call_target="tpu_custom_call" | custom-call | flops 1000 | bytes 1024 | tf_op jit(solution)/shard_map/pallas_call | solution.py:353
  64.6 0.0 collective-permute-done.7.refs_0_
  64.6 0.0 collective-permute-done.8.refs_1_
  64.6 2.4 %shard_map.51 = bf16[128,2048]{1,0:T(8,128)(2,1)S(1)} custom-call(s32[2]{0:T(128)S(1)} %pad_add_fusion.ids, bf16[128,256]{1,0:T(8,128)(2,1)S(1)} %collective-permute-done.7.refs_0_, bf16[128,256]{1,0:T(8,128)(2,1)S(1)} %collective-permute-done.8.refs_1_, bf16[1024,4096]{1,0:T(8,128)(2,1)S(1)} %bitcast.7, ...), custom_call_target="tpu_custom_call" | custom-call | flops 1000 | bytes 1024 | tf_op jit(solution)/shard_map/pallas_call | solution.py:353
  67.1 1.6 %collective-permute-start.16 = (bf16[128,2048]{1,0:T(8,128)(2,1)S(1)}, bf16[128,2048]{1,0:T(8,128)(2,1)S(1)}, u32[]{:S(2)}, u32[]{:S(2)}) collective-permute-start(bf16[128,2048]{1,0:T(8,128)(2,1)S(1)} %shard_map.51), channel_id=1, source_target_pairs={{0,2},{1,3},{2,0},{3,1},{4,6},{5,7},{6,4},{7,5},{8,10},{9,11},{10,... | collective-permute-start | bytes 1572872 | tf_op jit(solution)/shard_map/ppermute | solution.py:514
  68.7 2.4 %shard_map.52 = bf16[128,2048]{1,0:T(8,128)(2,1)S(1)} custom-call(s32[2]{0:T(128)S(1)} %pad_add_fusion.ids, bf16[128,256]{1,0:T(8,128)(2,1)S(1)} %collective-permute-done.7.refs_0_, bf16[128,256]{1,0:T(8,128)(2,1)S(1)} %collective-permute-done.8.refs_1_, bf16[1024,4096]{1,0:T(8,128)(2,1)S(1)} %bitcast.7, ...), custom_call_target="tpu_custom_call" | custom-call | flops 1000 | bytes 1024 | tf_op jit(solution)/shard_map/pallas_call | solution.py:353
  71.1 0.6 collective-permute-start.17
  71.7 4.3 %shard_map.53 = (bf16[128,512]{1,0:T(8,128)(2,1)S(1)}, bf16[128,512]{1,0:T(8,128)(2,1)S(1)}, bf16[128,512]{1,0:T(8,128)(2,1)S(1)}, bf16[128,512]{1,0:T(8,128)(2,1)S(1)}) custom-call(s32[2]{0:T(128)S(1)} %shard_map.46.ids, s32[2304]{0:T(1024)S(1)} %pad_dynamic-slice_fusion.docs, s32[1,2304]{1,0:T(1,128)S(1)} %reshape.7.docs_row, ...), custom_call_target="tpu_custom_call" | custom-call | flops 1000 | bytes 1024 | tf_op jit(solution)/shard_map/pallas_call | solution.py:353
  76.0 0.1 collective-permute-start.13
  76.0 0.6 collective-permute-start.14
  76.6 1.3 %collective-permute-start.15 = (bf16[128,512]{1,0:T(8,128)(2,1)S(1)}, bf16[128,512]{1,0:T(8,128)(2,1)S(1)}, u32[]{:S(2)}, u32[]{:S(2)}) collective-permute-start(bf16[128,512]{1,0:T(8,128)(2,1)S(1)} %get-tuple-element.69), channel_id=1, source_target_pairs={{0,5},{1,4},{2,7},{3,6},{4,1},{5,0},{6,3},{7,2},{8,13},{9,12},{10,... | collective-permute-start | bytes 393224 | tf_op jit(solution)/shard_map/ppermute | solution.py:482
  77.9 0.0 collective-permute-done.13.refs_1_
  77.9 4.5 %collective-permute-done.14.refs_2_ = bf16[128,512]{1,0:T(8,128)(2,1)S(1)} collective-permute-done((bf16[128,512]{1,0:T(8,128)(2,1)S(1)}, bf16[128,512]{1,0:T(8,128)(2,1)S(1)}, u32[]{:S(2)}, u32[]{:S(2)}) %collective-permute-start.14) | collective-permute-done | bytes 131104 | tf_op jit(solution)/shard_map/ppermute | solution.py:481
  82.4 1.9 %collective-permute-done.15.refs_3_ = bf16[128,512]{1,0:T(8,128)(2,1)S(1)} collective-permute-done((bf16[128,512]{1,0:T(8,128)(2,1)S(1)}, bf16[128,512]{1,0:T(8,128)(2,1)S(1)}, u32[]{:S(2)}, u32[]{:S(2)}) %collective-permute-start.15) | collective-permute-done | bytes 131104 | tf_op jit(solution)/shard_map/ppermute | solution.py:482
  84.3 6.0 %shard_map.54.staying = f32[128,4096]{1,0:T(8,128)S(1)} custom-call(s32[2]{0:T(128)S(1)} %pad_add_fusion.ids, bf16[128,512]{1,0:T(8,128)(2,1)S(1)} %get-tuple-element.66.refs_0_, bf16[128,512]{1,0:T(8,128)(2,1)S(1)} %collective-permute-done.13.refs_1_, bf16[128,512]{1,0:T(8,128)(2,1)S(1)} %collective-permute-done.14.refs_2_, ...), custom_call_target="tpu_custom_call" | custom-call | flops 1000 | bytes 1024 | tf_op jit(solution)/shard_map/pallas_call | solution.py:353
  90.3 0.0 collective-permute-done.16.refs_0_
  90.3 2.2 %collective-permute-done.17.refs_1_ = bf16[128,2048]{1,0:T(8,128)(2,1)S(1)} collective-permute-done((bf16[128,2048]{1,0:T(8,128)(2,1)S(1)}, bf16[128,2048]{1,0:T(8,128)(2,1)S(1)}, u32[]{:S(2)}, u32[]{:S(2)}) %collective-permute-start.17) | collective-permute-done | bytes 524320 | tf_op jit(solution)/shard_map/ppermute | solution.py:514
  92.5 1.1 %shard_map.55 = bf16[128,4096]{1,0:T(8,128)(2,1)} custom-call(f32[128,4096]{1,0:T(8,128)S(1)} %shard_map.54.staying, bf16[128,2048]{1,0:T(8,128)(2,1)S(1)} %collective-permute-done.16.refs_0_, bf16[128,2048]{1,0:T(8,128)(2,1)S(1)} %collective-permute-done.17.refs_1_), custom_call_target="tpu_custom_call" | custom-call | flops 1000 | bytes 1024 | tf_op jit(solution)/shard_map/pallas_call | solution.py:353
  (5 shorter events, 0.1 us)
Async XLA Ops:
  0.0 2.4 %copy-start = (bf16[2,512,1024]{2,1,0:T(8,128)(2,1)S(1)}, bf16[2,512,1024]{2,1,0:T(8,128)(2,1)}, u32[]{:S(2)}) copy-start(bf16[2,512,1024]{2,1,0:T(8,128)(2,1)} %param.7) | copy-start | bytes 6291460
  0.0 17.5 %collective-permute-start.1 = (bf16[1024,4096]{1,0:T(8,128)(2,1)}, bf16[1024,4096]{1,0:T(8,128)(2,1)}, u32[]{:S(2)}, u32[]{:S(2)}) collective-permute-start(bf16[1024,4096]{1,0:T(8,128)(2,1)} %refs_4_.1), channel_id=1, source_target_pairs={{0,1},{1,0},{2,3},{3,2},{4,5},{5,4},{6,7},{7,6},{8,9},{9,8},{10,11... | collective-permute-start | bytes 25165832 | tf_op jit(solution)/shard_map/ppermute | solution.py:412
  2.4 29.3 %copy-start.1 = (s32[4096]{0:T(1024)S(1)}, s32[4096]{0:T(1024)}, u32[]{:S(2)}) copy-start(s32[4096]{0:T(1024)} %param.9) | copy-start | bytes 49156
  2.6 14.9 %collective-permute-start = (bf16[2,512,256]{2,1,0:T(8,128)(2,1)S(1)}, bf16[2,512,256]{2,1,0:T(8,128)(2,1)}, u32[]{:S(2)}, u32[]{:S(2)}) collective-permute-start(bf16[2,512,256]{2,1,0:T(8,128)(2,1)S(1)} %get-tuple-element.71), channel_id=1, source_target_pairs={{0,4},{4,0},{8,12},{12,8},{16,20},{20,16},{24,28},{28,24},{1,5},{5... | collective-permute-start | bytes 1572872 | tf_op jit(solution)/shard_map/ppermute | solution.py:405
  4.1 40.3 %collective-permute-start.5 = (bf16[2,512,512]{2,1,0:T(8,128)(2,1)}, bf16[2,512,512]{2,1,0:T(8,128)(2,1)}, u32[]{:S(2)}, u32[]{:S(2)}) collective-permute-start(bf16[2,512,512]{2,1,0:T(8,128)(2,1)} %constant_dynamic-slice_fusion.4.kv_own), channel_id=1, source_target_pairs={{0,8},{4,12},{8,16},{12,20},{16,24},{20,28},{1,9},{5,13},{9,17},{1... | collective-permute-start | bytes 3145736 | tf_op jit(solution)/shard_map/ppermute | solution.py:402
  5.4 23.3 %collective-permute-start.4 = (bf16[2,512,256]{2,1,0:T(8,128)(2,1)S(1)}, bf16[2,512,256]{2,1,0:T(8,128)(2,1)}, u32[]{:S(2)}, u32[]{:S(2)}) collective-permute-start(bf16[2,512,256]{2,1,0:T(8,128)(2,1)S(1)} %get-tuple-element.70), channel_id=1, source_target_pairs={{0,4},{4,0},{8,12},{12,8},{16,20},{20,16},{24,28},{28,24},{1,5},{5... | collective-permute-start | bytes 1572872 | tf_op jit(solution)/shard_map/ppermute | solution.py:405
  17.5 21.8 %collective-permute-start.3 = (bf16[512,512]{1,0:T(8,128)(2,1)S(1)}, bf16[512,512]{1,0:T(8,128)(2,1)S(1)}, u32[]{:S(2)}, u32[]{:S(2)}) collective-permute-start(bf16[512,512]{1,0:T(8,128)(2,1)S(1)} %get-tuple-element.48), channel_id=1, source_target_pairs={{0,4},{4,0},{8,12},{12,8},{16,20},{20,16},{24,28},{28,24},{1,5},{5... | collective-permute-start | bytes 1572872 | tf_op jit(solution)/shard_map/ppermute | solution.py:415
  19.0 25.4 %collective-permute-start.2 = (bf16[2,512,256]{2,1,0:T(8,128)(2,1)}, bf16[2,512,256]{2,1,0:T(8,128)(2,1)}, u32[]{:S(2)}, u32[]{:S(2)}) collective-permute-start(bf16[2,512,256]{2,1,0:T(8,128)(2,1)} %collective-permute-done.kv_other_a), channel_id=1, source_target_pairs={{0,8},{4,12},{8,16},{12,20},{16,24},{20,28},{1,9},{5,13},{9,17},{1... | collective-permute-start | bytes 1572872 | tf_op jit(solution)/shard_map/ppermute | solution.py:416
  28.7 25.2 %collective-permute-start.6 = (bf16[2,512,256]{2,1,0:T(8,128)(2,1)}, bf16[2,512,256]{2,1,0:T(8,128)(2,1)}, u32[]{:S(2)}, u32[]{:S(2)}) collective-permute-start(bf16[2,512,256]{2,1,0:T(8,128)(2,1)} %collective-permute-done.4.kv_other_b), channel_id=1, source_target_pairs={{0,8},{4,12},{8,16},{12,20},{16,24},{20,28},{1,9},{5,13},{9,17},{1... | collective-permute-start | bytes 1572872 | tf_op jit(solution)/shard_map/ppermute | solution.py:416
  47.7 10.4 %collective-permute-start.9 = (bf16[128,256]{1,0:T(8,128)(2,1)S(1)}, bf16[128,256]{1,0:T(8,128)(2,1)S(1)}, u32[]{:S(2)}, u32[]{:S(2)}) collective-permute-start(bf16[128,256]{1,0:T(8,128)(2,1)S(1)} %get-tuple-element.60), channel_id=1, source_target_pairs={{0,1},{1,0},{2,3},{3,2},{4,5},{5,4},{6,7},{7,6},{8,9},{9,8},{10,11... | collective-permute-start | bytes 196616 | tf_op jit(solution)/shard_map/ppermute | solution.py:480
  47.8 11.5 %collective-permute-start.11 = (bf16[128,256]{1,0:T(8,128)(2,1)S(1)}, bf16[128,256]{1,0:T(8,128)(2,1)S(1)}, u32[]{:S(2)}, u32[]{:S(2)}) collective-permute-start(bf16[128,256]{1,0:T(8,128)(2,1)S(1)} %get-tuple-element.63), channel_id=1, source_target_pairs={{0,4},{4,0},{8,12},{12,8},{16,20},{20,16},{24,28},{28,24},{1,5},{5... | collective-permute-start | bytes 196616 | tf_op jit(solution)/shard_map/ppermute | solution.py:481
  49.4 10.0 %collective-permute-start.12 = (bf16[128,256]{1,0:T(8,128)(2,1)S(1)}, bf16[128,256]{1,0:T(8,128)(2,1)S(1)}, u32[]{:S(2)}, u32[]{:S(2)}) collective-permute-start(bf16[128,256]{1,0:T(8,128)(2,1)S(1)} %get-tuple-element.64), channel_id=1, source_target_pairs={{0,5},{1,4},{2,7},{3,6},{4,1},{5,0},{6,3},{7,2},{8,13},{9,12},{10,... | collective-permute-start | bytes 196616 | tf_op jit(solution)/shard_map/ppermute | solution.py:482
  49.7 9.7 %slice-start = ((s8[8388608]{0:T(1024)(128)(4,1)}), s8[4194304]{0:T(1024)(128)(4,1)S(1)}, s32[]{:S(2)}) async-start(s8[8388608]{0:T(1024)(128)(4,1)} %bitcast.6), calls=%async_computation.1 | async-start | bytes 8388608
  50.8 8.6 %slice-start.1 = ((s8[8388608]{0:T(1024)(128)(4,1)}), s8[4194304]{0:T(1024)(128)(4,1)S(1)}, s32[]{:S(2)}) async-start(s8[8388608]{0:T(1024)(128)(4,1)} %bitcast.6), calls=%async_computation.2 | async-start | bytes 8388608
  57.4 2.0 %collective-permute-start.10 = (bf16[128,256]{1,0:T(8,128)(2,1)S(1)}, bf16[128,256]{1,0:T(8,128)(2,1)S(1)}, u32[]{:S(2)}, u32[]{:S(2)}) collective-permute-start(bf16[128,256]{1,0:T(8,128)(2,1)S(1)} %get-tuple-element.62), channel_id=1, source_target_pairs={{0,1},{1,0},{2,3},{3,2},{4,5},{5,4},{6,7},{7,6},{8,9},{9,8},{10,11... | collective-permute-start | bytes 196616 | tf_op jit(solution)/shard_map/ppermute | solution.py:480
  57.5 7.1 %collective-permute-start.7 = (bf16[128,256]{1,0:T(8,128)(2,1)S(1)}, bf16[128,256]{1,0:T(8,128)(2,1)S(1)}, u32[]{:S(2)}, u32[]{:S(2)}) collective-permute-start(bf16[128,256]{1,0:T(8,128)(2,1)S(1)} %get-tuple-element.56), channel_id=1, source_target_pairs={{0,4},{4,0},{8,12},{12,8},{16,20},{20,16},{24,28},{28,24},{1,5},{5... | collective-permute-start | bytes 196616 | tf_op jit(solution)/shard_map/ppermute | solution.py:481
  58.1 6.5 %collective-permute-start.8 = (bf16[128,256]{1,0:T(8,128)(2,1)S(1)}, bf16[128,256]{1,0:T(8,128)(2,1)S(1)}, u32[]{:S(2)}, u32[]{:S(2)}) collective-permute-start(bf16[128,256]{1,0:T(8,128)(2,1)S(1)} %get-tuple-element.57), channel_id=1, source_target_pairs={{0,5},{1,4},{2,7},{3,6},{4,1},{5,0},{6,3},{7,2},{8,13},{9,12},{10,... | collective-permute-start | bytes 196616 | tf_op jit(solution)/shard_map/ppermute | solution.py:482
  67.1 23.2 %collective-permute-start.16 = (bf16[128,2048]{1,0:T(8,128)(2,1)S(1)}, bf16[128,2048]{1,0:T(8,128)(2,1)S(1)}, u32[]{:S(2)}, u32[]{:S(2)}) collective-permute-start(bf16[128,2048]{1,0:T(8,128)(2,1)S(1)} %shard_map.51), channel_id=1, source_target_pairs={{0,2},{1,3},{2,0},{3,1},{4,6},{5,7},{6,4},{7,5},{8,10},{9,11},{10,... | collective-permute-start | bytes 1572872 | tf_op jit(solution)/shard_map/ppermute | solution.py:514
  71.1 21.4 %collective-permute-start.17 = (bf16[128,2048]{1,0:T(8,128)(2,1)S(1)}, bf16[128,2048]{1,0:T(8,128)(2,1)S(1)}, u32[]{:S(2)}, u32[]{:S(2)}) collective-permute-start(bf16[128,2048]{1,0:T(8,128)(2,1)S(1)} %shard_map.52), channel_id=1, source_target_pairs={{0,2},{1,3},{2,0},{3,1},{4,6},{5,7},{6,4},{7,5},{8,10},{9,11},{10,... | collective-permute-start | bytes 1572872 | tf_op jit(solution)/shard_map/ppermute | solution.py:514
  76.0 1.9 %collective-permute-start.13 = (bf16[128,512]{1,0:T(8,128)(2,1)S(1)}, bf16[128,512]{1,0:T(8,128)(2,1)S(1)}, u32[]{:S(2)}, u32[]{:S(2)}) collective-permute-start(bf16[128,512]{1,0:T(8,128)(2,1)S(1)} %get-tuple-element.67), channel_id=1, source_target_pairs={{0,1},{1,0},{2,3},{3,2},{4,5},{5,4},{6,7},{7,6},{8,9},{9,8},{10,11... | collective-permute-start | bytes 393224 | tf_op jit(solution)/shard_map/ppermute | solution.py:480
  76.0 6.4 %collective-permute-start.14 = (bf16[128,512]{1,0:T(8,128)(2,1)S(1)}, bf16[128,512]{1,0:T(8,128)(2,1)S(1)}, u32[]{:S(2)}, u32[]{:S(2)}) collective-permute-start(bf16[128,512]{1,0:T(8,128)(2,1)S(1)} %get-tuple-element.68), channel_id=1, source_target_pairs={{0,4},{4,0},{8,12},{12,8},{16,20},{20,16},{24,28},{28,24},{1,5},{5... | collective-permute-start | bytes 393224 | tf_op jit(solution)/shard_map/ppermute | solution.py:481
  76.6 7.7 %collective-permute-start.15 = (bf16[128,512]{1,0:T(8,128)(2,1)S(1)}, bf16[128,512]{1,0:T(8,128)(2,1)S(1)}, u32[]{:S(2)}, u32[]{:S(2)}) collective-permute-start(bf16[128,512]{1,0:T(8,128)(2,1)S(1)} %get-tuple-element.69), channel_id=1, source_target_pairs={{0,5},{1,4},{2,7},{3,6},{4,1},{5,0},{6,3},{7,2},{8,13},{9,12},{10,... | collective-permute-start | bytes 393224 | tf_op jit(solution)/shard_map/ppermute | solution.py:482

commit v7 on v6

--- a/solution.py
+++ b/solution.py
@@ -271,7 +271,7 @@
         mine = pl.ds(multiple(step * TILE, TILE), TILE)
         for head in range(heads):
             total = stats[step, top_row(head) + 2 : top_row(head) + 3, :]
-            part = summed[step, head_cols(head), :] / total
+            part = summed[step, head_cols(head), :] * (1.0 / total)
             done[mine, head_cols(head)] = part.astype(BF16).T
         return 0
 

time: 94.2 us -> 94 us (level)
    ppermute x2, waiting for transfers between devices: 3.12 us -> 2.07 us  [per_device(): crossed = [lax.ppermute(part, 'ctx', hop) for part in kv_other]]
where the time goes in v7:
time: 94 us; the launch traced here: 93.4 us
  Pallas kernels  34.6 us (37%)
  waiting for transfers between devices  32.8 us (35%)
  starting transfers between devices  15.5 us (16%)
  local copies, waits for them, and re-layouts  8.78 us (9%)
    pallas_call x9, Pallas kernels, call(): pl.pallas_call(kernel, in_specs=specs, out_specs=[IN_VMEM] * len(outs), o...  33.4 us
    ppermute x2, waiting for transfers between devices, per_device(): lax.ppermute(lax.dynamic_slice_in_dim(keys_values, (1 - side) * half + gr...  18.6 us
    slice x3, local copies, waits for them, and re-layouts, per_device(): tails = [kv_own[:, last:]] + [part[:, last:] for part in kv_other]  4.82 us
    ppermute x3, waiting for transfers between devices, exchanged(): lax.ppermute(pieces[2], 'ctx', swap)  4.5 us
    dynamic_slice x2, local copies, waits for them, and re-layouts, mine(): return lax.dynamic_slice_in_dim(array, side * half, half, axis)  3.68 us
    ppermute x3, starting transfers between devices, exchanged(): lax.ppermute(pieces[2], 'ctx', swap)  3.12 us
    ppermute x1, waiting for transfers between devices, per_device(): q_other = lax.ppermute(q_send, 'ctx', swap)  2.84 us
    ppermute x2, waiting for transfers between devices, per_device(): arrived = [lax.ppermute(part, 'head', far_y) for part in leaving]  2.81 us
  transfers between devices with their start and end apart: 18, of which 7 were waited for; matrix products, arithmetic and copies ran while one was open for 10% of the time, Pallas kernels for 33%

profile of v7, /device:TPU:24, one launch (start us, length us, event | category | flops | bytes accessed | tf_op | source)
XLA Modules:
  0.0 93.4 jit_solution(16718261699255343938)
XLA Ops:
  0.0 0.0 copy-start
  0.0 0.0 collective-permute-start.1
  0.0 2.4 %constant_dynamic-slice_fusion.4.kv_own = bf16[2,512,512]{2,1,0:T(8,128)(2,1)} fusion(bf16[2,512,1024]{2,1,0:T(8,128)(2,1)} %param.7, s32[]{:T(128)S(6)} %select_n.27), kind=kLoop, calls=%fused_computation.10 | loop fusion | bytes 2097156 | tf_op jit(solution)/shard_map/dynamic_slice | solution.py:395
  2.4 0.0 copy-done
  2.4 0.0 copy-start.1
  2.4 0.1 constant_dynamic-slice_fusion
  2.6 1.6 %collective-permute-start = (bf16[2,512,256]{2,1,0:T(8,128)(2,1)S(1)}, bf16[2,512,256]{2,1,0:T(8,128)(2,1)}, u32[]{:S(2)}, u32[]{:S(2)}) collective-permute-start(bf16[2,512,256]{2,1,0:T(8,128)(2,1)S(1)} %get-tuple-element.71), channel_id=1, source_target_pairs={{0,4},{4,0},{8,12},{12,8},{16,20},{20,16},{24,28},{28,24},{1,5},{5... | collective-permute-start | bytes 1572872 | tf_op jit(solution)/shard_map/ppermute | solution.py:405
  4.1 1.3 %collective-permute-start.5 = (bf16[2,512,512]{2,1,0:T(8,128)(2,1)}, bf16[2,512,512]{2,1,0:T(8,128)(2,1)}, u32[]{:S(2)}, u32[]{:S(2)}) collective-permute-start(bf16[2,512,512]{2,1,0:T(8,128)(2,1)} %constant_dynamic-slice_fusion.4.kv_own), channel_id=1, source_target_pairs={{0,8},{4,12},{8,16},{12,20},{16,24},{20,28},{1,9},{5,13},{9,17},{1... | collective-permute-start | bytes 3145736 | tf_op jit(solution)/shard_map/ppermute | solution.py:402
  5.4 0.6 collective-permute-start.4
  6.0 1.3 %constant_dynamic-slice_fusion.1 = (bf16[512,512]{1,0:T(8,128)(2,1)S(1)}, bf16[512,512]{1,0:T(8,128)(2,1)S(1)}) fusion(bf16[512,1024]{1,0:T(8,128)(2,1)} %param.6, s32[]{:T(128)S(6)} %select_n.27, s32[]{:T(128)S(6)} %select_n.28), kind=kLoop, calls=%fused_computation.7 | loop fusion | bytes 2097160 | tf_op jit(solution)/shard_map/dynamic_slice | solution.py:395
  7.3 10.2 %collective-permute-done.kv_other_a = bf16[2,512,256]{2,1,0:T(8,128)(2,1)} collective-permute-done((bf16[2,512,256]{2,1,0:T(8,128)(2,1)S(1)}, bf16[2,512,256]{2,1,0:T(8,128)(2,1)}, u32[]{:S(2)}, u32[]{:S(2)}) %collective-permute-start) | collective-permute-done | bytes 524320 | tf_op jit(solution)/shard_map/ppermute | solution.py:405
  17.5 0.0 collective-permute-done.1.refs_7_.refs_3_.refs_5_
  17.5 1.5 %collective-permute-start.3 = (bf16[512,512]{1,0:T(8,128)(2,1)S(1)}, bf16[512,512]{1,0:T(8,128)(2,1)S(1)}, u32[]{:S(2)}, u32[]{:S(2)}) collective-permute-start(bf16[512,512]{1,0:T(8,128)(2,1)S(1)} %get-tuple-element.48), channel_id=1, source_target_pairs={{0,4},{4,0},{8,12},{12,8},{16,20},{20,16},{24,28},{28,24},{1,5},{5... | collective-permute-start | bytes 1572872 | tf_op jit(solution)/shard_map/ppermute | solution.py:415
  19.0 1.3 %collective-permute-start.2 = (bf16[2,512,256]{2,1,0:T(8,128)(2,1)}, bf16[2,512,256]{2,1,0:T(8,128)(2,1)}, u32[]{:S(2)}, u32[]{:S(2)}) collective-permute-start(bf16[2,512,256]{2,1,0:T(8,128)(2,1)} %collective-permute-done.kv_other_a), channel_id=1, source_target_pairs={{0,8},{4,12},{8,16},{12,20},{16,24},{20,28},{1,9},{5,13},{9,17},{1... | collective-permute-start | bytes 1572872 | tf_op jit(solution)/shard_map/ppermute | solution.py:416
  20.3 8.5 %collective-permute-done.4.kv_other_b = bf16[2,512,256]{2,1,0:T(8,128)(2,1)} collective-permute-done((bf16[2,512,256]{2,1,0:T(8,128)(2,1)S(1)}, bf16[2,512,256]{2,1,0:T(8,128)(2,1)}, u32[]{:S(2)}, u32[]{:S(2)}) %collective-permute-start.4) | collective-permute-done | bytes 524320 | tf_op jit(solution)/shard_map/ppermute | solution.py:405
  28.7 1.3 %collective-permute-start.6 = (bf16[2,512,256]{2,1,0:T(8,128)(2,1)}, bf16[2,512,256]{2,1,0:T(8,128)(2,1)}, u32[]{:S(2)}, u32[]{:S(2)}) collective-permute-start(bf16[2,512,256]{2,1,0:T(8,128)(2,1)} %collective-permute-done.4.kv_other_b), channel_id=1, source_target_pairs={{0,8},{4,12},{8,16},{12,20},{16,24},{20,28},{1,9},{5,13},{9,17},{1... | collective-permute-start | bytes 1572872 | tf_op jit(solution)/shard_map/ppermute | solution.py:416
  30.0 1.7 %slice.18 = bf16[2,128,512]{2,1,0:T(8,128)(2,1)} slice(bf16[2,512,512]{2,1,0:T(8,128)(2,1)} %constant_dynamic-slice_fusion.4.kv_own), slice={[0:2], [384:512], [0:512]} | slice | bytes 524288 | tf_op jit(solution)/shard_map/slice | solution.py:446
  31.7 0.0 copy-done.1
  31.7 0.1 pad_dynamic-slice_fusion.docs
  31.8 0.8 compare_reduce_fusion
  33.2 0.1 pad_add_fusion.ids
  33.3 1.6 %slice.24 = bf16[2,128,256]{2,1,0:T(8,128)(2,1)} slice(bf16[2,512,256]{2,1,0:T(8,128)(2,1)} %collective-permute-done.4.kv_other_b), slice={[0:2], [384:512], [0:256]} | slice | bytes 262144 | tf_op jit(solution)/shard_map/slice | solution.py:446
  34.9 1.6 %slice.19 = bf16[2,128,256]{2,1,0:T(8,128)(2,1)} slice(bf16[2,512,256]{2,1,0:T(8,128)(2,1)} %collective-permute-done.kv_other_a), slice={[0:2], [384:512], [0:256]} | slice | bytes 262144 | tf_op jit(solution)/shard_map/slice | solution.py:446
  36.4 2.8 %collective-permute-done.3.q_other = bf16[512,512]{1,0:T(8,128)(2,1)S(1)} collective-permute-done((bf16[512,512]{1,0:T(8,128)(2,1)S(1)}, bf16[512,512]{1,0:T(8,128)(2,1)S(1)}, u32[]{:S(2)}, u32[]{:S(2)}) %collective-permute-start.3) | collective-permute-done | bytes 524320 | tf_op jit(solution)/shard_map/ppermute | solution.py:415
  39.3 6.4 %shard_map.47 = (f32[512,1024]{1,0:T(8,128)S(1)}, f32[8,1024]{1,0:T(8,128)S(1)}) custom-call(s32[2]{0:T(128)S(1)} %pad_add_fusion.ids, s32[2304]{0:T(1024)S(1)} %pad_dynamic-slice_fusion.docs, s32[1,2304]{1,0:T(1,128)S(1)} %reshape.7.docs_row, bf16[512,512]{1,0:T(8,128)(2,1)S(1)} %get-tuple-element.72.q_own, ...), custom_call_target="tpu_custom_call" | custom-call | flops 7000 | bytes 1024 | tf_op jit(solution)/shard_map/pallas_call | solution.py:353
  45.8 0.0 collective-permute-done.5.same
  45.8 0.0 collective-permute-done.2.refs_0_.rest_0_
  45.8 3.0 %shard_map.49 = (bf16[128,256]{1,0:T(8,128)(2,1)S(1)}, bf16[128,256]{1,0:T(8,128)(2,1)S(1)}, bf16[128,256]{1,0:T(8,128)(2,1)S(1)}, bf16[128,256]{1,0:T(8,128)(2,1)S(1)}) custom-call(s32[2]{0:T(128)S(1)} %pad_add_fusion.ids, s32[2304]{0:T(1024)S(1)} %pad_dynamic-slice_fusion.docs, s32[1,2304]{1,0:T(1,128)S(1)} %reshape.7.docs_row, ...), custom_call_target="tpu_custom_call" | custom-call | flops 1000 | bytes 1024 | tf_op jit(solution)/shard_map/pallas_call | solution.py:353
  48.8 0.1 collective-permute-start.9
  48.8 1.6 %collective-permute-start.11 = (bf16[128,256]{1,0:T(8,128)(2,1)S(1)}, bf16[128,256]{1,0:T(8,128)(2,1)S(1)}, u32[]{:S(2)}, u32[]{:S(2)}) collective-permute-start(bf16[128,256]{1,0:T(8,128)(2,1)S(1)} %get-tuple-element.63), channel_id=1, source_target_pairs={{0,4},{4,0},{8,12},{12,8},{16,20},{20,16},{24,28},{28,24},{1,5},{5... | collective-permute-start | bytes 196616 | tf_op jit(solution)/shard_map/ppermute | solution.py:481
  50.4 0.3 collective-permute-start.12
  50.7 0.0 slice-start
  50.7 1.1 %shard_map.46.ids = s32[2]{0:T(128)S(1)} custom-call(s32[2]{0:T(128)S(1)} %pad_add_fusion.ids, bf16[2,512,256]{2,1,0:T(8,128)(2,1)} %collective-permute-done.2.refs_0_.rest_0_), custom_call_target="tpu_custom_call" | custom-call | flops 550000000 | bytes 1024 | tf_op jit(solution)/shard_map/pallas_call | solution.py:340
  51.9 0.0 slice-start.1
  51.9 2.1 %collective-permute-done.6.rest_0_.rest_1_ = bf16[2,512,256]{2,1,0:T(8,128)(2,1)} collective-permute-done((bf16[2,512,256]{2,1,0:T(8,128)(2,1)}, bf16[2,512,256]{2,1,0:T(8,128)(2,1)}, u32[]{:S(2)}, u32[]{:S(2)}) %collective-permute-start.6) | collective-permute-done | bytes 524320 | tf_op jit(solution)/shard_map/ppermute | solution.py:416
  53.9 3.1 %shard_map.48 = (bf16[128,256]{1,0:T(8,128)(2,1)S(1)}, bf16[128,256]{1,0:T(8,128)(2,1)S(1)}, bf16[128,256]{1,0:T(8,128)(2,1)S(1)}, bf16[128,256]{1,0:T(8,128)(2,1)S(1)}) custom-call(s32[2]{0:T(128)S(1)} %shard_map.46.ids, s32[2304]{0:T(1024)S(1)} %pad_dynamic-slice_fusion.docs, s32[1,2304]{1,0:T(1,128)S(1)} %reshape.7.docs_row, ...), custom_call_target="tpu_custom_call" | custom-call | flops 5000000000 | bytes 1024 | tf_op jit(solution)/shard_map/pallas_call | solution.py:353
  57.1 0.1 collective-permute-start.10
  57.1 0.8 collective-permute-start.7
  57.9 0.0 collective-permute-done.9.refs_1_
  57.9 1.1 %collective-permute-start.8 = (bf16[128,256]{1,0:T(8,128)(2,1)S(1)}, bf16[128,256]{1,0:T(8,128)(2,1)S(1)}, u32[]{:S(2)}, u32[]{:S(2)}) collective-permute-start(bf16[128,256]{1,0:T(8,128)(2,1)S(1)} %get-tuple-element.57), channel_id=1, source_target_pairs={{0,5},{1,4},{2,7},{3,6},{4,1},{5,0},{6,3},{7,2},{8,13},{9,12},{10,... | collective-permute-start | bytes 196616 | tf_op jit(solution)/shard_map/ppermute | solution.py:482
  59.0 0.0 collective-permute-done.11.refs_4_
  59.0 0.0 collective-permute-done.12.refs_5_
  59.0 0.0 collective-permute-done.10.refs_3_
  59.0 0.0 slice-done
  59.0 0.0 slice-done.1
  59.0 5.2 %shard_map.50.refs_4_ = f32[128,4096]{1,0:T(8,128)S(1)} custom-call(s32[2]{0:T(128)S(1)} %pad_add_fusion.ids, bf16[128,256]{1,0:T(8,128)(2,1)S(1)} %get-tuple-element.59.refs_0_, bf16[128,256]{1,0:T(8,128)(2,1)S(1)} %collective-permute-done.9.refs_1_, bf16[128,256]{1,0:T(8,128)(2,1)S(1)} %get-tuple-element.61.refs_2_, ...), custom_call_target="tpu_custom_call" | custom-call | flops 1000 | bytes 1024 | tf_op jit(solution)/shard_map/pallas_call | solution.py:353
  64.3 0.0 collective-permute-done.7.refs_0_
  64.3 0.0 collective-permute-done.8.refs_1_
  64.3 2.4 %shard_map.51 = bf16[128,2048]{1,0:T(8,128)(2,1)S(1)} custom-call(s32[2]{0:T(128)S(1)} %pad_add_fusion.ids, bf16[128,256]{1,0:T(8,128)(2,1)S(1)} %collective-permute-done.7.refs_0_, bf16[128,256]{1,0:T(8,128)(2,1)S(1)} %collective-permute-done.8.refs_1_, bf16[1024,4096]{1,0:T(8,128)(2,1)S(1)} %bitcast.7, ...), custom_call_target="tpu_custom_call" | custom-call | flops 1000 | bytes 1024 | tf_op jit(solution)/shard_map/pallas_call | solution.py:353
  66.7 1.6 %collective-permute-start.16 = (bf16[128,2048]{1,0:T(8,128)(2,1)S(1)}, bf16[128,2048]{1,0:T(8,128)(2,1)S(1)}, u32[]{:S(2)}, u32[]{:S(2)}) collective-permute-start(bf16[128,2048]{1,0:T(8,128)(2,1)S(1)} %shard_map.51), channel_id=1, source_target_pairs={{0,2},{1,3},{2,0},{3,1},{4,6},{5,7},{6,4},{7,5},{8,10},{9,11},{10,... | collective-permute-start | bytes 1572872 | tf_op jit(solution)/shard_map/ppermute | solution.py:514
  68.3 2.4 %shard_map.52 = bf16[128,2048]{1,0:T(8,128)(2,1)S(1)} custom-call(s32[2]{0:T(128)S(1)} %pad_add_fusion.ids, bf16[128,256]{1,0:T(8,128)(2,1)S(1)} %collective-permute-done.7.refs_0_, bf16[128,256]{1,0:T(8,128)(2,1)S(1)} %collective-permute-done.8.refs_1_, bf16[1024,4096]{1,0:T(8,128)(2,1)S(1)} %bitcast.7, ...), custom_call_target="tpu_custom_call" | custom-call | flops 1000 | bytes 1024 | tf_op jit(solution)/shard_map/pallas_call | solution.py:353
  70.8 0.6 collective-permute-start.17
  71.3 3.7 %shard_map.53 = (bf16[128,512]{1,0:T(8,128)(2,1)S(1)}, bf16[128,512]{1,0:T(8,128)(2,1)S(1)}, bf16[128,512]{1,0:T(8,128)(2,1)S(1)}, bf16[128,512]{1,0:T(8,128)(2,1)S(1)}) custom-call(s32[2]{0:T(128)S(1)} %shard_map.46.ids, s32[2304]{0:T(1024)S(1)} %pad_dynamic-slice_fusion.docs, s32[1,2304]{1,0:T(1,128)S(1)} %reshape.7.docs_row, ...), custom_call_target="tpu_custom_call" | custom-call | flops 1000 | bytes 1024 | tf_op jit(solution)/shard_map/pallas_call | solution.py:353
  75.1 0.1 collective-permute-start.13
  75.1 0.8 collective-permute-start.14
  75.9 1.1 %collective-permute-start.15 = (bf16[128,512]{1,0:T(8,128)(2,1)S(1)}, bf16[128,512]{1,0:T(8,128)(2,1)S(1)}, u32[]{:S(2)}, u32[]{:S(2)}) collective-permute-start(bf16[128,512]{1,0:T(8,128)(2,1)S(1)} %get-tuple-element.69), channel_id=1, source_target_pairs={{0,5},{1,4},{2,7},{3,6},{4,1},{5,0},{6,3},{7,2},{8,13},{9,12},{10,... | collective-permute-start | bytes 393224 | tf_op jit(solution)/shard_map/ppermute | solution.py:482
  77.0 0.0 collective-permute-done.13.refs_1_
  77.0 4.5 %collective-permute-done.14.refs_2_ = bf16[128,512]{1,0:T(8,128)(2,1)S(1)} collective-permute-done((bf16[128,512]{1,0:T(8,128)(2,1)S(1)}, bf16[128,512]{1,0:T(8,128)(2,1)S(1)}, u32[]{:S(2)}, u32[]{:S(2)}) %collective-permute-start.14) | collective-permute-done | bytes 131104 | tf_op jit(solution)/shard_map/ppermute | solution.py:481
  81.5 1.9 %collective-permute-done.15.refs_3_ = bf16[128,512]{1,0:T(8,128)(2,1)S(1)} collective-permute-done((bf16[128,512]{1,0:T(8,128)(2,1)S(1)}, bf16[128,512]{1,0:T(8,128)(2,1)S(1)}, u32[]{:S(2)}, u32[]{:S(2)}) %collective-permute-start.15) | collective-permute-done | bytes 131104 | tf_op jit(solution)/shard_map/ppermute | solution.py:482
  83.4 6.0 %shard_map.54.staying = f32[128,4096]{1,0:T(8,128)S(1)} custom-call(s32[2]{0:T(128)S(1)} %pad_add_fusion.ids, bf16[128,512]{1,0:T(8,128)(2,1)S(1)} %get-tuple-element.66.refs_0_, bf16[128,512]{1,0:T(8,128)(2,1)S(1)} %collective-permute-done.13.refs_1_, bf16[128,512]{1,0:T(8,128)(2,1)S(1)} %collective-permute-done.14.refs_2_, ...), custom_call_target="tpu_custom_call" | custom-call | flops 1000 | bytes 1024 | tf_op jit(solution)/shard_map/pallas_call | solution.py:353
  89.4 0.0 collective-permute-done.16.refs_0_
  89.4 2.8 %collective-permute-done.17.refs_1_ = bf16[128,2048]{1,0:T(8,128)(2,1)S(1)} collective-permute-done((bf16[128,2048]{1,0:T(8,128)(2,1)S(1)}, bf16[128,2048]{1,0:T(8,128)(2,1)S(1)}, u32[]{:S(2)}, u32[]{:S(2)}) %collective-permute-start.17) | collective-permute-done | bytes 524320 | tf_op jit(solution)/shard_map/ppermute | solution.py:514
  92.2 1.1 %shard_map.55 = bf16[128,4096]{1,0:T(8,128)(2,1)} custom-call(f32[128,4096]{1,0:T(8,128)S(1)} %shard_map.54.staying, bf16[128,2048]{1,0:T(8,128)(2,1)S(1)} %collective-permute-done.16.refs_0_, bf16[128,2048]{1,0:T(8,128)(2,1)S(1)} %collective-permute-done.17.refs_1_), custom_call_target="tpu_custom_call" | custom-call | flops 1000 | bytes 1024 | tf_op jit(solution)/shard_map/pallas_call | solution.py:353
  (5 shorter events, 0.1 us)
Async XLA Ops:
  0.0 2.4 %copy-start = (bf16[2,512,1024]{2,1,0:T(8,128)(2,1)S(1)}, bf16[2,512,1024]{2,1,0:T(8,128)(2,1)}, u32[]{:S(2)}) copy-start(bf16[2,512,1024]{2,1,0:T(8,128)(2,1)} %param.7) | copy-start | bytes 6291460
  0.0 17.5 %collective-permute-start.1 = (bf16[1024,4096]{1,0:T(8,128)(2,1)}, bf16[1024,4096]{1,0:T(8,128)(2,1)}, u32[]{:S(2)}, u32[]{:S(2)}) collective-permute-start(bf16[1024,4096]{1,0:T(8,128)(2,1)} %refs_4_.1), channel_id=1, source_target_pairs={{0,1},{1,0},{2,3},{3,2},{4,5},{5,4},{6,7},{7,6},{8,9},{9,8},{10,11... | collective-permute-start | bytes 25165832 | tf_op jit(solution)/shard_map/ppermute | solution.py:412
  2.4 29.3 %copy-start.1 = (s32[4096]{0:T(1024)S(1)}, s32[4096]{0:T(1024)}, u32[]{:S(2)}) copy-start(s32[4096]{0:T(1024)} %param.9) | copy-start | bytes 49156
  2.6 14.9 %collective-permute-start = (bf16[2,512,256]{2,1,0:T(8,128)(2,1)S(1)}, bf16[2,512,256]{2,1,0:T(8,128)(2,1)}, u32[]{:S(2)}, u32[]{:S(2)}) collective-permute-start(bf16[2,512,256]{2,1,0:T(8,128)(2,1)S(1)} %get-tuple-element.71), channel_id=1, source_target_pairs={{0,4},{4,0},{8,12},{12,8},{16,20},{20,16},{24,28},{28,24},{1,5},{5... | collective-permute-start | bytes 1572872 | tf_op jit(solution)/shard_map/ppermute | solution.py:405
  4.1 41.7 %collective-permute-start.5 = (bf16[2,512,512]{2,1,0:T(8,128)(2,1)}, bf16[2,512,512]{2,1,0:T(8,128)(2,1)}, u32[]{:S(2)}, u32[]{:S(2)}) collective-permute-start(bf16[2,512,512]{2,1,0:T(8,128)(2,1)} %constant_dynamic-slice_fusion.4.kv_own), channel_id=1, source_target_pairs={{0,8},{4,12},{8,16},{12,20},{16,24},{20,28},{1,9},{5,13},{9,17},{1... | collective-permute-start | bytes 3145736 | tf_op jit(solution)/shard_map/ppermute | solution.py:402
  5.4 23.3 %collective-permute-start.4 = (bf16[2,512,256]{2,1,0:T(8,128)(2,1)S(1)}, bf16[2,512,256]{2,1,0:T(8,128)(2,1)}, u32[]{:S(2)}, u32[]{:S(2)}) collective-permute-start(bf16[2,512,256]{2,1,0:T(8,128)(2,1)S(1)} %get-tuple-element.70), channel_id=1, source_target_pairs={{0,4},{4,0},{8,12},{12,8},{16,20},{20,16},{24,28},{28,24},{1,5},{5... | collective-permute-start | bytes 1572872 | tf_op jit(solution)/shard_map/ppermute | solution.py:405
  17.5 21.8 %collective-permute-start.3 = (bf16[512,512]{1,0:T(8,128)(2,1)S(1)}, bf16[512,512]{1,0:T(8,128)(2,1)S(1)}, u32[]{:S(2)}, u32[]{:S(2)}) collective-permute-start(bf16[512,512]{1,0:T(8,128)(2,1)S(1)} %get-tuple-element.48), channel_id=1, source_target_pairs={{0,4},{4,0},{8,12},{12,8},{16,20},{20,16},{24,28},{28,24},{1,5},{5... | collective-permute-start | bytes 1572872 | tf_op jit(solution)/shard_map/ppermute | solution.py:415
  19.0 26.8 %collective-permute-start.2 = (bf16[2,512,256]{2,1,0:T(8,128)(2,1)}, bf16[2,512,256]{2,1,0:T(8,128)(2,1)}, u32[]{:S(2)}, u32[]{:S(2)}) collective-permute-start(bf16[2,512,256]{2,1,0:T(8,128)(2,1)} %collective-permute-done.kv_other_a), channel_id=1, source_target_pairs={{0,8},{4,12},{8,16},{12,20},{16,24},{20,28},{1,9},{5,13},{9,17},{1... | collective-permute-start | bytes 1572872 | tf_op jit(solution)/shard_map/ppermute | solution.py:416
  28.7 25.2 %collective-permute-start.6 = (bf16[2,512,256]{2,1,0:T(8,128)(2,1)}, bf16[2,512,256]{2,1,0:T(8,128)(2,1)}, u32[]{:S(2)}, u32[]{:S(2)}) collective-permute-start(bf16[2,512,256]{2,1,0:T(8,128)(2,1)} %collective-permute-done.4.kv_other_b), channel_id=1, source_target_pairs={{0,8},{4,12},{8,16},{12,20},{16,24},{20,28},{1,9},{5,13},{9,17},{1... | collective-permute-start | bytes 1572872 | tf_op jit(solution)/shard_map/ppermute | solution.py:416
  48.8 9.2 %collective-permute-start.9 = (bf16[128,256]{1,0:T(8,128)(2,1)S(1)}, bf16[128,256]{1,0:T(8,128)(2,1)S(1)}, u32[]{:S(2)}, u32[]{:S(2)}) collective-permute-start(bf16[128,256]{1,0:T(8,128)(2,1)S(1)} %get-tuple-element.60), channel_id=1, source_target_pairs={{0,1},{1,0},{2,3},{3,2},{4,5},{5,4},{6,7},{7,6},{8,9},{9,8},{10,11... | collective-permute-start | bytes 196616 | tf_op jit(solution)/shard_map/ppermute | solution.py:480
  48.8 10.2 %collective-permute-start.11 = (bf16[128,256]{1,0:T(8,128)(2,1)S(1)}, bf16[128,256]{1,0:T(8,128)(2,1)S(1)}, u32[]{:S(2)}, u32[]{:S(2)}) collective-permute-start(bf16[128,256]{1,0:T(8,128)(2,1)S(1)} %get-tuple-element.63), channel_id=1, source_target_pairs={{0,4},{4,0},{8,12},{12,8},{16,20},{20,16},{24,28},{28,24},{1,5},{5... | collective-permute-start | bytes 196616 | tf_op jit(solution)/shard_map/ppermute | solution.py:481
  50.4 8.6 %collective-permute-start.12 = (bf16[128,256]{1,0:T(8,128)(2,1)S(1)}, bf16[128,256]{1,0:T(8,128)(2,1)S(1)}, u32[]{:S(2)}, u32[]{:S(2)}) collective-permute-start(bf16[128,256]{1,0:T(8,128)(2,1)S(1)} %get-tuple-element.64), channel_id=1, source_target_pairs={{0,5},{1,4},{2,7},{3,6},{4,1},{5,0},{6,3},{7,2},{8,13},{9,12},{10,... | collective-permute-start | bytes 196616 | tf_op jit(solution)/shard_map/ppermute | solution.py:482
  50.7 8.3 %slice-start = ((s8[8388608]{0:T(1024)(128)(4,1)}), s8[4194304]{0:T(1024)(128)(4,1)S(1)}, s32[]{:S(2)}) async-start(s8[8388608]{0:T(1024)(128)(4,1)} %bitcast.6), calls=%async_computation.1 | async-start | bytes 8388608
  51.9 7.2 %slice-start.1 = ((s8[8388608]{0:T(1024)(128)(4,1)}), s8[4194304]{0:T(1024)(128)(4,1)S(1)}, s32[]{:S(2)}) async-start(s8[8388608]{0:T(1024)(128)(4,1)} %bitcast.6), calls=%async_computation.2 | async-start | bytes 8388608
  57.1 2.0 %collective-permute-start.10 = (bf16[128,256]{1,0:T(8,128)(2,1)S(1)}, bf16[128,256]{1,0:T(8,128)(2,1)S(1)}, u32[]{:S(2)}, u32[]{:S(2)}) collective-permute-start(bf16[128,256]{1,0:T(8,128)(2,1)S(1)} %get-tuple-element.62), channel_id=1, source_target_pairs={{0,1},{1,0},{2,3},{3,2},{4,5},{5,4},{6,7},{7,6},{8,9},{9,8},{10,11... | collective-permute-start | bytes 196616 | tf_op jit(solution)/shard_map/ppermute | solution.py:480
  57.1 7.1 %collective-permute-start.7 = (bf16[128,256]{1,0:T(8,128)(2,1)S(1)}, bf16[128,256]{1,0:T(8,128)(2,1)S(1)}, u32[]{:S(2)}, u32[]{:S(2)}) collective-permute-start(bf16[128,256]{1,0:T(8,128)(2,1)S(1)} %get-tuple-element.56), channel_id=1, source_target_pairs={{0,4},{4,0},{8,12},{12,8},{16,20},{20,16},{24,28},{28,24},{1,5},{5... | collective-permute-start | bytes 196616 | tf_op jit(solution)/shard_map/ppermute | solution.py:481
  57.9 6.3 %collective-permute-start.8 = (bf16[128,256]{1,0:T(8,128)(2,1)S(1)}, bf16[128,256]{1,0:T(8,128)(2,1)S(1)}, u32[]{:S(2)}, u32[]{:S(2)}) collective-permute-start(bf16[128,256]{1,0:T(8,128)(2,1)S(1)} %get-tuple-element.57), channel_id=1, source_target_pairs={{0,5},{1,4},{2,7},{3,6},{4,1},{5,0},{6,3},{7,2},{8,13},{9,12},{10,... | collective-permute-start | bytes 196616 | tf_op jit(solution)/shard_map/ppermute | solution.py:482
  66.7 22.7 %collective-permute-start.16 = (bf16[128,2048]{1,0:T(8,128)(2,1)S(1)}, bf16[128,2048]{1,0:T(8,128)(2,1)S(1)}, u32[]{:S(2)}, u32[]{:S(2)}) collective-permute-start(bf16[128,2048]{1,0:T(8,128)(2,1)S(1)} %shard_map.51), channel_id=1, source_target_pairs={{0,2},{1,3},{2,0},{3,1},{4,6},{5,7},{6,4},{7,5},{8,10},{9,11},{10,... | collective-permute-start | bytes 1572872 | tf_op jit(solution)/shard_map/ppermute | solution.py:514
  70.8 21.4 %collective-permute-start.17 = (bf16[128,2048]{1,0:T(8,128)(2,1)S(1)}, bf16[128,2048]{1,0:T(8,128)(2,1)S(1)}, u32[]{:S(2)}, u32[]{:S(2)}) collective-permute-start(bf16[128,2048]{1,0:T(8,128)(2,1)S(1)} %shard_map.52), channel_id=1, source_target_pairs={{0,2},{1,3},{2,0},{3,1},{4,6},{5,7},{6,4},{7,5},{8,10},{9,11},{10,... | collective-permute-start | bytes 1572872 | tf_op jit(solution)/shard_map/ppermute | solution.py:514
  75.1 1.9 %collective-permute-start.13 = (bf16[128,512]{1,0:T(8,128)(2,1)S(1)}, bf16[128,512]{1,0:T(8,128)(2,1)S(1)}, u32[]{:S(2)}, u32[]{:S(2)}) collective-permute-start(bf16[128,512]{1,0:T(8,128)(2,1)S(1)} %get-tuple-element.67), channel_id=1, source_target_pairs={{0,1},{1,0},{2,3},{3,2},{4,5},{5,4},{6,7},{7,6},{8,9},{9,8},{10,11... | collective-permute-start | bytes 393224 | tf_op jit(solution)/shard_map/ppermute | solution.py:480
  75.1 6.4 %collective-permute-start.14 = (bf16[128,512]{1,0:T(8,128)(2,1)S(1)}, bf16[128,512]{1,0:T(8,128)(2,1)S(1)}, u32[]{:S(2)}, u32[]{:S(2)}) collective-permute-start(bf16[128,512]{1,0:T(8,128)(2,1)S(1)} %get-tuple-element.68), channel_id=1, source_target_pairs={{0,4},{4,0},{8,12},{12,8},{16,20},{20,16},{24,28},{28,24},{1,5},{5... | collective-permute-start | bytes 393224 | tf_op jit(solution)/shard_map/ppermute | solution.py:481
  75.9 7.5 %collective-permute-start.15 = (bf16[128,512]{1,0:T(8,128)(2,1)S(1)}, bf16[128,512]{1,0:T(8,128)(2,1)S(1)}, u32[]{:S(2)}, u32[]{:S(2)}) collective-permute-start(bf16[128,512]{1,0:T(8,128)(2,1)S(1)} %get-tuple-element.69), channel_id=1, source_target_pairs={{0,5},{1,4},{2,7},{3,6},{4,1},{5,0},{6,3},{7,2},{8,13},{9,12},{10,... | collective-permute-start | bytes 393224 | tf_op jit(solution)/shard_map/ppermute | solution.py:482
